TPU v7x, 32 devices: a whole 2x2x4 slice. The times are simulated.
32 devices in a mesh: seq: 4 (over z), row: 8 (over y, x, core).
Axes of the slice: x: 2, y: 2, z: 4, core: 2. Of those that a mesh axis runs over, the one named last changes fastest.
Arguments:
- tokens: bfloat16 [16, 2048, 1024], P('row', 'seq'), may hold values from -6 to 6
- segment_ids: int32 [16, 2048], P('row', 'seq'), may hold values from 0 to 3, as said below
- memory: bfloat16 [16, 512, 1024], P('row', 'seq'), may hold values from -6 to 6
- cotangent: bfloat16 [16, 2048, 1024], P('row', 'seq'), may hold values from -6 to 6
- gain_attend: float32 [1024], replicated, may hold values from 0.1 to 1.9
- gain_cross: float32 [1024], replicated, may hold values from 0.1 to 1.9
- gain_feed: float32 [1024], replicated, may hold values from 0.1 to 1.9
- bias_table: float32 [32, 16], replicated, may hold values from -4 to 4
- self_query: bfloat16 [1024, 1024], replicated, may hold values from -0.1875 to 0.1875
- self_keyvalue: bfloat16 [1024, 1024], replicated, may hold values from -0.1875 to 0.1875
- self_output: bfloat16 [1024, 1024], replicated, may hold values from -2 to 2
- cross_query: bfloat16 [1024, 1024], replicated, may hold values from -0.1875 to 0.1875
- cross_keyvalue: bfloat16 [1024, 1024], replicated, may hold values from -0.1875 to 0.1875
- cross_output: bfloat16 [1024, 1024], replicated, may hold values from -2 to 2
- feed_gate: bfloat16 [1024, 2816], replicated, may hold values from -0.1875 to 0.1875
- feed_up: bfloat16 [1024, 2816], replicated, may hold values from -0.1875 to 0.1875
- feed_down: bfloat16 [2816, 1024], replicated, may hold values from -0.109375 to 0.109375
Outputs:
- layer_output: bfloat16 [16, 2048, 1024], P('row', 'seq')
- tokens_grad: bfloat16 [16, 2048, 1024], P('row', 'seq')
- memory_grad: bfloat16 [16, 512, 1024], P('row', 'seq')
- self_query_grad: float32 [1024, 1024], P(('seq', 'row'))
- self_keyvalue_grad: float32 [1024, 1024], P(('seq', 'row'))
- self_output_grad: float32 [1024, 1024], P(('seq', 'row'))
- cross_query_grad: float32 [1024, 1024], P(('seq', 'row'))
- cross_keyvalue_grad: float32 [1024, 1024], P(('seq', 'row'))
- cross_output_grad: float32 [1024, 1024], P(('seq', 'row'))
- feed_gate_grad: float32 [1024, 2816], P(('seq', 'row'))
- feed_up_grad: float32 [1024, 2816], P(('seq', 'row'))
- feed_down_grad: float32 [2816, 1024], P(('seq', 'row'))
- gain_attend_grad: float32 [1024], replicated
- gain_cross_grad: float32 [1024], replicated
- gain_feed_grad: float32 [1024], replicated
- bias_table_grad: float32 [32, 16], replicated
Inputs may be any that keep to these rules, and one draw needn't show every extreme that they name: `segment_ids`: along each row the document numbers start at 0 and never fall; documents never cross rows.
All inputs are finite; a program needn't handle non-finite values.
Results may differ from a plain program's by a relative error of at most 0.03.
Values may be sent and summed in bfloat16 or wider, within the bound.
A program may use at most 576 MiB of HBM per device.

v0:
```python
from functools import partial
import math

import jax
import jax.numpy as jnp
import numpy as np
from jax import lax
from jax.sharding import PartitionSpec as P

HEADS = 16
KV_HEADS = 8
HEAD = 64
BUCKETS = 32
MAX_DIST = 128


HIGHEST = lax.Precision.HIGHEST


def passed_along(shard, axis, by):
    devices = lax.axis_size(axis)
    pairs = [(i, i + by) for i in range(devices) if 0 <= i + by < devices]
    return lax.ppermute(shard, axis, pairs)


def passed_along_2(shard, axis, by):
    devices = lax.axis_size(axis)
    return lax.ppermute(shard, axis, [(i, (i + by) % devices) for i in range(devices)])


def bucket_level(distance):
    exact_part = BUCKETS // 2
    if distance < exact_part:
        return distance
    which_bucket = exact_part + math.floor(
        math.log(distance / exact_part) / math.log(MAX_DIST / exact_part) * (BUCKETS - exact_part)
    )
    return min(BUCKETS - 1, which_bucket)


def bucket_limits():
    bounds = []
    distance = 0
    for which_bucket in range(1, BUCKETS):
        while bucket_level(distance) < which_bucket:
            distance = distance + 1
        bounds.append(distance)
    return np.array(bounds, dtype=np.int32)


def norm_rows(values, gain):
    return values * lax.rsqrt(jnp.mean(values * values, axis=-1, keepdims=True) + 1e-06) * gain


def gated_mix(gate_pre, up_pre):
    return jax.nn.gelu(gate_pre, approximate=True) * up_pre


def matmul_low(left, right):
    return jnp.dot(left, right, preferred_element_type=jnp.float32)


def matmul_tn(left, right):
    return lax.dot_general(
        left, right, (((0,), (0,)), ((), ())), preferred_element_type=jnp.float32
    )


def matmul_nt(left, right):
    return lax.dot_general(
        left, right, (((1,), (1,)), ((), ())), preferred_element_type=jnp.float32
    )


def self_scores(
    queries, key_heads, own_segments, key_segments, query_places, key_places, bias_table
):
    raw_scores = (
        jnp.einsum("rqkgd,rtkd->rkgqt", queries, key_heads, preferred_element_type=jnp.float32)
        * 0.125
    )
    distance = query_places[:, None] - key_places[None, :]
    limits = jnp.asarray(bucket_limits())
    levels = jnp.sum(
        (jnp.maximum(distance, 0)[None] >= limits[:, None, None]).astype(jnp.int32), axis=0
    )
    one_hot = (levels[None] == jnp.arange(BUCKETS, dtype=jnp.int32)[:, None, None]).astype(
        jnp.float32
    )
    heads_bias = jnp.einsum("bqt,bh->hqt", one_hot, bias_table, precision=HIGHEST)
    heads_bias = heads_bias.reshape(
        queries.shape[2], queries.shape[3], distance.shape[0], distance.shape[1]
    )
    allowed = (own_segments[:, :, None] == key_segments[:, None, :]) & (distance >= 0)[None]
    scores = jnp.where(allowed[:, None, None], raw_scores + heads_bias[None], -1e30)
    return (scores, one_hot)


def on_device(
    tokens,
    segment_ids,
    memory,
    cotangent,
    gain_attend,
    gain_cross,
    gain_feed,
    bias_table,
    self_query,
    self_keyvalue,
    self_output,
    cross_query,
    cross_keyvalue,
    cross_output,
    feed_gate,
    feed_up,
    feed_down,
):
    row_count, shard_len, model_width = tokens.shape
    flat_rows = row_count * shard_len
    seq_count = lax.axis_size("seq")
    seq_place = lax.axis_index("seq")
    kv_width = KV_HEADS * HEAD
    group_size = HEADS // KV_HEADS
    query_places = seq_place * shard_len + jnp.arange(shard_len, dtype=jnp.int32)
    inputs = tokens.astype(jnp.float32).reshape(flat_rows, model_width)
    normed_one_low = norm_rows(inputs, gain_attend).astype(jnp.bfloat16)
    queries = matmul_low(normed_one_low, self_query).astype(jnp.bfloat16)
    queries = queries.reshape(row_count, shard_len, KV_HEADS, group_size, HEAD)
    self_pairs = (
        matmul_low(normed_one_low, self_keyvalue)
        .astype(jnp.bfloat16)
        .reshape(row_count, shard_len, 2 * kv_width)
    )
    all_segments = lax.all_gather(segment_ids, "seq", axis=1, tiled=True)

    def block_keys(travel, cycle_step):
        source = (seq_place - cycle_step) % seq_count
        key_heads = travel[:, :, :kv_width].reshape(row_count, shard_len, KV_HEADS, HEAD)
        value_heads = travel[:, :, kv_width:].reshape(row_count, shard_len, KV_HEADS, HEAD)
        key_segments = lax.dynamic_slice_in_dim(all_segments, source * shard_len, shard_len, 1)
        key_places = source * shard_len + jnp.arange(shard_len, dtype=jnp.int32)
        scores, one_hot = self_scores(
            queries, key_heads, segment_ids, key_segments, query_places, key_places, bias_table
        )
        return (key_heads, value_heads, scores, one_hot)

    def forward_block(carried, travel, cycle_step):
        running_max, totals, accumulated = carried
        key_heads, value_heads, scores, one_hot = block_keys(travel, cycle_step)
        new_max = jnp.maximum(running_max, jnp.max(scores, axis=-1))
        weights = jnp.exp(scores - new_max[..., None])
        rescale = jnp.exp(running_max - new_max)
        totals = totals * rescale + jnp.sum(weights, axis=-1)
        accumulated = accumulated * rescale[..., None] + jnp.einsum(
            "rkgqt,rtkd->rkgqd",
            weights.astype(jnp.bfloat16),
            value_heads,
            preferred_element_type=jnp.float32,
        )
        return (new_max, totals, accumulated)

    running_max = jnp.full((row_count, KV_HEADS, group_size, shard_len), -1e30, jnp.float32)
    carried = (
        running_max,
        jnp.zeros_like(running_max),
        jnp.zeros((row_count, KV_HEADS, group_size, shard_len, HEAD), jnp.float32),
    )
    travel = self_pairs
    for cycle_step in range(seq_count):
        step_fn = partial(forward_block, cycle_step=cycle_step)
        carried = step_fn(carried, travel)
        if cycle_step + 1 < seq_count:
            travel = passed_along(travel, "seq", 1)
    running_max, totals, accumulated = carried
    attended = accumulated / totals[..., None]
    log_norm = running_max + jnp.log(totals)
    attended_low = (
        jnp.transpose(attended, (0, 3, 1, 2, 4))
        .reshape(flat_rows, HEADS * HEAD)
        .astype(jnp.bfloat16)
    )
    after_self = inputs + matmul_low(attended_low, self_output)
    normed_two_low = norm_rows(after_self, gain_cross).astype(jnp.bfloat16)
    cross_heads = matmul_low(normed_two_low, cross_query).astype(jnp.bfloat16)
    cross_heads = cross_heads.reshape(row_count, shard_len, KV_HEADS, group_size, HEAD)
    memory_rows = memory.reshape(-1, model_width)
    memory_pairs = (
        matmul_low(memory_rows, cross_keyvalue)
        .astype(jnp.bfloat16)
        .reshape(row_count, memory.shape[1], 2 * kv_width)
    )
    memory_all = lax.all_gather(memory_pairs, "seq", axis=1, tiled=True)
    memory_keys = memory_all[:, :, :kv_width].reshape(row_count, -1, KV_HEADS, HEAD)
    memory_values = memory_all[:, :, kv_width:].reshape(row_count, -1, KV_HEADS, HEAD)
    cross_raw = (
        jnp.einsum(
            "rqkgd,rtkd->rkgqt", cross_heads, memory_keys, preferred_element_type=jnp.float32
        )
        * 0.125
    )
    cross_max = jnp.max(cross_raw, axis=-1, keepdims=True)
    cross_exp = jnp.exp(cross_raw - cross_max)
    cross_sum = jnp.sum(cross_exp, axis=-1, keepdims=True)
    cross_log = cross_max + jnp.log(cross_sum)
    cross_prob = (cross_exp / cross_sum).astype(jnp.bfloat16)
    crossed = jnp.einsum(
        "rkgqt,rtkd->rkgqd", cross_prob, memory_values, preferred_element_type=jnp.float32
    )
    crossed_low = (
        jnp.transpose(crossed, (0, 3, 1, 2, 4))
        .reshape(flat_rows, HEADS * HEAD)
        .astype(jnp.bfloat16)
    )
    after_cross = after_self + matmul_low(crossed_low, cross_output)
    normed_three_low = norm_rows(after_cross, gain_feed).astype(jnp.bfloat16)
    gate_pre = matmul_low(normed_three_low, feed_gate)
    up_pre = matmul_low(normed_three_low, feed_up)
    hidden_low = gated_mix(gate_pre, up_pre).astype(jnp.bfloat16)
    output = after_cross + matmul_low(hidden_low, feed_down)
    layer_output = output.astype(jnp.bfloat16).reshape(row_count, shard_len, model_width)
    grad_rows = cotangent.reshape(flat_rows, model_width)
    grad_feed_down = matmul_tn(hidden_low, grad_rows)
    grad_hidden = matmul_nt(grad_rows, feed_down)
    unused_mix, mix_back = jax.vjp(gated_mix, gate_pre, up_pre)
    grad_gate, grad_up = mix_back(grad_hidden)
    gate_low = grad_gate.astype(jnp.bfloat16)
    up_low = grad_up.astype(jnp.bfloat16)
    grad_feed_gate = matmul_tn(normed_three_low, gate_low)
    grad_feed_up = matmul_tn(normed_three_low, up_low)
    grad_normed_three = matmul_nt(gate_low, feed_gate) + matmul_nt(up_low, feed_up)
    unused_three, norm_back_three = jax.vjp(norm_rows, after_cross, gain_feed)
    grad_cross_norm, grad_gain_feed = norm_back_three(grad_normed_three)
    grad_after_cross = grad_rows.astype(jnp.float32) + grad_cross_norm
    branch_two = grad_after_cross.astype(jnp.bfloat16)
    grad_cross_output = matmul_tn(crossed_low, branch_two)
    grad_crossed = matmul_nt(branch_two, cross_output).astype(jnp.bfloat16)
    grad_crossed = grad_crossed.reshape(row_count, shard_len, KV_HEADS, group_size, HEAD)
    delta_cross = jnp.einsum("rqkgd,rkgqd->rkgq", grad_crossed.astype(jnp.float32), crossed)
    again_raw = (
        jnp.einsum(
            "rqkgd,rtkd->rkgqt", cross_heads, memory_keys, preferred_element_type=jnp.float32
        )
        * 0.125
    )
    again_prob = jnp.exp(again_raw - cross_log)
    grad_cross_prob = jnp.einsum(
        "rqkgd,rtkd->rkgqt", grad_crossed, memory_values, preferred_element_type=jnp.float32
    )
    grad_cross_scores = (again_prob * (grad_cross_prob - delta_cross[..., None])).astype(
        jnp.bfloat16
    )
    grad_cross_heads = (
        jnp.einsum(
            "rkgqt,rtkd->rqkgd", grad_cross_scores, memory_keys, preferred_element_type=jnp.float32
        )
        * 0.125
    )
    grad_memory_keys = (
        jnp.einsum(
            "rkgqt,rqkgd->rtkd", grad_cross_scores, cross_heads, preferred_element_type=jnp.float32
        )
        * 0.125
    )
    grad_memory_values = jnp.einsum(
        "rkgqt,rqkgd->rtkd",
        again_prob.astype(jnp.bfloat16),
        grad_crossed,
        preferred_element_type=jnp.float32,
    )
    memory_terms = jnp.concatenate(
        [
            grad_memory_keys.reshape(row_count, -1, kv_width),
            grad_memory_values.reshape(row_count, -1, kv_width),
        ],
        axis=2,
    )
    memory_share = lax.psum_scatter(
        memory_terms.astype(jnp.bfloat16), "seq", scatter_dimension=1, tiled=True
    )
    memory_share_rows = memory_share.reshape(-1, 2 * kv_width)
    grad_cross_keyvalue = matmul_tn(memory_rows, memory_share_rows)
    memory_grad = (
        matmul_nt(memory_share_rows, cross_keyvalue).astype(jnp.bfloat16).reshape(memory.shape)
    )
    cross_heads_low = grad_cross_heads.astype(jnp.bfloat16).reshape(flat_rows, HEADS * HEAD)
    grad_cross_query = matmul_tn(normed_two_low, cross_heads_low)
    grad_normed_two = matmul_nt(cross_heads_low, cross_query)
    unused_two, norm_back_two = jax.vjp(norm_rows, after_self, gain_cross)
    grad_self_norm, grad_gain_cross = norm_back_two(grad_normed_two)
    grad_after_self = grad_after_cross + grad_self_norm
    branch_one = grad_after_self.astype(jnp.bfloat16)
    grad_self_output = matmul_tn(attended_low, branch_one)
    grad_attended = matmul_nt(branch_one, self_output).astype(jnp.bfloat16)
    grad_attended = grad_attended.reshape(row_count, shard_len, KV_HEADS, group_size, HEAD)
    delta_self = jnp.einsum("rqkgd,rkgqd->rkgq", grad_attended.astype(jnp.float32), attended)

    def backward_block(carried, travel, travel_grads, cycle_step):
        grad_queries, bias_grad = carried
        key_heads, value_heads, scores, one_hot = block_keys(travel, cycle_step)
        back_probs = jnp.exp(scores - log_norm[..., None])
        grad_probs = jnp.einsum(
            "rqkgd,rtkd->rkgqt", grad_attended, value_heads, preferred_element_type=jnp.float32
        )
        grad_scores = (back_probs * (grad_probs - delta_self[..., None])).astype(jnp.bfloat16)
        grad_queries = (
            grad_queries
            + jnp.einsum(
                "rkgqt,rtkd->rqkgd", grad_scores, key_heads, preferred_element_type=jnp.float32
            )
            * 0.125
        )
        grad_keys = (
            jnp.einsum(
                "rkgqt,rqkgd->rtkd", grad_scores, queries, preferred_element_type=jnp.float32
            )
            * 0.125
        )
        grad_values = jnp.einsum(
            "rkgqt,rqkgd->rtkd",
            back_probs.astype(jnp.bfloat16),
            grad_attended,
            preferred_element_type=jnp.float32,
        )
        travel_grads = travel_grads + jnp.concatenate(
            [
                grad_keys.reshape(row_count, shard_len, kv_width),
                grad_values.reshape(row_count, shard_len, kv_width),
            ],
            axis=2,
        )
        score_total = jnp.sum(grad_scores.astype(jnp.float32), axis=0).reshape(
            HEADS, shard_len, shard_len
        )
        bias_grad = bias_grad + jnp.einsum("bqt,hqt->bh", one_hot, score_total, precision=HIGHEST)
        return ((grad_queries, bias_grad), travel_grads)

    carried = (
        jnp.zeros((row_count, shard_len, KV_HEADS, group_size, HEAD), jnp.float32),
        jnp.zeros((BUCKETS, HEADS), jnp.float32),
    )
    travel = self_pairs
    travel_grads = jnp.zeros((row_count, shard_len, 2 * kv_width), jnp.float32)
    for cycle_step in range(seq_count):
        step_fn = partial(backward_block, cycle_step=cycle_step)
        carried, travel_grads = step_fn(carried, travel, travel_grads)
        if cycle_step + 1 < seq_count:
            travel = passed_along(travel, "seq", 1)
        travel_grads = passed_along_2(travel_grads.astype(jnp.bfloat16), "seq", 1).astype(
            travel_grads.dtype
        )
    grad_queries, bias_grad = carried
    queries_low = grad_queries.astype(jnp.bfloat16).reshape(flat_rows, HEADS * HEAD)
    pairs_low = travel_grads.astype(jnp.bfloat16).reshape(flat_rows, 2 * kv_width)
    grad_self_query = matmul_tn(normed_one_low, queries_low)
    grad_self_keyvalue = matmul_tn(normed_one_low, pairs_low)
    grad_normed_one = matmul_nt(queries_low, self_query) + matmul_nt(pairs_low, self_keyvalue)
    unused_one, norm_back_one = jax.vjp(norm_rows, inputs, gain_attend)
    grad_input_norm, grad_gain_attend = norm_back_one(grad_normed_one)
    tokens_grad = (
        (grad_after_self + grad_input_norm)
        .astype(jnp.bfloat16)
        .reshape(row_count, shard_len, model_width)
    )
    summed = (
        lax.psum_scatter(grad_self_query, ("seq", "row"), scatter_dimension=0, tiled=True),
        lax.psum_scatter(grad_self_keyvalue, ("seq", "row"), scatter_dimension=0, tiled=True),
        lax.psum_scatter(grad_self_output, ("seq", "row"), scatter_dimension=0, tiled=True),
        lax.psum_scatter(grad_cross_query, ("seq", "row"), scatter_dimension=0, tiled=True),
        lax.psum_scatter(grad_cross_keyvalue, ("seq", "row"), scatter_dimension=0, tiled=True),
        lax.psum_scatter(grad_cross_output, ("seq", "row"), scatter_dimension=0, tiled=True),
        lax.psum_scatter(grad_feed_gate, ("seq", "row"), scatter_dimension=0, tiled=True),
        lax.psum_scatter(grad_feed_up, ("seq", "row"), scatter_dimension=0, tiled=True),
        lax.psum_scatter(grad_feed_down, ("seq", "row"), scatter_dimension=0, tiled=True),
    )
    small_sums = lax.psum(
        (grad_gain_attend, grad_gain_cross, grad_gain_feed, bias_grad), ("seq", "row")
    )
    return (
        layer_output,
        tokens_grad,
        memory_grad,
        summed[0],
        summed[1],
        summed[2],
        summed[3],
        summed[4],
        summed[5],
        summed[6],
        summed[7],
        summed[8],
        small_sums[0],
        small_sums[1],
        small_sums[2],
        small_sums[3],
    )


def solution(mesh):
    in_specs = (
        P("row", "seq", None),
        P("row", "seq"),
        P("row", "seq", None),
        P("row", "seq", None),
        P(),
        P(),
        P(),
        P(),
        P(),
        P(),
        P(),
        P(),
        P(),
        P(),
        P(),
        P(),
        P(),
    )
    out_specs = (
        P("row", "seq", None),
        P("row", "seq", None),
        P("row", "seq", None),
        P(("seq", "row"), None),
        P(("seq", "row"), None),
        P(("seq", "row"), None),
        P(("seq", "row"), None),
        P(("seq", "row"), None),
        P(("seq", "row"), None),
        P(("seq", "row"), None),
        P(("seq", "row"), None),
        P(("seq", "row"), None),
        P(),
        P(),
        P(),
        P(),
    )
    return jax.shard_map(
        on_device, mesh=mesh, in_specs=in_specs, out_specs=out_specs, check_vma=False
    )
```

profile of v0, /device:TPU:0, one launch (start us, length us, event | category | flops | bytes accessed | tf_op | source)
XLA Modules:
  0.0 2180.7 jit_solution(6565067983935060971)
XLA Ops:
  32.6 76.1 %all_gather.6 = s32[2,2048]{1,0:T(2,128)S(1)} all-gather(s32[2,512]{1,0:T(2,128)S(1)} %copy-done.77), channel_id=1, replica_groups=mesh['seq'=4,'row'=8] {'seq'}, dimensions={1}, use_global_device_ids=true | all-gather | bytes 20480 | tf_op jit(solution)/shard_map/all_gather | solution.py:134
  325.0 20.3 fusion.166
  433.4 20.2 fusion.167
  453.6 22.1 %collective-permute-done.2 = bf16[2,512,1024]{2,1,0:T(8,128)(2,1)S(1)} collective-permute-done((bf16[2,512,1024]{2,1,0:T(8,128)(2,1)}, bf16[2,512,1024]{2,1,0:T(8,128)(2,1)S(1)}, u32[]{:S(2)}, u32[]{:S(2)}) %collective-permute-start.2) | collective-permute-done | bytes 2097184 | tf_op jit(solution)/shard_map/ppermute | solution.py:23
  479.7 20.7 fusion.164
  660.5 25.2 %multiply_convert_fusion = (bf16[1024,2816]{1,0:T(8,128)(2,1)}, bf16[1024,2816]{1,0:T(8,128)(2,1)}, bf16[1024,2816]{1,0:T(8,128)(2,1)}) fusion(f32[1024,2816]{1,0:T(8,128)} %fusion.168, f32[1024,2816]{1,0:T(8,128)} %fusion.169, bf16[1024,1024]{1,0:T(8,128)(2,1)} %bitcast.536, bf16[2816,1024]{1,0:T(8,128)(2,1)} %param.41), kind=kOutput, calls=%fused_computation.106 | convolution fusion | flops 5980553216 | bytes 48234496 | tf_op jit(solution)/shard_map/dot_general | solution.py:70
  843.7 25.7 %convert_reduce_fusion.2 = (f32[8,2,512,512]{2,3,1,0:T(8,128)}, bf16[2,8,2,512,512]{3,4,2,1,0:T(8,128)(2,1)}) fusion(f32[2,8,2,512]{3,2,1,0:T(2,128)S(1)} %multiply_reduce_fusion, bf16[2,512,8,64,1]{1,3,4,2,0:T(8,128)(2,1)S(1)} %bitcast.497, bf16[2,512,8,2,64]{1,0,4,3,2:T(2,128)(2,1)S(1)} %reshape.659, f32[2,8,2,512,512]{3,4,2,1,0:T(8,128)} %get-tuple-element.145, ...), kind=kOutput, calls=%fused_computation.30 | convolution fusion | flops 1119879168 | bytes 70385664 | tf_op jit(solution)/shard_map/rqkgd,rtkd->rkgqt/dot_general | solution.py:301
  876.5 26.6 %convert_reduce_fusion.1 = (f32[8,2,512,512]{2,3,1,0:T(8,128)}, bf16[2,8,2,512,512]{3,4,2,1,0:T(8,128)(2,1)}) fusion(f32[2,8,2,512]{3,2,1,0:T(2,128)S(1)} %multiply_reduce_fusion, bf16[2,512,8,64,1]{1,3,4,2,0:T(8,128)(2,1)} %bitcast.499, bf16[2,512,8,2,64]{1,0,4,3,2:T(2,128)(2,1)S(1)} %reshape.659, f32[2,8,2,512,512]{3,4,2,1,0:T(8,128)} %get-tuple-element.147, ...), kind=kOutput, calls=%fused_computation.29 | convolution fusion | flops 1119879168 | bytes 70385664 | tf_op jit(solution)/shard_map/rqkgd,rtkd->rkgqt/dot_general | solution.py:301
  903.1 26.0 %convert_reduce_fusion.3 = (f32[8,2,512,512]{2,3,1,0:T(8,128)}, bf16[2,8,2,512,512]{3,4,2,1,0:T(8,128)(2,1)}) fusion(f32[2,8,2,512]{3,2,1,0:T(2,128)S(1)} %multiply_reduce_fusion, bf16[2,512,8,64,1]{1,3,4,2,0:T(8,128)(2,1)S(1)} %bitcast.495, bf16[2,512,8,2,64]{1,0,4,3,2:T(2,128)(2,1)S(1)} %reshape.659, f32[2,8,2,512,512]{3,4,2,1,0:T(8,128)} %get-tuple-element.143, ...), kind=kOutput, calls=%fused_computation.31 | convolution fusion | flops 1119879168 | bytes 70385664 | tf_op jit(solution)/shard_map/rqkgd,rtkd->rkgqt/dot_general | solution.py:301
  957.4 26.1 %convert_reduce_fusion = (f32[8,2,512,512]{2,3,1,0:T(8,128)}, bf16[2,8,2,512,512]{3,4,2,1,0:T(8,128)(2,1)}) fusion(f32[2,8,2,512]{3,2,1,0:T(2,128)S(1)} %multiply_reduce_fusion, bf16[2,512,8,64,1]{1,3,4,2,0:T(8,128)(2,1)S(1)} %bitcast.493, bf16[2,512,8,2,64]{1,0,4,3,2:T(2,128)(2,1)S(1)} %reshape.659, f32[2,8,2,512,512]{3,4,2,1,0:T(8,128)} %get-tuple-element.141, ...), kind=kOutput, calls=%fused_computation.28 | convolution fusion | flops 1119879168 | bytes 70385664 | tf_op jit(solution)/shard_map/rqkgd,rtkd->rkgqt/dot_general | solution.py:301
  1204.3 52.5 %collective-permute-done.6 = bf16[2,512,1024]{2,1,0:T(8,128)(2,1)S(1)} collective-permute-done((bf16[2,512,1024]{2,1,0:T(8,128)(2,1)S(1)}, bf16[2,512,1024]{2,1,0:T(8,128)(2,1)S(1)}, u32[]{:S(2)}, u32[]{:S(2)}) %collective-permute-start.6) | collective-permute-done | bytes 2097184 | tf_op jit(solution)/shard_map/ppermute | solution.py:28
  1300.8 20.3 copy.350
  1321.1 20.3 copy.351
  1341.4 20.2 copy.352
  1361.6 20.3 copy.349
  1388.7 20.5 fusion.116
  1409.2 20.5 fusion.122
  1429.7 20.7 fusion.121
  1486.3 37.9 %all-reduce = (f32[1024]{0:T(1024)}, f32[1024]{0:T(1024)}, f32[1024]{0:T(1024)}, f32[32,16]{0,1:T(8,128)}) all-reduce(f32[1024]{0:T(1024)S(1)} %get-tuple-element.84, f32[1024]{0:T(1024)S(1)} %copy-done.87, f32[1024]{0:T(1024)S(1)} %copy-done.86, f32[32,16]{0,1:T(8,128)S(1)} %fusion.120), channel_id=1, replica_groups=mesh['seq'=4,'row'=8] {'seq','row'}, use_global_device_ids=true, to_apply=%region_35.36 | all-reduce | flops 3584 | bytes 28672 | tf_op jit(solution)/shard_map/psum | solution.py:375
  1530.1 42.8 %reduce-scatter.31.cloned.1.call-done = f32[32,1024]{1,0:T(8,128)} async-done(((f32[1024,1024]{1,0:T(8,128)}), f32[32,1024]{1,0:T(8,128)}) %reduce-scatter.31.cloned.1.call-update) | async-done | bytes 131088
  1572.9 139.7 %reduce-scatter.17.cloned.1.call-done = f32[32,1024]{1,0:T(8,128)} async-done(((f32[1024,1024]{1,0:T(8,128)}), f32[32,1024]{1,0:T(8,128)}) %reduce-scatter.17.cloned.1.call-update) | async-done | bytes 131088 | tf_op jit(solution)/shard_map/reduce_scatter | solution.py:366
  1712.5 154.0 %reduce-scatter.27.cloned.1.call-done = f32[32,2816]{1,0:T(8,128)} async-done(((f32[1024,2816]{1,0:T(8,128)}), f32[32,2816]{1,0:T(8,128)}) %reduce-scatter.27.cloned.1.call-update) | async-done | bytes 360464 | tf_op jit(solution)/shard_map/reduce_scatter | solution.py:372
  1866.5 153.6 %reduce-scatter.25.cloned.1.call-done = f32[32,2816]{1,0:T(8,128)} async-done(((f32[1024,2816]{1,0:T(8,128)}), f32[32,2816]{1,0:T(8,128)}) %reduce-scatter.25.cloned.1.call-update) | async-done | bytes 360464 | tf_op jit(solution)/shard_map/reduce_scatter | solution.py:371
  2020.1 153.8 %reduce-scatter.29.cloned.1.call-done = f32[88,1024]{1,0:T(8,128)} async-done(((f32[2816,1024]{1,0:T(8,128)}), f32[88,1024]{1,0:T(8,128)}) %reduce-scatter.29.cloned.1.call-update) | async-done | bytes 360464 | tf_op jit(solution)/shard_map/reduce_scatter | solution.py:373
  (415 shorter events, 999.1 us)
Async XLA Ops:
  7.2 559.9 %copy-start = (bf16[1024,1024]{1,0:T(8,128)(2,1)S(1)}, bf16[1024,1024]{1,0:T(8,128)(2,1)}, u32[]{:S(2)}) copy-start(bf16[1024,1024]{1,0:T(8,128)(2,1)} %param.36) | copy-start | bytes 6291460
  7.2 402.5 %all-gather.2.cloned.1.call-start = ((), (), s32[]{:S(2)}) async-start(), calls=%async_computation.10 | async-start | bytes 2621440 | tf_op jit(solution)/shard_map/all_gather | solution.py:192
  10.7 1085.2 %reduce-scatter.13.cloned.1.call-start = ((), (), s32[]{:S(2)}) async-start(), calls=%async_computation.11 | async-start | bytes 2621440 | tf_op jit(solution)/shard_map/reduce_scatter | solution.py:277
  20.0 299.7 %collective-permute-start = (bf16[2,512,1024]{2,1,0:T(8,128)(2,1)}, bf16[2,512,1024]{2,1,0:T(8,128)(2,1)}, u32[]{:S(2)}, u32[]{:S(2)}) collective-permute-start(bf16[2,512,1024]{2,1,0:T(8,128)(2,1)} %bitcast.3), channel_id=1, source_target_pairs={{0,8},{8,16},{16,24},{1,9},{9,17},{17,25},{2,10},{10,18},{18,26},{... | collective-permute-start | bytes 6291464 | tf_op jit(solution)/shard_map/ppermute | solution.py:23
  139.3 220.0 %copy-start.19 = (bf16[2,512,512]{1,2,0:T(8,128)(2,1)}, bf16[2,512,512]{1,2,0:T(8,128)(2,1)S(1)}, u32[]{:S(2)}) copy-start(bf16[2,512,512]{1,2,0:T(8,128)(2,1)S(1)} %copy.276) | copy-start | bytes 3145732
  319.7 223.5 %copy-start.57 = (f32[2,8,2,512]{3,2,1,0:T(2,128)}, f32[2,8,2,512]{3,2,1,0:T(2,128)S(1)}, u32[]{:S(2)}) copy-start(f32[2,8,2,512]{3,2,1,0:T(2,128)S(1)} %get-tuple-element.142) | copy-start | bytes 196612
  346.1 154.2 %copy-start.50 = (f32[2,8,2,512]{3,2,1,0:T(2,128)}, f32[2,8,2,512]{3,2,1,0:T(2,128)S(1)}, u32[]{:S(2)}) copy-start(f32[2,8,2,512]{3,2,1,0:T(2,128)S(1)} %get-tuple-element.99) | copy-start | bytes 196612
  359.3 183.9 %copy-start.59 = (f32[2,8,2,512]{3,2,1,0:T(2,128)}, f32[2,8,2,512]{3,2,1,0:T(2,128)S(1)}, u32[]{:S(2)}) copy-start(f32[2,8,2,512]{3,2,1,0:T(2,128)S(1)} %fusion.24) | copy-start | bytes 196612
  376.3 47.0 %collective-permute-start.1 = (bf16[2,512,1024]{2,1,0:T(8,128)(2,1)}, bf16[2,512,1024]{2,1,0:T(8,128)(2,1)}, u32[]{:S(2)}, u32[]{:S(2)}) collective-permute-start(bf16[2,512,1024]{2,1,0:T(8,128)(2,1)} %collective-permute-done), channel_id=1, source_target_pairs={{0,8},{8,16},{16,24},{1,9},{9,17},{17,25},{2,10},{10,18},{18,26},{... | collective-permute-start | bytes 6291464 | tf_op jit(solution)/shard_map/ppermute | solution.py:23
  428.9 46.8 %collective-permute-start.2 = (bf16[2,512,1024]{2,1,0:T(8,128)(2,1)}, bf16[2,512,1024]{2,1,0:T(8,128)(2,1)S(1)}, u32[]{:S(2)}, u32[]{:S(2)}) collective-permute-start(bf16[2,512,1024]{2,1,0:T(8,128)(2,1)} %collective-permute-done.1), channel_id=1, source_target_pairs={{0,8},{8,16},{16,24},{1,9},{9,17},{17,25},{2,10},{10,18},{18,26},{... | collective-permute-start | bytes 6291464 | tf_op jit(solution)/shard_map/ppermute | solution.py:23
  784.2 745.8 %reduce-scatter.23.cloned.1.call-start = ((), (), s32[]{:S(2)}) async-start(), calls=%async_computation.16 | async-start | bytes 4325376 | tf_op jit(solution)/shard_map/reduce_scatter | solution.py:370
  791.5 738.5 %reduce-scatter.21.cloned.1.call-start = ((), (), s32[]{:S(2)}) async-start(), calls=%async_computation.15 | async-start | bytes 4325376 | tf_op jit(solution)/shard_map/reduce_scatter | solution.py:368
  834.4 695.7 %reduce-scatter.19.cloned.1.call-start = ((), (), s32[]{:S(2)}) async-start(), calls=%async_computation.14 | async-start | bytes 4325376 | tf_op jit(solution)/shard_map/reduce_scatter | solution.py:367
  929.1 600.9 %reduce-scatter.15.cloned.1.call-start = ((), (), s32[]{:S(2)}) async-start(), calls=%async_computation.12 | async-start | bytes 4325376 | tf_op jit(solution)/shard_map/reduce_scatter | solution.py:365
  1004.6 568.3 %reduce-scatter.31.cloned.1.call-start = ((), (), s32[]{:S(2)}) async-start(), calls=%async_computation.20 | async-start | bytes 4325376
  1035.7 55.0 %collective-permute-start.3 = (bf16[2,512,1024]{2,1,0:T(8,128)(2,1)}, bf16[2,512,1024]{2,1,0:T(8,128)(2,1)}, u32[]{:S(2)}, u32[]{:S(2)}) collective-permute-start(bf16[2,512,1024]{2,1,0:T(8,128)(2,1)} %pad_maximum_fusion), channel_id=1, source_target_pairs={{0,8},{8,16},{16,24},{24,0},{1,9},{9,17},{17,25},{25,1},{2,10},{10... | collective-permute-start | bytes 6291464 | tf_op jit(solution)/shard_map/ppermute | solution.py:28
  1095.6 45.6 %collective-permute-start.4 = (bf16[2,512,1024]{2,1,0:T(8,128)(2,1)}, bf16[2,512,1024]{2,1,0:T(8,128)(2,1)}, u32[]{:S(2)}, u32[]{:S(2)}) collective-permute-start(bf16[2,512,1024]{2,1,0:T(8,128)(2,1)} %fusion.88), channel_id=1, source_target_pairs={{0,8},{8,16},{16,24},{24,0},{1,9},{9,17},{17,25},{25,1},{2,10},{10... | collective-permute-start | bytes 6291464 | tf_op jit(solution)/shard_map/ppermute | solution.py:28
  1105.1 607.5 %reduce-scatter.17.cloned.1.call-start = ((), (), s32[]{:S(2)}) async-start(), calls=%async_computation.13 | async-start | bytes 4325376 | tf_op jit(solution)/shard_map/reduce_scatter | solution.py:366
  1146.2 55.1 %collective-permute-start.5 = (bf16[2,512,1024]{2,1,0:T(8,128)(2,1)}, bf16[2,512,1024]{2,1,0:T(8,128)(2,1)}, u32[]{:S(2)}, u32[]{:S(2)}) collective-permute-start(bf16[2,512,1024]{2,1,0:T(8,128)(2,1)} %fusion.89), channel_id=1, source_target_pairs={{0,8},{8,16},{16,24},{24,0},{1,9},{9,17},{17,25},{25,1},{2,10},{10... | collective-permute-start | bytes 6291464 | tf_op jit(solution)/shard_map/ppermute | solution.py:28
  1204.2 52.6 %collective-permute-start.6 = (bf16[2,512,1024]{2,1,0:T(8,128)(2,1)S(1)}, bf16[2,512,1024]{2,1,0:T(8,128)(2,1)S(1)}, u32[]{:S(2)}, u32[]{:S(2)}) collective-permute-start(bf16[2,512,1024]{2,1,0:T(8,128)(2,1)S(1)} %fusion.90), channel_id=1, source_target_pairs={{0,8},{8,16},{16,24},{24,0},{1,9},{9,17},{17,25},{25,1},{2,10},{10... | collective-permute-start | bytes 6291464 | tf_op jit(solution)/shard_map/ppermute | solution.py:28
  1262.6 603.9 %reduce-scatter.27.cloned.1.call-start = ((), (), s32[]{:S(2)}) async-start(), calls=%async_computation.18 | async-start | bytes 11894784 | tf_op jit(solution)/shard_map/reduce_scatter | solution.py:372
  1275.8 744.4 %reduce-scatter.25.cloned.1.call-start = ((), (), s32[]{:S(2)}) async-start(), calls=%async_computation.17 | async-start | bytes 11894784 | tf_op jit(solution)/shard_map/reduce_scatter | solution.py:371
  1287.6 886.3 %reduce-scatter.29.cloned.1.call-start = ((), (), s32[]{:S(2)}) async-start(), calls=%async_computation.19 | async-start | bytes 11894784 | tf_op jit(solution)/shard_map/reduce_scatter | solution.py:373
  1524.2 649.7 %copy-start.1 = (bf16[1024,1024]{1,0:T(8,128)(2,1)S(1)}, bf16[1024,1024]{1,0:T(8,128)(2,1)}, u32[]{:S(2)}) copy-start(bf16[1024,1024]{1,0:T(8,128)(2,1)} %param.36) | copy-start | bytes 6291460
  (106 other events, 1314.4 us)
Sparse Core Ops, SparseCore 0:
  10.8 74.8 all-gather.1
  784.3 45.6 reduce-scatter.12
  833.0 140.5 reduce-scatter.22
  976.4 144.3 reduce-scatter.20
  1123.6 168.8 reduce-scatter.18
  1295.3 137.4 reduce-scatter.14
  1435.7 137.0 reduce-scatter.30
  1575.8 136.6 reduce-scatter.16
  1715.5 150.9 reduce-scatter.26
  1869.4 150.7 reduce-scatter.24
  2023.1 150.7 reduce-scatter.28
where the time goes:
time: 2190 us; the launch traced here: 2180 us
  matrix products  802 us (37%)
  waiting for transfers between devices  767 us (35%)
  local copies, waits for them, and re-layouts  304 us (14%)
  other arithmetic  155 us (7%)
  blocking collectives  114 us (5%)
  starting transfers between devices  22 us (1%)
    reduce_scatter x1, waiting for transfers between devices, on_device(): lax.psum_scatter(grad_feed_up, ('seq', 'row'), scatter_dimension=0, tiled...  154 us
    reduce_scatter x1, waiting for transfers between devices, on_device(): lax.psum_scatter(grad_feed_down, ('seq', 'row'), scatter_dimension=0, til...  154 us
    reduce_scatter x1, waiting for transfers between devices, on_device(): lax.psum_scatter(grad_feed_gate, ('seq', 'row'), scatter_dimension=0, til...  154 us
    reduce_scatter x1, waiting for transfers between devices, on_device(): lax.psum_scatter(grad_self_keyvalue, ('seq', 'row'), scatter_dimension=0,...  140 us
    dot_general x4, matrix products, backward_block(): jnp.einsum('rqkgd,rtkd->rkgqt', grad_attended, value_heads, preferred_ele...  104 us
    ppermute x4, waiting for transfers between devices, passed_along_2(): lax.ppermute(shard, axis, [(i, (i + by) % devices) for i in range(devices)])  94 us
    reshape x4, local copies, waits for them, and re-layouts, backward_block(): jnp.sum(grad_scores.astype(jnp.float32), axis=0)  81.1 us
    dot_general x4, matrix products, self_scores(): jnp.einsum('rqkgd,rtkd->rkgqt', queries, key_heads, preferred_element_typ...  80.9 us
  transfers between devices with their start and end apart: 18, of which 11 were waited for; matrix products, arithmetic and copies ran while one was open for 43% of the time, Pallas kernels for 0%

commit v1 on v0

v1 whole, which is shorter than its diff:
```python
import functools
import math

import jax
import jax.numpy as jnp
import numpy as np
from jax import lax
from jax.experimental import pallas as pl
from jax.experimental.pallas import tpu as pltpu
from jax.sharding import PartitionSpec as P

HEADS = 16
BUCKETS = 32
MAX_DIST = 128
HIGHEST = lax.Precision.HIGHEST
F32, BF16 = jnp.float32, jnp.bfloat16
MASK = -float(2.0**100)
NEAR = 128
VMEM = 56 * 1024 * 1024
GELU_A = math.sqrt(2.0 / math.pi)
GELU_B = GELU_A * 0.044715


def bucket_level(distance):
    exact_part = BUCKETS // 2
    if distance < exact_part:
        return distance
    which_bucket = exact_part + math.floor(
        math.log(distance / exact_part) / math.log(MAX_DIST / exact_part) * (BUCKETS - exact_part)
    )
    return min(BUCKETS - 1, which_bucket)


def call(kernel, inputs, in_specs, out_shape, out_specs, name, flops, grid=(), scratch=(), prefetch=0,
         hold=(), after=(), alias=None):
    hold, after = list(hold), list(after)
    count_in, count_out = len(inputs), len(out_shape)
    anywhere = pl.BlockSpec(memory_space=pl.ANY)

    def body(*refs):
        kept = count_in + len(hold) + len(after)
        kernel(*refs[:count_in], *refs[kept:kept + count_out], *refs[kept + count_out + len(hold):])

    aliases = {count_in + i: count_out + i for i in range(len(hold))}
    aliases.update(alias or {})
    outs = pl.pallas_call(
        body,
        grid_spec=pltpu.PrefetchScalarGridSpec(
            num_scalar_prefetch=prefetch,
            grid=grid,
            in_specs=list(in_specs) + [anywhere] * (len(hold) + len(after)),
            out_specs=list(out_specs) + [anywhere] * len(hold),
            scratch_shapes=list(scratch),
        ),
        out_shape=list(out_shape) + [jax.ShapeDtypeStruct(x.shape, x.dtype) for x in hold],
        input_output_aliases=aliases,
        compiler_params=pltpu.CompilerParams(vmem_limit_bytes=VMEM),
        cost_estimate=pl.CostEstimate(flops=int(flops), bytes_accessed=10**7, transcendentals=0),
        name=name,
    )(*inputs, *hold, *after)
    return list(outs[:count_out]), list(outs[count_out:])


def nt(a, b):
    return lax.dot_general(a, b, (((1,), (1,)), ((), ())), preferred_element_type=F32)


def nn(a, b):
    return jnp.dot(a, b, preferred_element_type=F32)


def tn(a, b):
    return lax.dot_general(a, b, (((0,), (0,)), ((), ())), preferred_element_type=F32)


def halves(block):
    low = lax.broadcasted_iota(jnp.int32, block.shape, 1) < 64
    zero = jnp.zeros_like(block)
    return jnp.where(low, block, zero), jnp.where(low, zero, block)


def lanes(a, b):
    return jnp.concatenate([a, b], axis=1)


def rows(a, b):
    return jnp.concatenate([a, b], axis=0)


def chunk_of(member, part, chunks):
    return jnp.where(part == 0, member, chunks - 1 - member)


def slot_of(member, chunk, chunks):
    high = (chunk >= chunks // 2).astype(jnp.int32)
    other = jnp.where(chunk >= chunks // 2, chunks - 1 - chunk, chunk)
    return 2 * jnp.bitwise_xor(other, member) + high


def first_block(meta, member, chunk, chunks):
    mine = meta[1 + slot_of(member, chunk, chunks)]

    def skip(block, start):
        last = meta[1 + chunks + slot_of(member, block, chunks)]
        return start + jnp.where((block < chunk) & (last < mine), 1, 0)

    return lax.fori_loop(0, chunks, skip, jnp.int32(0))


def self_forward_kernel(chunks, sub, meta, q_ref, k_ref, v_ref, qf_ref, kf_ref, near_ref, corner_ref,
                        o_ref, lse_ref, acc_ref, m_ref):
    size = q_ref.shape[0]
    member = meta[0]
    chunk = chunk_of(member, pl.program_id(1), chunks)
    q_both = [lanes(part, qf_ref[...]) for part in halves(q_ref[...])]

    def values(at, length):
        low, high = halves(v_ref[pl.ds(at, length), :])
        one_low, one_high = halves(jnp.ones((length, 128), BF16))
        return rows(lanes(low, one_low), lanes(high, one_high))

    own = pl.multiple_of(slot_of(member, chunk, chunks) * size, size)
    for strip in range(size // sub):
        span = (strip + 1) * sub
        here = slice(strip * sub, span)
        keys = lanes(k_ref[pl.ds(own, span), :], kf_ref[pl.ds(own, span), :])
        weights = []
        for head in range(2):
            s = nt(q_both[head][here], keys)
            last = s[:, span - sub:] + near_ref[head]
            if strip:
                edge = s[:, span - sub - NEAR:span - sub]
                edge = rows(edge[:NEAR] + corner_ref[head], edge[NEAR:])
                s = jnp.concatenate([s[:, :span - sub - NEAR], edge, last], axis=1)
            else:
                s = last
            top = jnp.max(s, axis=1, keepdims=True)
            m_ref[head, here, :] = jnp.broadcast_to(top, (sub, 128))
            weights.append(jnp.exp(s - top).astype(BF16))
        acc_ref[here, :] = nn(lanes(*weights), values(own, span))

    def far(block, carry):
        at = pl.multiple_of(slot_of(member, block, chunks) * size, size)
        keys = lanes(k_ref[pl.ds(at, size), :], kf_ref[pl.ds(at, size), :])
        flag = jnp.where(block == chunk - 1, 1.0, 0.0).astype(F32)
        weights, scales = [], []
        for head in range(2):
            s = nt(q_both[head], keys)
            edge = s[:NEAR, size - NEAR:] + corner_ref[head] * flag
            s = rows(lanes(s[:NEAR, :size - NEAR], edge), s[NEAR:])
            old = m_ref[head]
            top = jnp.maximum(old, jnp.max(s, axis=1, keepdims=True))
            scales.append(jnp.exp(old - top))
            m_ref[head] = top
            weights.append(jnp.exp(s - top[:, :1]).astype(BF16))
        low = lax.broadcasted_iota(jnp.int32, (size, 128), 1) < 64
        scale = jnp.where(low, scales[0], scales[1])
        acc_ref[...] = acc_ref[...] * lanes(scale, scale) + nn(lanes(*weights), values(at, size))
        return carry

    lax.fori_loop(first_block(meta, member, chunk, chunks), chunk, far, 0)
    low = lax.broadcasted_iota(jnp.int32, (size, 128), 1) < 64
    total = acc_ref[:, 128:]
    o_ref[...] = (acc_ref[:, :128] / total).astype(BF16)
    lse_ref[...] = jnp.where(low, m_ref[0], m_ref[1]) + jnp.log(total)


def pieces(column, shape):
    lane = lax.broadcasted_iota(jnp.int32, shape, 1)
    high = column.astype(BF16).astype(F32)
    rest = column - high
    middle = rest.astype(BF16).astype(F32)
    low = rest - middle
    full = jnp.where(lane == 4, high, jnp.where(lane == 5, middle, jnp.where(lane == 6, low, 0.0)))
    return full.astype(BF16)


def back_operands(q_ref, do_ref, o_ref, lse_ref, qf):
    shape = q_ref.shape
    q_both = halves(q_ref[...])
    do_both = halves(do_ref[...])
    product = do_ref[...].astype(F32) * o_ref[...].astype(F32)
    low = lax.broadcasted_iota(jnp.int32, shape, 1) < 64
    deltas = [jnp.sum(jnp.where(low, product, 0.0), axis=1, keepdims=True),
              jnp.sum(jnp.where(low, 0.0, product), axis=1, keepdims=True)]
    logs = [lse_ref[:, 0:1], lse_ref[:, 64:65]]
    extra = [pieces(log, shape) for log in logs]
    if qf is not None:
        extra = [part + qf for part in extra]
    q_wide = [lanes(part, more) for part, more in zip(q_both, extra)]
    do_wide = [lanes(part, pieces(delta, shape)) for part, delta in zip(do_both, deltas)]
    return q_both, do_both, q_wide, do_wide


def diagonal_sums(block):
    count, wide = block.shape[0], 2 * block.shape[1]
    block = lanes(block, jnp.zeros_like(block))
    while count > 8:
        count = count // 2
        block = block[:count] + pltpu.roll(block[count:], wide - count, 1)
    return block


def self_backward_kernel(chunks, sub, meta, q_ref, do_ref, o_ref, lse_ref, k_ref, v_ref, qf_ref, kf_ref,
                         near_ref, corner_ref, dq_ref, dkv_ref, near_out, corner_out,
                         dq_acc, dk_acc, dv_acc, near_acc, corner_acc):
    size = q_ref.shape[0]
    member = meta[0]
    chunk = chunk_of(member, pl.program_id(2), chunks)
    first = (pl.program_id(1) == 0) & (pl.program_id(2) == 0)
    last = (pl.program_id(1) == 1) & (pl.program_id(2) == 1)

    @pl.when(first)
    def _():
        dk_acc[...] = jnp.zeros_like(dk_acc)
        dv_acc[...] = jnp.zeros_like(dv_acc)

    @pl.when(pl.program_id(2) == 0)
    def _():
        near_acc[...] = jnp.zeros_like(near_acc)
        corner_acc[...] = jnp.zeros_like(corner_acc)

    q_both, do_both, q_wide, do_wide = back_operands(q_ref, do_ref, o_ref, lse_ref, qf_ref[...])
    own = pl.multiple_of(slot_of(member, chunk, chunks) * size, size)
    dq_acc[...] = jnp.zeros_like(dq_acc)

    def add(at, length, here, weights, grads, keys):
        dv_acc[pl.ds(at, length), :] += nn(lanes(*weights), rows(do_both[0][here], do_both[1][here]))
        dk_acc[pl.ds(at, length), :] += nn(lanes(*grads), rows(q_both[0][here], q_both[1][here]))
        dq_acc[here, :] += tn(rows(*grads), rows(*halves(keys)))

    for strip in range(size // sub):
        at = pl.multiple_of(own + strip * sub, sub)
        here = slice(strip * sub, size)
        k, v, kf = (ref[pl.ds(at, sub), :] for ref in (k_ref, v_ref, kf_ref))
        keys, vals = lanes(k, kf), lanes(v, kf)
        weights, grads = [], []
        for head in range(2):
            s = nt(keys, q_wide[head][here])
            dp = nt(vals, do_wide[head][here])
            block = s[:, :sub] + near_ref[head]
            more = (strip + 1) * sub < size
            if more:
                edge = s[sub - NEAR:, sub:sub + NEAR] + corner_ref[head]
                rest = s[:, sub:]
                rest = rows(rest[:sub - NEAR], lanes(edge, rest[sub - NEAR:, NEAR:]))
                s = lanes(block, rest)
            else:
                s = block
            p = jnp.exp(s)
            ds = p * dp
            near_acc[head] += ds[:, :sub]
            if more:
                corner_acc[head] += ds[sub - NEAR:, sub:sub + NEAR]
            weights.append(p.astype(BF16))
            grads.append(ds.astype(BF16))
        add(at, sub, here, weights, grads, k)

    def far(block, carry):
        at = pl.multiple_of(slot_of(member, block, chunks) * size, size)
        k, v, kf = (ref[pl.ds(at, size), :] for ref in (k_ref, v_ref, kf_ref))
        keys, vals = lanes(k, kf), lanes(v, kf)
        flag = jnp.where(block == chunk - 1, 1.0, 0.0).astype(F32)
        weights, grads = [], []
        for head in range(2):
            s = nt(keys, q_wide[head])
            dp = nt(vals, do_wide[head])
            edge = s[size - NEAR:, :NEAR] + corner_ref[head] * flag
            s = rows(s[:size - NEAR], lanes(edge, s[size - NEAR:, NEAR:]))
            p = jnp.exp(s)
            ds = p * dp
            corner_acc[head] += ds[size - NEAR:, :NEAR] * flag
            weights.append(p.astype(BF16))
            grads.append(ds.astype(BF16))
        add(at, size, slice(None), weights, grads, k)
        return carry

    lax.fori_loop(first_block(meta, member, chunk, chunks), chunk, far, 0)
    dq_ref[...] = (dq_acc[...] * 0.125).astype(BF16)

    @pl.when(last)
    def _():
        dkv_ref[0] = dk_acc[...].astype(BF16)
        dkv_ref[1] = dv_acc[...].astype(BF16)

    @pl.when(pl.program_id(2) == 1)
    def _():
        for head in range(2):
            near_out[head] = diagonal_sums(near_acc[head])
            corner_out[head] = diagonal_sums(corner_acc[head])


def self_forward(meta, q, kv, qf, kf, near, corner, chunks, hold=(), after=()):
    size = q.shape[0] // 2
    sub = min(256, size)
    length = kv.shape[0]
    own = pl.BlockSpec((size, 128), lambda b, c, m: (c, b))
    return call(
        functools.partial(self_forward_kernel, chunks, sub),
        (meta, q, kv, kv, qf, kf, near, corner),
        [
            own,
            pl.BlockSpec((length, 128), lambda b, c, m: (0, b // 2)),
            pl.BlockSpec((length, 128), lambda b, c, m: (0, 4 + b // 2)),
            pl.BlockSpec((size, 128), lambda b, c, m: (c, 0)),
            pl.BlockSpec((length, 128), lambda b, c, m: (0, 0)),
            pl.BlockSpec((2, sub, sub), lambda b, c, m: (b, 0, 0)),
            pl.BlockSpec((2, NEAR, NEAR), lambda b, c, m: (b, 0, 0)),
        ],
        [jax.ShapeDtypeStruct(q.shape, BF16), jax.ShapeDtypeStruct(q.shape, F32)],
        [own, own],
        "self_forward", 4e10, grid=(8, 2), prefetch=1, hold=hold, after=after,
        scratch=[pltpu.VMEM((size, 256), F32), pltpu.VMEM((2, size, 128), F32)],
    )


def self_backward(meta, q, do, o, lse, kv, qf, kf, near, corner, chunks, part, parts, before, hold=(), after=()):
    pairs = 4 // parts
    shift = pairs * part
    size = q.shape[0] // 2
    sub = min(256, size)
    length = kv.shape[0]
    own = pl.BlockSpec((size, 128), lambda g, b, c, m: (c, 2 * (g + shift) + b))
    inputs = [meta, q, do, o, lse, kv, kv, qf, kf, near, corner]
    in_specs = [
        own, own, own, own,
        pl.BlockSpec((length, 128), lambda g, b, c, m: (0, g + shift)),
        pl.BlockSpec((length, 128), lambda g, b, c, m: (0, 4 + g + shift)),
        pl.BlockSpec((size, 128), lambda g, b, c, m: (c, 0)),
        pl.BlockSpec((length, 128), lambda g, b, c, m: (0, 0)),
        pl.BlockSpec((2, sub, sub), lambda g, b, c, m: (2 * (g + shift) + b, 0, 0)),
        pl.BlockSpec((2, NEAR, NEAR), lambda g, b, c, m: (2 * (g + shift) + b, 0, 0)),
    ]
    kernel = functools.partial(self_backward_kernel, chunks, sub)
    alias = None
    if before is not None:
        count = len(inputs)
        alias = {count + i: i for i in range(len(before))}
        inputs += before
        in_specs += [pl.BlockSpec(memory_space=pl.ANY)] * len(before)
        inner = kernel

        def kernel(*refs):
            inner(*refs[:count], *refs[count + len(before):])

    return call(
        kernel, tuple(inputs), in_specs,
        [
            jax.ShapeDtypeStruct(q.shape, BF16),
            jax.ShapeDtypeStruct((2, length, 512), BF16),
            jax.ShapeDtypeStruct((16, 8, 2 * sub), F32),
            jax.ShapeDtypeStruct((16, 8, 2 * NEAR), F32),
        ],
        [
            own,
            pl.BlockSpec((2, length, 128), lambda g, b, c, m: (0, 0, g + shift)),
            pl.BlockSpec((2, 8, 2 * sub), lambda g, b, c, m: (2 * (g + shift) + b, 0, 0)),
            pl.BlockSpec((2, 8, 2 * NEAR), lambda g, b, c, m: (2 * (g + shift) + b, 0, 0)),
        ],
        "self_backward", 6e10 / parts, grid=(pairs, 2, 2), prefetch=1, hold=hold, after=after, alias=alias,
        scratch=[
            pltpu.VMEM((size, 128), F32),
            pltpu.VMEM((length, 128), F32),
            pltpu.VMEM((length, 128), F32),
            pltpu.VMEM((2, sub, sub), F32),
            pltpu.VMEM((2, NEAR, NEAR), F32),
        ],
    )


def cross_forward_kernel(q_ref, k_ref, v_ref, o_ref, lse_ref):
    length = k_ref.shape[0]
    keys = k_ref[...]
    low, high = halves(v_ref[...])
    one_low, one_high = halves(jnp.ones((length, 128), BF16))
    values = rows(lanes(low, one_low), lanes(high, one_high))
    weights, tops = [], []
    for part in halves(q_ref[...]):
        s = nt(part, keys)
        top = jnp.max(s, axis=1, keepdims=True)
        tops.append(top)
        weights.append(jnp.exp(s - top).astype(BF16))
    acc = nn(lanes(*weights), values)
    is_low = lax.broadcasted_iota(jnp.int32, q_ref.shape, 1) < 64
    total = acc[:, 128:]
    o_ref[...] = (acc[:, :128] / total).astype(BF16)
    lse_ref[...] = jnp.where(is_low, tops[0], tops[1]) + jnp.log(total)


def cross_backward_kernel(q_ref, do_ref, o_ref, lse_ref, k_ref, v_ref, dq_ref, dkv_ref, dk_acc, dv_acc):
    first = (pl.program_id(1) == 0) & (pl.program_id(2) == 0)
    last = (pl.program_id(1) == 1) & (pl.program_id(2) == 1)

    @pl.when(first)
    def _():
        dk_acc[...] = jnp.zeros_like(dk_acc)
        dv_acc[...] = jnp.zeros_like(dv_acc)

    q_both, do_both, q_wide, do_wide = back_operands(q_ref, do_ref, o_ref, lse_ref, None)
    k = k_ref[...]
    lane = lax.broadcasted_iota(jnp.int32, k.shape, 1)
    minus = jnp.where((lane >= 4) & (lane < 7), -1.0, 0.0).astype(BF16)
    keys, vals = lanes(k, minus), lanes(v_ref[...], minus)
    weights, grads = [], []
    for head in range(2):
        p = jnp.exp(nt(keys, q_wide[head]))
        ds = p * nt(vals, do_wide[head])
        weights.append(p.astype(BF16))
        grads.append(ds.astype(BF16))
    dv_acc[...] += nn(lanes(*weights), rows(*do_both))
    dk_acc[...] += nn(lanes(*grads), rows(*q_both))
    dq_ref[...] = (tn(rows(*grads), rows(*halves(k))) * 0.125).astype(BF16)

    @pl.when(last)
    def _():
        dkv_ref[0] = dk_acc[...].astype(BF16)
        dkv_ref[1] = dv_acc[...].astype(BF16)


def cross_forward(q, kv, hold=(), after=()):
    size, length = q.shape[0] // 2, kv.shape[0]
    own = pl.BlockSpec((size, 128), lambda b, c: (c, b))
    return call(
        cross_forward_kernel, (q, kv, kv),
        [
            own,
            pl.BlockSpec((length, 128), lambda b, c: (0, b // 2)),
            pl.BlockSpec((length, 128), lambda b, c: (0, 4 + b // 2)),
        ],
        [jax.ShapeDtypeStruct(q.shape, BF16), jax.ShapeDtypeStruct(q.shape, F32)],
        [own, own],
        "cross_forward", 15e9, grid=(8, 2), hold=hold, after=after,
    )


def cross_backward(q, do, o, lse, kv, hold=(), after=()):
    size, length = q.shape[0] // 2, kv.shape[0]
    own = pl.BlockSpec((size, 128), lambda g, b, c: (c, 2 * g + b))
    return call(
        cross_backward_kernel, (q, do, o, lse, kv, kv),
        [
            own, own, own, own,
            pl.BlockSpec((length, 128), lambda g, b, c: (0, g)),
            pl.BlockSpec((length, 128), lambda g, b, c: (0, 4 + g)),
        ],
        [jax.ShapeDtypeStruct(q.shape, BF16), jax.ShapeDtypeStruct((2, length, 512), BF16)],
        [own, pl.BlockSpec((2, length, 128), lambda g, b, c: (0, 0, g))],
        "cross_backward", 30e9, grid=(4, 2, 2), hold=hold, after=after,
        scratch=[pltpu.VMEM((length, 128), F32), pltpu.VMEM((length, 128), F32)],
    )


def bias_kernel(sub, near_ref, corner_ref, near_out, back_out, corner_out, corner_back):
    for head in range(2):
        wide = jnp.broadcast_to(near_ref[head, :1], (sub, 2 * sub))
        block = pltpu.roll(wide, 0, 1, stride=1, stride_axis=0)[:, :sub]
        back_out[head] = block
        near_out[head] = block.T
        wide = jnp.broadcast_to(corner_ref[head, :1], (NEAR, 2 * NEAR))
        block = pltpu.roll(wide, 0, 1, stride=1, stride_axis=0)[:, :NEAR]
        corner_back[head] = block
        corner_out[head] = block.T


def bias_tiles(near, corner, sub):
    def spec(a, b):
        return pl.BlockSpec((2, a, b), lambda h: (h, 0, 0))

    def shape(a):
        return jax.ShapeDtypeStruct((16, a, a), F32)

    return pl.pallas_call(
        functools.partial(bias_kernel, sub),
        grid=(8,),
        in_specs=[spec(8, 2 * sub), spec(8, 2 * NEAR)],
        out_specs=[spec(sub, sub), spec(sub, sub), spec(NEAR, NEAR), spec(NEAR, NEAR)],
        out_shape=[shape(sub), shape(sub), shape(NEAR), shape(NEAR)],
        compiler_params=pltpu.CompilerParams(vmem_limit_bytes=VMEM),
        name="bias_tiles",
    )(near, corner)


def inverse_rms(h):
    return lax.rsqrt(jnp.mean(h * h, axis=1, keepdims=True) + 1e-06)


def norm(values, gain):
    return (values * inverse_rms(values) * gain).astype(BF16)


def norm_back(h, dn, gain):
    scale = inverse_rms(h)
    unit = h * scale
    spread = dn * unit
    share = jnp.mean(spread * gain, axis=1, keepdims=True)
    gain_part = jnp.sum(spread.reshape(-1, 8, spread.shape[1]), axis=0)
    return scale * (dn * gain - unit * share), gain_part


def entry_kernel(x_ref, gain_ref, weight_ref, n_ref, kv_ref):
    n_ref[...] = norm(x_ref[...].astype(F32), gain_ref[...])
    kv_ref[...] = nn(n_ref[...], weight_ref[...]).astype(BF16)


def middle_kernel(x_ref, o_ref, out_ref, gain_ref, query_ref, h_ref, n_ref, c_ref):
    h = x_ref[...].astype(F32) + nn(o_ref[...], out_ref[...])
    h_ref[...] = h
    n_ref[...] = norm(h, gain_ref[...])
    c_ref[...] = nn(n_ref[...], query_ref[...]).astype(BF16) * BF16(0.125)


def back_middle_kernel(dc_ref, query_ref, h_ref, gain_ref, dh_ref, out_ref, dh1_ref, r_ref, do_ref, dgain_ref):
    @pl.when(pl.program_id(0) == 0)
    def _():
        dgain_ref[...] = jnp.zeros_like(dgain_ref)

    back, part = norm_back(h_ref[...], nt(dc_ref[...], query_ref[...]), gain_ref[...])
    dgain_ref[...] += part
    dh1 = dh_ref[...] + back
    dh1_ref[...] = dh1
    r_ref[...] = dh1.astype(BF16)
    do_ref[...] = nt(r_ref[...], out_ref[...]).astype(BF16)


def exit_kernel(dq_ref, query_ref, dkv_ref, keyvalue_ref, x_ref, gain_ref, dh_ref, dx_ref, dgain_ref):
    @pl.when(pl.program_id(0) == 0)
    def _():
        dgain_ref[...] = jnp.zeros_like(dgain_ref)

    dn = nt(dq_ref[...], query_ref[...]) + nt(dkv_ref[...], keyvalue_ref[...])
    back, part = norm_back(x_ref[...].astype(F32), dn, gain_ref[...])
    dgain_ref[...] += part
    dx_ref[...] = (dh_ref[...] + back).astype(BF16)


def by_rows(kernel, name, flops, arrays, outs, width, dgain=False, hold=(), after=()):
    tokens = next(x.shape[0] for x, cut in arrays if cut)
    tile = min(256, tokens)
    blocks = pl.BlockSpec((tile, width), lambda i: (i, 0))
    in_specs = [blocks if cut else pl.BlockSpec(x.shape, lambda i: (0, 0)) for x, cut in arrays]
    shapes = [jax.ShapeDtypeStruct((tokens, width), kind) for kind in outs]
    specs = [blocks] * len(outs)
    if dgain:
        shapes.append(jax.ShapeDtypeStruct((8, width), F32))
        specs.append(pl.BlockSpec((8, width), lambda i: (0, 0)))
    return call(kernel, tuple(x for x, _ in arrays), in_specs, shapes, specs, name, flops,
                grid=(tokens // tile,), hold=hold, after=after)


def feed_kernel(tile_rows, h1_ref, co_ref, cross_ref, g_ref, gain_ref, gate_ref, up_ref, down_ref,
                out_ref, n_ref, hidden_ref, dgu_ref, dh_ref, low_ref, dco_ref, dgain_ref,
                out_acc, dn_acc, h_acc):
    tokens, width = h1_ref.shape
    count = tokens // tile_rows
    tile = gate_ref.shape[1]
    step = pl.program_id(0)

    def each(body):
        def one(i, carry):
            body(pl.ds(pl.multiple_of(i * tile_rows, tile_rows), tile_rows))
            return carry

        lax.fori_loop(0, count, one, 0)

    @pl.when(step == 0)
    def _():
        def start(at):
            h = h1_ref[at, :] + nn(co_ref[at, :], cross_ref[...])
            h_acc[at, :] = h
            n_ref[at, :] = norm(h, gain_ref[...])
            out_acc[at, :] = jnp.zeros((tile_rows, width), F32)
            dn_acc[at, :] = jnp.zeros((tile_rows, width), F32)

        each(start)
        dgain_ref[...] = jnp.zeros_like(dgain_ref)

    def main(at):
        n = n_ref[at, :]
        gate = nn(n, gate_ref[...])
        up = nn(n, up_ref[...])
        dhidden = nt(g_ref[at, :], down_ref[...])
        square = gate * gate
        bend = jnp.tanh(gate * (GELU_A + GELU_B * square))
        half = 0.5 + 0.5 * bend
        gelu = gate * half
        slope = half + gate * (0.5 - 0.5 * bend * bend) * (GELU_A + 3.0 * GELU_B * square)
        hidden = (gelu * up).astype(BF16)
        dgate = (dhidden * up * slope).astype(BF16)
        dup = (dhidden * gelu).astype(BF16)
        hidden_ref[at, :] = hidden
        dgu_ref[at, :tile] = dgate
        dgu_ref[at, tile:] = dup
        out_acc[at, :] += nn(hidden, down_ref[...])
        dn_acc[at, :] += nt(dgate, gate_ref[...]) + nt(dup, up_ref[...])

    each(main)

    @pl.when(step == pl.num_programs(0) - 1)
    def _():
        def finish(at):
            h = h_acc[at, :]
            out_ref[at, :] = (h + out_acc[at, :]).astype(BF16)
            back, gain_part = norm_back(h, dn_acc[at, :], gain_ref[...])
            dh = g_ref[at, :].astype(F32) + back
            dh_ref[at, :] = dh
            low_ref[at, :] = dh.astype(BF16)
            dco_ref[at, :] = nt(low_ref[at, :], cross_ref[...]).astype(BF16)
            dgain_ref[...] += gain_part

        each(finish)


def feed_forward(h, co, cross_output, g, gain, feed_gate, feed_up, feed_down, hold=(), after=()):
    tokens, width = h.shape
    hidden = feed_gate.shape[1]
    tile = 256
    whole = pl.BlockSpec((tokens, width), lambda i: (0, 0), pipeline_mode=pl.Buffered(1))
    square = pl.BlockSpec((width, width), lambda i: (0, 0), pipeline_mode=pl.Buffered(1))
    row = pl.BlockSpec((1, width), lambda i: (0, 0))
    low, wide = jax.ShapeDtypeStruct(h.shape, BF16), jax.ShapeDtypeStruct(h.shape, F32)
    return call(
        functools.partial(feed_kernel, 256),
        (h, co, cross_output, g, gain, feed_gate, feed_up, feed_down),
        [
            whole, whole, square, whole, row,
            pl.BlockSpec((width, tile), lambda i: (0, i)),
            pl.BlockSpec((width, tile), lambda i: (0, i)),
            pl.BlockSpec((tile, width), lambda i: (i, 0)),
        ],
        [low, low, jax.ShapeDtypeStruct((tokens, hidden), BF16), jax.ShapeDtypeStruct((tokens, 2 * hidden), BF16),
         wide, low, low, jax.ShapeDtypeStruct((8, width), F32)],
        [whole, whole, pl.BlockSpec((tokens, tile), lambda i: (0, i)), pl.BlockSpec((tokens, 2 * tile), lambda i: (0, i)),
         whole, whole, whole, pl.BlockSpec((8, width), lambda i: (0, 0))],
        "feed_forward", 45e9, grid=(hidden // tile,), hold=hold, after=after,
        scratch=[pltpu.VMEM((tokens, width), F32) for _ in range(3)],
    )


class Group:
    def __init__(self):
        self.S, self.R = lax.axis_size("seq"), lax.axis_size("row")
        self.s, self.r = lax.axis_index("seq"), lax.axis_index("row")
        self.core = self.r % 2
        self.chunks = self.S
        self.members = self.S // 2
        self.member = (self.s // 4) * 2 + self.core
        self.first_half = self.s < self.S // 2
        self.even_row = self.s % 2 == 0
        self.places = [(s, r) for s in range(self.S) for r in range(self.R)]

    def index(self, s, r):
        return s * self.R + r

    def send(self, x, target):
        pairs = [(self.index(s, r), self.index(*target(s, r))) for s, r in self.places]
        return lax.ppermute(x, ("seq", "row"), pairs)

    def route(self, way):
        S = self.S

        def target(s, r):
            second = (s >= S // 2) if way == 0 else (s < S // 2)
            row = 2 * (r % 2) + (1 if second else 0)
            member = min(s, S - 1 - s)
            return (row + 4 * (member // 2), r - r % 2 + member % 2)

        return [(self.index(s, r), self.index(*target(s, r))) for s, r in self.places]

    def part(self, x, way):
        return jnp.where(self.first_half == (way == 0), x[0], x[1])

    def go(self, x, way):
        return lax.ppermute(x, ("seq", "row"), self.route(way))

    def back_part(self, low, high, way):
        return jnp.where(self.even_row == (way == 0), low, high)

    def back(self, x, way):
        return lax.ppermute(x, ("seq", "row"), [(t, f) for f, t in self.route(way)])

    def low_high(self, a, b):
        return jnp.where(self.even_row, a, b), jnp.where(self.even_row, b, a)

    def two_rows(self, a, b):
        return jnp.where(self.first_half, a, b), jnp.where(self.first_half, b, a)

    def peer(self, x, distance):
        return self.send(x, lambda s, r: (s ^ (4 * (distance >> 1)), r ^ (distance & 1)))

    def peers(self, x):
        return [x] + [self.peer(x, p) for p in range(1, self.members)]

    def core_swap(self, x):
        return self.send(x, lambda s, r: (s, r ^ 1))

    def all_sum(self, x):
        for axis, size in (("row", self.R), ("seq", self.S)):
            step = 1
            while step < size:
                x = x + lax.ppermute(x, axis, [(i, i ^ step) for i in range(size)])
                step *= 2
        return x

    def halves_of(self, left):
        half = left.shape[1] // 2
        theirs = lax.dynamic_slice_in_dim(left, (1 - self.core) * half, half, 1)
        return theirs, lax.dynamic_slice_in_dim(left, self.core * half, half, 1)

    def bit(self, name):
        return ((self.s if name[0] == "seq" else self.r) >> name[1]) & 1

    def names(self):
        top = self.S.bit_length() - 2
        row_bits = list(range(1, self.R.bit_length() - 1))
        return [("seq", k) for k in reversed(range(top))] + [("row", k) for k in reversed(row_bits)] + [("row", 0)]

    def begin(self, x):
        names = self.names()
        return x.reshape((2,) * len(names) + (x.shape[0] // 2 ** len(names), x.shape[1])), names

    def split(self, x, names, name):
        at = names.index(name)
        flat = x.reshape(math.prod(x.shape[:at]), 2, math.prod(x.shape[at + 1:-1]), x.shape[-1])
        give = lax.dynamic_index_in_dim(flat, 1 - self.bit(name), 1, keepdims=False)
        keep = lax.dynamic_index_in_dim(flat, self.bit(name), 1, keepdims=False)
        return give, keep

    def swap(self, give, name):
        size = self.S if name[0] == "seq" else self.R
        return lax.ppermute(give, name[0], [(i, i ^ (1 << name[1])) for i in range(size)])

    def merge(self, keep, got, x, names, name):
        at = names.index(name)
        total = (keep.astype(F32) + got.astype(F32)).astype(BF16)
        return total.reshape(x.shape[:at] + x.shape[at + 1:]), names[:at] + names[at + 1:]

    def last_sends(self, x):
        top = self.S.bit_length() - 2
        upper, half = self.s >> top, self.S // 2
        straight = lax.dynamic_index_in_dim(x, upper, 0, keepdims=False)
        crossed = lax.dynamic_index_in_dim(x, 1 - upper, 0, keepdims=False)
        one = self.send(straight, lambda s, r: ((r % 2) * half + s % half, (r - r % 2) + s // half))
        two = self.send(crossed, lambda s, r: ((r % 2) * half + s % half, (r - r % 2) + 1 - s // half))
        return one, two


class Scatter:
    def __init__(self, group, x, flip=False):
        self.group = group
        self.x, self.names = group.begin(x)
        row_names = [name for name in self.names if name[0] == "row" and name[1]]
        seq_names = [name for name in self.names if name[0] == "seq"]
        self.stages = (row_names if flip else row_names[::-1]) + seq_names[::-1]

    def start(self):
        if self.stages:
            self.give = self.group.split(self.x, self.names, self.stages[0])[0]
            self.got = self.group.swap(self.give, self.stages[0])
        else:
            self.got = self.group.last_sends(self.x)
            self.give = self.x

    def end(self):
        name = self.stages.pop(0)
        keep = self.group.split(self.x, self.names, name)[1]
        self.x, self.names = self.group.merge(keep, self.got, self.x, self.names, name)

    def step(self):
        if self.stages:
            self.end()
            self.start()

    def result(self):
        while self.stages:
            self.step()
        return self.got[0].astype(F32) + self.got[1].astype(F32)


def through(function, *args, run=(), hold=(), **more):
    hold = list(hold)
    outs, kept = function(*args, hold=hold + [one.x for one in run], after=[one.give for one in run], **more)
    for one, x in zip(run, kept[len(hold):]):
        one.x = x
    return outs, kept[:len(hold)]


def by_pairs(weight, axis):
    shape = weight.shape
    split = shape[:axis] + (shape[axis] // 256, 2, 2, 64) + shape[axis + 1:]
    return jnp.swapaxes(weight.reshape(split), axis + 1, axis + 2).reshape(shape)


def bias_rows(bias_table, sub):
    table = by_heads((bias_table - bias_table[BUCKETS - 1:]).T)
    levels = np.array([bucket_level(d) for d in range(2 * NEAR)])
    values = jnp.dot(table, jnp.asarray(np.eye(BUCKETS, dtype=np.float32)[levels].T), precision=HIGHEST)
    near = values[:, :sub] if sub <= 2 * NEAR else jnp.pad(values, ((0, 0), (0, sub - 2 * NEAR)))
    near = jnp.concatenate([near, jnp.full((HEADS, sub), MASK, F32)], axis=1)
    corner = jnp.concatenate([values[:, NEAR:], jnp.zeros((HEADS, 1), F32), values[:, 1:NEAR]], axis=1)
    return [jnp.broadcast_to(a[:, None], (HEADS, 8, a.shape[1])) for a in (near, corner)]


def by_heads(x):
    return jnp.swapaxes(x.reshape((4, 2, 2) + x.shape[1:]), 1, 2).reshape(x.shape)


def bias_table_sums(near, corner):
    def fold(wide, distances):
        matrix = np.zeros((8, wide, BUCKETS), np.float32)
        for row in range(8):
            for lane in range(wide):
                distance = distances((lane - row) % wide)
                if distance is not None:
                    matrix[row, lane, bucket_level(distance)] = 1.0
        return jnp.asarray(matrix.reshape(8 * wide, BUCKETS))

    sub = near.shape[2] // 2
    first = fold(2 * sub, lambda d: d if d < sub else None)
    second = fold(2 * NEAR, lambda d: NEAR + d if d < NEAR else (d - NEAR if d > NEAR else None))
    total = jnp.dot(near.reshape(HEADS, -1), first, precision=HIGHEST)
    total = total + jnp.dot(corner.reshape(HEADS, -1), second, precision=HIGHEST)
    rest = -jnp.sum(total[:, :BUCKETS - 1], axis=1, keepdims=True)
    return by_heads(jnp.concatenate([total[:, :BUCKETS - 1], rest], axis=1)).T


def on_device(tokens, segment_ids, memory, cotangent, gain_attend, gain_cross, gain_feed, bias_table,
              self_query, self_keyvalue, self_output, cross_query, cross_keyvalue, cross_output,
              feed_gate, feed_up, feed_down):
    group = Group()
    size, width = tokens.shape[1:]
    span = memory.shape[1]
    chunks = group.chunks
    sub = min(256, size)
    pad = 16

    numbers = jnp.pad(segment_ids.astype(BF16)[:, None, :], ((0, 0), (0, pad - 1), (0, width - size)))
    token_message = jnp.concatenate([tokens, numbers], axis=1)
    way_a = group.go(group.part(token_message, 0), 0)
    way_b = group.go(group.part(token_message, 1), 1)

    memory_rows = memory.reshape(-1, width)
    pairs = nn(memory_rows, cross_keyvalue).astype(BF16).reshape(2, span, width)
    own_query, own_output = by_pairs(self_query, 1), by_pairs(self_output, 0)
    other_query, other_output = by_pairs(cross_query, 1), by_pairs(cross_output, 0)
    near, near_back, corner, corner_back = bias_tiles(*bias_rows(bias_table, sub), sub)
    pairs_a, pairs_b = group.part(pairs, 0), group.part(pairs, 1)

    low, high = group.low_high(way_a, way_b)
    x = rows(low[:size], high[:size])
    memory_a = group.go(pairs_a, 0)

    (n1, kv), (pairs_b,) = by_rows(
        entry_kernel, "entry", 2e9, [(x, True), (gain_attend[None], False), (self_keyvalue, False)], [BF16, BF16], width,
        hold=[pairs_b], after=[pairs_a, own_query, own_output, other_query, other_output, near])
    memory_b = group.go(pairs_b, 1)
    kv_messages = group.peers(jnp.concatenate([kv, low[size:], high[size:]], axis=0))
    q = nn(n1, own_query).astype(BF16) * BF16(0.125)
    kv = jnp.concatenate([part[:2 * size] for part in kv_messages], axis=0)
    segments = jnp.concatenate([part[2 * size::pad, :size] for part in kv_messages], axis=0).astype(jnp.int32)
    meta = jnp.concatenate([group.member[None].astype(jnp.int32), segments[:, 0], segments[:, -1]])
    lane = jnp.arange(128)[None]
    same = (segments.reshape(-1, 1) == lane) & (lane < 4)
    key_marks = jnp.where(lane < 4, jnp.where(same, 0.0, MASK), jnp.where(lane < 7, -1.0, 0.0)).astype(BF16)
    query_marks = same[: 2 * size].astype(BF16)
    grad_a, grad_b = group.part(cotangent, 0), group.part(cotangent, 1)
    g_a = group.go(grad_a, 0)
    (o, lse), (grad_b, memory_a) = self_forward(
        meta, q, kv, query_marks, key_marks, near, corner, chunks, hold=[grad_b, memory_a], after=[grad_a, memory_b])
    g_b = group.go(grad_b, 1)
    memory_kv = rows(*group.low_high(memory_a, memory_b))
    (h1, n2, c), (memory_kv,) = by_rows(
        middle_kernel, "middle", 5e9,
        [(x, True), (o, True), (own_output, False), (gain_cross[None], False), (other_query, False)],
        [F32, BF16, BF16], width, hold=[memory_kv], after=[grad_b, g_a])
    memory_kv = jnp.concatenate(group.peers(memory_kv), axis=0)
    (co, cross_lse), _ = cross_forward(c, memory_kv, after=[grad_b])
    g = rows(*group.low_high(g_a, g_b))
    (out, n3, hidden, dgu, dh2, r2, dco, dgain_feed), _ = feed_forward(
        h1, co, other_output, g, gain_feed[None], feed_gate, feed_up, feed_down)
    out_parts = [group.back_part(out[:size], out[size:], way) for way in range(2)]
    out_a = group.back(out_parts[0], 0)

    hidden_theirs, hidden_mine = group.halves_of(hidden)
    n3_theirs, n3_mine = group.halves_of(n3)
    down_other = group.core_swap(tn(hidden_theirs, g).astype(BF16))
    dgu_other = group.core_swap(tn(n3_theirs, dgu).astype(BF16))
    down_part = (tn(hidden_mine, g) + down_other.astype(F32)).astype(BF16)
    dgu_part = (tn(n3_mine, dgu) + dgu_other.astype(F32)).astype(BF16)
    quarter = dgu_part.shape[1] // 4
    feed = [
        Scatter(group, down_part),
        Scatter(group, dgu_part[:, :quarter]),
        Scatter(group, dgu_part[:, quarter:], True),
    ]
    for one in feed:
        one.start()

    out_b = group.back(out_parts[1], 1)
    (dc, dm), (out_a,) = through(
        cross_backward, c, dco, co, cross_lse, memory_kv, run=feed, hold=[out_a])
    dm = lanes(dm[0], dm[1]).reshape(group.members, 2 * span, width)
    dm_parts = [dm[0]] + [group.peer(dm[p], p) for p in range(1, group.members)]
    (dh1, r1, do, dgain_cross), (out_a, dm_own) = through(
        by_rows, back_middle_kernel, "back_middle", 5e9,
        [(dc, True), (other_query, False), (h1, True), (gain_cross[None], False), (dh2, True), (own_output, False)],
        [F32, BF16, BF16], width, dgain=True, run=feed, hold=[out_a, dm_parts[0]])
    layer_output = jnp.stack(group.two_rows(out_a, out_b))
    dm = sum((part.astype(F32) for part in dm_parts[1:]), dm_own.astype(F32)).astype(BF16)
    dm_a = group.back(group.back_part(dm[:span], dm[span:], 0), 0)
    dm_b = group.back(group.back_part(dm[:span], dm[span:], 1), 1)
    for one in feed:
        one.step()
    cross_lefts = [group.halves_of(left) for left in (co, n2, o)]
    cross_others = [group.core_swap(tn(left[0], right).astype(BF16)) for left, right in zip(cross_lefts, (r2, dc, r1))]
    cross_parts = [
        (tn(left[1], right) + other.astype(F32)).astype(BF16)
        for left, right, other in zip(cross_lefts, (r2, dc, r1), cross_others)
    ]
    dm = rows(*group.two_rows(dm_a, dm_b))
    memory_lefts = group.halves_of(memory_rows)
    memory_other = group.core_swap(tn(memory_lefts[0], dm).astype(BF16))
    memory_grad = nt(dm, cross_keyvalue).astype(BF16).reshape(memory.shape)
    memory_part = (tn(memory_lefts[1], dm) + memory_other.astype(F32)).astype(BF16)
    cross = [
        Scatter(group, jnp.concatenate([by_pairs(cross_parts[0], 0), cross_parts[1]], axis=1)),
        Scatter(group, jnp.concatenate([by_pairs(cross_parts[2], 0), memory_part], axis=1), True),
    ]
    for one in cross:
        one.start()

    back = None
    parts = 4
    for part in range(parts):
        back, _ = through(
            self_backward, meta, q, do, o, lse, kv, query_marks, key_marks, near_back, corner_back, chunks,
            part, parts, back, run=feed + cross)
        if part == 0:
            for one in feed:
                one.step()
        if part == 1:
            for one in cross:
                one.step()
        if part == 2:
            for one in feed + cross:
                one.step()
    dq, dkv, near_sum, corner_sum = back
    dkv = lanes(dkv[0], dkv[1]).reshape(group.members, 2 * size, width)
    dkv = sum((group.peer(dkv[p], p).astype(F32) for p in range(1, group.members)), dkv[0].astype(F32)).astype(BF16)
    (tokens_grad, dgain_attend), _ = through(
        by_rows, exit_kernel, "exit", 5e9,
        [(dq, True), (own_query, False), (dkv, True), (self_keyvalue, False), (x, True), (gain_attend[None], False), (dh1, True)],
        [BF16], width, dgain=True, run=cross)
    token_a = group.back(group.back_part(tokens_grad[:size], tokens_grad[size:], 0), 0)
    left = group.halves_of(n1)
    right = lanes(dq, dkv)
    other = group.core_swap(tn(left[0], right).astype(BF16))
    own_part = (tn(left[1], right) + other.astype(F32)).astype(BF16)
    own = [Scatter(group, own_part[:, :width]), Scatter(group, own_part[:, width:], True)]
    for one in own:
        one.start()
    token_b = group.back(group.back_part(tokens_grad[:size], tokens_grad[size:], 1), 1)
    tokens_grad = jnp.stack(group.two_rows(token_a, token_b))
    grad_own = [one.result() for one in own]
    grad_cross = [one.result() for one in cross]
    grad_feed = [one.result() for one in feed]

    dbias = bias_table_sums(near_sum, corner_sum)
    small = jnp.stack([jnp.sum(dgain_attend, axis=0), jnp.sum(dgain_cross, axis=0), jnp.sum(dgain_feed, axis=0),
                       jnp.pad(dbias.reshape(-1), (0, width - dbias.size))])
    small = group.all_sum(small)

    dgu = jnp.concatenate(grad_feed[1:], axis=1).reshape(-1, feed_gate.shape[1] // 256, 2, 256)
    return (
        layer_output,
        tokens_grad,
        memory_grad,
        by_pairs(grad_own[0], 1),
        grad_own[1],
        grad_cross[1][:, :width],
        by_pairs(grad_cross[0][:, width:], 1),
        grad_cross[1][:, width:],
        grad_cross[0][:, :width],
        dgu[:, :, 0].reshape(-1, feed_gate.shape[1]),
        dgu[:, :, 1].reshape(-1, feed_gate.shape[1]),
        grad_feed[0],
        small[0],
        small[1],
        small[2],
        small[3, :dbias.size].reshape(dbias.shape),
    )


def solution(mesh):
    data, whole, grads = P("row", "seq", None), P(), P(("seq", "row"), None)
    in_specs = (data, P("row", "seq"), data, data) + (whole,) * 13
    out_specs = (data,) * 3 + (grads,) * 9 + (whole,) * 4
    return jax.shard_map(on_device, mesh=mesh, in_specs=in_specs, out_specs=out_specs, check_vma=False)
```

time: 2190 us -> 773 us (0.35)
  matrix products: 802 us -> 68 us
  waiting for transfers between devices: 767 us -> 91.1 us
  Pallas kernels: 0 us -> 307 us
  local copies, waits for them, and re-layouts: 304 us -> 89.3 us
  blocking collectives: 114 us -> 0 us
  starting transfers between devices: 22 us -> 126 us
  other arithmetic: 155 us -> 76.8 us
    dot_general x65 -> x20, matrix products: 802 us -> 68 us  [the longest x14 58.4 us: tn(): lax.dot_general(a, b, (((0,), (0,)), ((), ())), preferred_element_type=F32)]
    reduce_scatter x9 -> x0, waiting for transfers between devices: 601 us -> none  [the longest x1 154 us: on_device(): lax.psum_scatter(grad_feed_up, ('seq', 'row'), scatter_dimension=0, tiled...]
    pallas_call x0 -> x13, Pallas kernels: none -> 307 us  [the longest x12 300 us: call(): pl.pallas_call(body, grid_spec=pltpu.PrefetchScalarGridSpec(num_scalar_pr...]
    reshape x20 -> x13, local copies, waits for them, and re-layouts: 152 us -> 19.1 us  [the longest x4 10.7 us: by_pairs(): jnp.swapaxes(weight.reshape(split), axis + 1, axis + 2).reshape(shape)]
    ppermute x7 -> x63, starting transfers between devices: 21.1 us -> 126 us  [the longest x25 42.7 us: send(): return lax.ppermute(x, ('seq', 'row'), pairs)]
    reduce_sum x7 -> x4, other arithmetic: 88.1 us -> 2.26 us  [the longest x1 0.77 us: on_device(): jnp.sum(dgain_cross, axis=0)]
    add x5 -> x0, local copies, waits for them, and re-layouts: 79.4 us -> none  [the longest x4 77.2 us: self_scores(): raw_scores + heads_bias[None]]
    all_gather x1 -> x0, blocking collectives: 76.1 us -> none  [on_device(): all_segments = lax.all_gather(segment_ids, 'seq', axis=1, tiled=True)]
  transfers between devices with their start and end apart: 18 -> 63, of which waited for: 11 -> 17; matrix products, arithmetic and copies ran while one was open for 43% -> 26% of each run, Pallas kernels for 0% -> 29%
where the time goes in v1:
time: 773 us; the launch traced here: 761 us
  Pallas kernels  307 us (40%)
  starting transfers between devices  126 us (16%)
  waiting for transfers between devices  91.1 us (12%)
  local copies, waits for them, and re-layouts  89.3 us (12%)
  other arithmetic  76.8 us (10%)
  matrix products  68 us (9%)
    pallas_call x12, Pallas kernels, call(): pl.pallas_call(body, grid_spec=pltpu.PrefetchScalarGridSpec(num_scalar_pr...  300 us
    dot_general x14, matrix products, tn(): lax.dot_general(a, b, (((0,), (0,)), ((), ())), preferred_element_type=F32)  58.4 us
    ppermute x25, starting transfers between devices, send(): return lax.ppermute(x, ('seq', 'row'), pairs)  42.7 us
    ppermute x5, waiting for transfers between devices, all_sum(): x = x + lax.ppermute(x, axis, [(i, i ^ step) for i in range(size)])  35.2 us
    ppermute x21, starting transfers between devices, swap(): lax.ppermute(give, name[0], [(i, i ^ 1 << name[1]) for i in range(size)])  27.9 us
    ppermute x21, waiting for transfers between devices, swap(): lax.ppermute(give, name[0], [(i, i ^ 1 << name[1]) for i in range(size)])  25.9 us
    unnamed x174, local copies, waits for them, and re-layouts  25.5 us
    ppermute x25, waiting for transfers between devices, send(): return lax.ppermute(x, ('seq', 'row'), pairs)  25.4 us
  transfers between devices with their start and end apart: 63, of which 17 were waited for; matrix products, arithmetic and copies ran while one was open for 26% of the time, Pallas kernels for 29%

profile of v1, /device:TPU:0, one launch (start us, length us, event | category | flops | bytes accessed | tf_op | source)
XLA Modules:
  0.0 761.3 jit_solution(3916027684197041448)
XLA Ops:
  44.9 7.1 bias_tiles.1
  66.5 8.0 %collective-permute-start.2 = (bf16[1056,1024]{1,0:T(8,128)(2,1)}, bf16[1056,1024]{1,0:T(8,128)(2,1)}, u32[]{:S(2)}, u32[]{:S(2)}) collective-permute-start(bf16[1056,1024]{1,0:T(8,128)(2,1)} %pad_maximum_fusion.6), channel_id=1, source_target_pairs={{0,1},{1,0},{2,3},{3,2},{4,5},{5,4},{6,7},{7,6},{8,9},{9,8},{10,11... | collective-permute-start | bytes 6488072 | tf_op jit(solution)/shard_map/ppermute | solution.py:656
  76.6 9.5 %collective-permute-start.5 = (bf16[512,1024]{1,0:T(8,128)(2,1)}, bf16[512,1024]{1,0:T(8,128)(2,1)}, u32[]{:S(2)}, u32[]{:S(2)}) collective-permute-start(bf16[512,1024]{1,0:T(8,128)(2,1)} %get-tuple-element.242.refs_10_), channel_id=1, source_target_pairs={{0,0},{1,16},{2,2},{3,18},{4,4},{5,20},{6,6},{7,22},{8,1},{9,17},{... | collective-permute-start | bytes 3145736 | tf_op jit(solution)/shard_map/ppermute | solution.py:673
  104.4 55.0 %self_forward.1 = (bf16[1024,1024]{1,0:T(8,128)(2,1)}, f32[1024,1024]{1,0:T(8,128)}, bf16[512,1024]{1,0:T(8,128)(2,1)}, bf16[128,1024]{1,0:T(8,128)(2,1)}) custom-call(s32[9]{0:T(128)} %pad_add_fusion.refs_0_, bf16[1024,1024]{1,0:T(8,128)(2,1)} %convert_multiply_fusion.refs_1_, ...), custom_call_target="tpu_custom_call", output_to_operand_aliasing={{2}: (8, {}), {3}: (9, {})} | custom-call | flops 40000000000 | bytes 10000000 | tf_op jit(solution)/shard_map/self_forward/pallas_call | solution.py:46
  161.3 9.3 %middle.1 = (f32[1024,1024]{1,0:T(8,128)}, bf16[1024,1024]{1,0:T(8,128)(2,1)}, bf16[1024,1024]{1,0:T(8,128)(2,1)}, bf16[256,1024]{1,0:T(8,128)(2,1)}) custom-call(bf16[1024,1024]{1,0:T(8,128)(2,1)} %pad_maximum_fusion.8.refs_0_.refs_4_, bf16[1024,1024]{1,0:T(8,128)(2,1)} %get-tuple-element.98.refs_1_.refs_3_, ...), custom_call_target="tpu_custom_call", output_to_operand_aliasing={{3}: (5, {})} | custom-call | flops 5000000000 | bytes 10000000 | tf_op jit(solution)/shard_map/middle/pallas_call | solution.py:46
  170.6 9.5 %collective-permute-start.6 = (bf16[256,1024]{1,0:T(8,128)(2,1)}, bf16[256,1024]{1,0:T(8,128)(2,1)}, u32[]{:S(2)}, u32[]{:S(2)}) collective-permute-start(bf16[256,1024]{1,0:T(8,128)(2,1)} %get-tuple-element.103), channel_id=1, source_target_pairs={{0,1},{1,0},{2,3},{3,2},{4,5},{5,4},{6,7},{7,6},{8,9},{9,8},{10,11... | collective-permute-start | bytes 1572872 | tf_op jit(solution)/shard_map/ppermute | solution.py:656
  185.7 19.7 %cross_forward.1 = (bf16[1024,1024]{1,0:T(8,128)(2,1)}, f32[1024,1024]{1,0:T(8,128)}) custom-call(bf16[1024,1024]{1,0:T(8,128)(2,1)} %get-tuple-element.101.refs_0_, bf16[512,1024]{1,0:T(8,128)(2,1)} %copy-done.62, bf16[512,1024]{1,0:T(8,128)(2,1)} %copy-done.62, bf16[512,1024]{1,0:T(8,128)(2,1)} %get-tuple-element.100.refs_6_.refs_3_), custom_call_target="tpu_custom_call" | custom-call | flops 15000000512 | bytes 10000000 | tf_op jit(solution)/shard_map/cross_forward/pallas_call | solution.py:46
  209.8 70.2 %feed_forward.1 = (bf16[1024,1024]{1,0:T(8,128)(2,1)}, bf16[1024,1024]{1,0:T(8,128)(2,1)}, bf16[1024,2816]{1,0:T(8,128)(2,1)}, bf16[1024,5632]{1,0:T(8,128)(2,1)...) custom-call(f32[1024,1024]{1,0:T(8,128)} %get-tuple-element.102.refs_0_.re, ...), custom_call_target="tpu_custom_call" | custom-call | flops 44999999488 | bytes 10000000 | tf_op jit(solution)/shard_map/feed_forward/pallas_call | solution.py:46
  279.9 10.9 %convolution_convert_fusion = bf16[512,5632]{1,0:T(8,128)(2,1)} fusion(bf16[1024,5632]{1,0:T(8,128)(2,1)} %get-tuple-element.110, bf16[1024,1024]{1,0:T(8,128)(2,1)} %get-tuple-element.109, s32[]{:T(128)S(6)} %select_n.320), kind=kOutput, calls=%fused_computation.1 | convolution fusion | flops 5908463616 | bytes 18350084 | tf_op jit(solution)/shard_map/dot_general | solution.py:73
  292.5 7.0 convolution_convert_fusion.1
  305.3 9.5 %collective-permute-start.8 = (bf16[512,1024]{1,0:T(8,128)(2,1)}, bf16[512,1024]{1,0:T(8,128)(2,1)}, u32[]{:S(2)}, u32[]{:S(2)}) collective-permute-start(bf16[512,1024]{1,0:T(8,128)(2,1)} %get-tuple-element.238), channel_id=1, source_target_pairs={{0,0},{16,1},{2,2},{18,3},{4,4},{20,5},{6,6},{22,7},{1,8},{17,9},{... | collective-permute-start | bytes 3145736 | tf_op jit(solution)/shard_map/ppermute | solution.py:679
  331.2 8.7 %add_convert_fusion = bf16[512,5632]{1,0:T(8,128)(2,1)S(1)} fusion(bf16[512,5632]{1,0:T(8,128)(2,1)} %collective-permute-done.10, bf16[1024,5632]{1,0:T(8,128)(2,1)S(1)} %bitcast.302, bf16[1024,1024]{1,0:T(8,128)(2,1)} %get-tuple-element.109, s32[]{:T(128)S(6)} %select_n.319), kind=kOutput, calls=%fused_computation | convolution fusion | flops 5914230784 | bytes 24117252 | tf_op jit(solution)/shard_map/dot_general | solution.py:73
  346.2 31.1 %cross_backward.1 = (bf16[1024,1024]{1,0:T(8,128)(2,1)}, bf16[2,512,512]{2,1,0:T(8,128)(2,1)}, bf16[512,1024]{1,0:T(8,128)(2,1)}, bf16[2,2,2,2,88,1024]{5,4,3,2,...) custom-call(bf16[1024,1024]{1,0:T(8,128)(2,1)} %get-tuple-element.10, ...), custom_call_target="tpu_custom_call", output_to_operand_aliasing={{2}: (6, {}), {3}: (7, {}), {4}: (8, {}), {5}: (9, {})} | custom-call | flops 30000001024 | bytes 10000000 | tf_op jit(solution)/shard_map/cross_backward/pallas_call | solution.py:46
  379.7 11.8 %back_middle.1 = (f32[1024,1024]{1,0:T(8,128)}, bf16[1024,1024]{1,0:T(8,128)(2,1)}, bf16[1024,1024]{1,0:T(8,128)(2,1)}, f32[8,1024]{1,0:T(8,128)}, bf16[512,1024...) custom-call(bf16[1024,1024]{1,0:T(8,128)(2,1)} %get-tuple-element.11, ...), custom_call_target="tpu_custom_call", output_to_operand_aliasing={{4}: (6, {}), {5}: (7, {}), {6}: (8, {}), {7}: (9, {}), {8}... | custom-call | flops 5000000000 | bytes 10000000 | tf_op jit(solution)/shard_map/back_middle/pallas_call | solution.py:46
  401.2 7.5 collective-permute-start.16
  461.1 21.7 %self_backward.4 = (bf16[1024,1024]{1,0:T(8,128)(2,1)}, bf16[2,2048,512]{2,1,0:T(8,128)(2,1)}, f32[16,8,512]{2,1,0:T(8,128)}, f32[16,8,256]{2,1,0:T(8,128)}, bf1...) custom-call(s32[9]{0:T(128)} %pad_add_fusion.refs_0_, ...), custom_call_target="tpu_custom_call", output_to_operand_aliasing={{4}: (11, {}), {5}: (12, {}), {6}: (13, {}), {7}: (14, {}),... | custom-call | flops 15000000512 | bytes 10000000 | tf_op jit(solution)/shard_map/self_backward/pallas_call | solution.py:46
  491.5 7.4 collective-permute-done.24
  501.6 21.3 %self_backward.5 = (bf16[1024,1024]{1,0:T(8,128)(2,1)}, bf16[2,2048,512]{2,1,0:T(8,128)(2,1)}, f32[16,8,512]{2,1,0:T(8,128)}, f32[16,8,256]{2,1,0:T(8,128)}, bf1...) custom-call(s32[9]{0:T(128)} %pad_add_fusion.refs_0_, ...), custom_call_target="tpu_custom_call", output_to_operand_aliasing={{4}: (15, {}), {5}: (16, {}), {6}: (17, {}), {7}: (18, {}),... | custom-call | flops 15000000512 | bytes 10000000 | tf_op jit(solution)/shard_map/self_backward/pallas_call | solution.py:46
  531.0 21.5 %self_backward.6 = (bf16[1024,1024]{1,0:T(8,128)(2,1)}, bf16[2,2048,512]{2,1,0:T(8,128)(2,1)}, f32[16,8,512]{2,1,0:T(8,128)}, f32[16,8,256]{2,1,0:T(8,128)}, bf1...) custom-call(s32[9]{0:T(128)} %pad_add_fusion.refs_0_, ...), custom_call_target="tpu_custom_call", output_to_operand_aliasing={{4}: (15, {}), {5}: (16, {}), {6}: (17, {}), {7}: (18, {}),... | custom-call | flops 15000000512 | bytes 10000000 | tf_op jit(solution)/shard_map/self_backward/pallas_call | solution.py:46
  563.6 7.6 %collective-permute-done.57 = bf16[88,1024]{1,0:T(8,128)(2,1)S(1)} collective-permute-done((bf16[88,1024]{1,0:T(8,128)(2,1)S(1)}, bf16[88,1024]{1,0:T(8,128)(2,1)S(1)}, u32[]{:S(2)}, u32[]{:S(2)}) %collective-permute-start.57) | collective-permute-done | bytes 180256 | tf_op jit(solution)/shard_map/ppermute | solution.py:656
  577.0 21.3 %self_backward.7 = (bf16[1024,1024]{1,0:T(8,128)(2,1)}, bf16[2,2048,512]{2,1,0:T(8,128)(2,1)}, f32[16,8,512]{2,1,0:T(8,128)}, f32[16,8,256]{2,1,0:T(8,128)}, bf1...) custom-call(s32[9]{0:T(128)} %pad_add_fusion.refs_0_, ...), custom_call_target="tpu_custom_call", output_to_operand_aliasing={{4}: (15, {}), {5}: (16, {}), {6}: (17, {}), {7}: (18, {}),... | custom-call | flops 15000000512 | bytes 10000000 | tf_op jit(solution)/shard_map/self_backward/pallas_call | solution.py:46
  627.1 10.7 %exit.1 = (bf16[1024,1024]{1,0:T(8,128)(2,1)}, f32[8,1024]{1,0:T(8,128)}, bf16[2,2,32,2048]{3,2,1,0:T(8,128)(2,1)}, bf16[2,2,32,2048]{3,2,1,0:T(8,128)(2,1)}) custom-call(bf16[1024,1024]{1,0:T(8,128)(2,1)} %get-tuple-element.157.refs_0_, bf16[1024,1024]{1,0:T(8,128)(2,1)} %copy.206.refs_5_.refs_1_, ...), custom_call_target="tpu_custom_call", output_to_operand_aliasing={{2}: (7, {}), {3}: (8, {})} | custom-call | flops 5000000000 | bytes 10000000 | tf_op jit(solution)/shard_map/exit/pallas_call | solution.py:46
  662.8 16.6 %collective-permute-done.61 = f32[4,1024]{1,0:T(4,128)S(1)} collective-permute-done((f32[4,1024]{1,0:T(4,128)S(1)}, f32[4,1024]{1,0:T(4,128)S(1)}, u32[]{:S(2)}, u32[]{:S(2)}) %collective-permute-start.61) | collective-permute-done | bytes 16416 | tf_op jit(solution)/shard_map/ppermute | solution.py:700
  680.5 15.6 %collective-permute-done.62 = f32[4,1024]{1,0:T(4,128)S(1)} collective-permute-done((f32[4,1024]{1,0:T(4,128)S(1)}, f32[4,1024]{1,0:T(4,128)S(1)}, u32[]{:S(2)}, u32[]{:S(2)}) %collective-permute-start.62) | collective-permute-done | bytes 16416 | tf_op jit(solution)/shard_map/ppermute | solution.py:700
  (479 shorter events, 340.1 us)
Async XLA Ops:
  7.7 45.9 %collective-permute-start = (bf16[528,1024]{1,0:T(8,128)(2,1)}, bf16[528,1024]{1,0:T(8,128)(2,1)S(1)}, u32[]{:S(2)}, u32[]{:S(2)}) collective-permute-start(bf16[528,1024]{1,0:T(8,128)(2,1)} %get-tuple-element.228), channel_id=1, source_target_pairs={{0,0},{1,16},{2,2},{3,18},{4,4},{5,20},{6,6},{7,22},{8,1},{9,17},{... | collective-permute-start | bytes 3244040 | tf_op jit(solution)/shard_map/ppermute | solution.py:673
  9.6 44.1 %collective-permute-start.1 = (bf16[528,1024]{1,0:T(8,128)(2,1)}, bf16[528,1024]{1,0:T(8,128)(2,1)}, u32[]{:S(2)}, u32[]{:S(2)}) collective-permute-start(bf16[528,1024]{1,0:T(8,128)(2,1)} %get-tuple-element.229), channel_id=1, source_target_pairs={{0,8},{1,24},{2,10},{3,26},{4,12},{5,28},{6,14},{7,30},{8,9},{9,25... | collective-permute-start | bytes 3244040 | tf_op jit(solution)/shard_map/ppermute | solution.py:673
  76.6 84.6 %collective-permute-start.5 = (bf16[512,1024]{1,0:T(8,128)(2,1)}, bf16[512,1024]{1,0:T(8,128)(2,1)}, u32[]{:S(2)}, u32[]{:S(2)}) collective-permute-start(bf16[512,1024]{1,0:T(8,128)(2,1)} %get-tuple-element.242.refs_10_), channel_id=1, source_target_pairs={{0,0},{1,16},{2,2},{3,18},{4,4},{5,20},{6,6},{7,22},{8,1},{9,17},{... | collective-permute-start | bytes 3145736 | tf_op jit(solution)/shard_map/ppermute | solution.py:673
  290.9 40.2 %collective-permute-start.10 = (bf16[512,5632]{1,0:T(8,128)(2,1)}, bf16[512,5632]{1,0:T(8,128)(2,1)}, u32[]{:S(2)}, u32[]{:S(2)}) collective-permute-start(bf16[512,5632]{1,0:T(8,128)(2,1)} %convolution_convert_fusion), channel_id=1, source_target_pairs={{0,1},{1,0},{2,3},{3,2},{4,5},{5,4},{6,7},{7,6},{8,9},{9,8},{10,11... | collective-permute-start | bytes 17301512 | tf_op jit(solution)/shard_map/ppermute | solution.py:656
  305.3 40.9 %collective-permute-start.8 = (bf16[512,1024]{1,0:T(8,128)(2,1)}, bf16[512,1024]{1,0:T(8,128)(2,1)}, u32[]{:S(2)}, u32[]{:S(2)}) collective-permute-start(bf16[512,1024]{1,0:T(8,128)(2,1)} %get-tuple-element.238), channel_id=1, source_target_pairs={{0,0},{16,1},{2,2},{18,3},{4,4},{20,5},{6,6},{22,7},{1,8},{17,9},{... | collective-permute-start | bytes 3145736 | tf_op jit(solution)/shard_map/ppermute | solution.py:679
  314.8 94.0 %collective-permute-start.11 = (bf16[512,1024]{1,0:T(8,128)(2,1)}, bf16[512,1024]{1,0:T(8,128)(2,1)}, u32[]{:S(2)}, u32[]{:S(2)}) collective-permute-start(bf16[512,1024]{1,0:T(8,128)(2,1)} %get-tuple-element.239), channel_id=1, source_target_pairs={{8,0},{24,1},{10,2},{26,3},{12,4},{28,5},{14,6},{30,7},{9,8},{25,9... | collective-permute-start | bytes 3145736 | tf_op jit(solution)/shard_map/ppermute | solution.py:679
  329.6 84.7 %collective-permute-start.12 = (bf16[4,176,1024]{2,1,0:T(8,128)(2,1)S(1)}, bf16[4,176,1024]{2,1,0:T(8,128)(2,1)}, u32[]{:S(2)}, u32[]{:S(2)}) collective-permute-start(bf16[4,176,1024]{2,1,0:T(8,128)(2,1)S(1)} %dynamic-slice_bitcast_fusion.1.refs_10_.refs_11_), channel_id=1, source_target_pairs={{0,2},{1,3},{2,0},{3,1},{4,6},{5,7},{6,4},{7,5},{8,10},{9,11},{10,... | collective-permute-start | bytes 4325384 | tf_op jit(solution)/shard_map/ppermute | solution.py:730
  342.6 81.2 %collective-permute-start.13 = (bf16[4,64,1408]{2,1,0:T(8,128)(2,1)}, bf16[4,64,1408]{2,1,0:T(8,128)(2,1)}, u32[]{:S(2)}, u32[]{:S(2)}) collective-permute-start(bf16[4,64,1408]{2,1,0:T(8,128)(2,1)} %dynamic-slice_bitcast_fusion.4.refs_11_.refs_12_), channel_id=1, source_target_pairs={{0,2},{1,3},{2,0},{3,1},{4,6},{5,7},{6,4},{7,5},{8,10},{9,11},{10,... | collective-permute-start | bytes 2162696 | tf_op jit(solution)/shard_map/ppermute | solution.py:730
  345.4 111.8 %collective-permute-start.14 = (bf16[2,128,4224]{2,1,0:T(8,128)(2,1)}, bf16[2,128,4224]{2,1,0:T(8,128)(2,1)}, u32[]{:S(2)}, u32[]{:S(2)}) collective-permute-start(bf16[2,128,4224]{2,1,0:T(8,128)(2,1)} %dynamic-slice_bitcast_fusion.refs_12_.refs_13_), channel_id=1, source_target_pairs={{0,4},{1,5},{2,6},{3,7},{4,0},{5,1},{6,2},{7,3},{8,12},{9,13},{10,... | collective-permute-start | bytes 6488072 | tf_op jit(solution)/shard_map/ppermute | solution.py:730
  401.2 43.3 %collective-permute-start.16 = (bf16[512,1024]{1,0:T(8,128)(2,1)}, bf16[512,1024]{1,0:T(8,128)(2,1)}, u32[]{:S(2)}, u32[]{:S(2)}) collective-permute-start(bf16[512,1024]{1,0:T(8,128)(2,1)} %convolution_convert_fusion.5), channel_id=1, source_target_pairs={{0,1},{1,0},{2,3},{3,2},{4,5},{5,4},{6,7},{7,6},{8,9},{9,8},{10,11... | collective-permute-start | bytes 3145736 | tf_op jit(solution)/shard_map/ppermute | solution.py:656
  432.0 53.3 %collective-permute-start.22 = (bf16[2,176,1024]{2,1,0:T(8,128)(2,1)}, bf16[2,176,1024]{2,1,0:T(8,128)(2,1)S(1)}, u32[]{:S(2)}, u32[]{:S(2)}) collective-permute-start(bf16[2,176,1024]{2,1,0:T(8,128)(2,1)} %dynamic-slice_bitcast_fusion.3.refs_16_), channel_id=1, source_target_pairs={{0,4},{1,5},{2,6},{3,7},{4,0},{5,1},{6,2},{7,3},{8,12},{9,13},{10,... | collective-permute-start | bytes 2162696 | tf_op jit(solution)/shard_map/ppermute | solution.py:730
  436.7 50.9 %collective-permute-start.23 = (bf16[2,64,1408]{2,1,0:T(8,128)(2,1)}, bf16[2,64,1408]{2,1,0:T(8,128)(2,1)}, u32[]{:S(2)}, u32[]{:S(2)}) collective-permute-start(bf16[2,64,1408]{2,1,0:T(8,128)(2,1)} %dynamic-slice_bitcast_fusion.9.refs_17_), channel_id=1, source_target_pairs={{0,4},{1,5},{2,6},{3,7},{4,0},{5,1},{6,2},{7,3},{8,12},{9,13},{10,... | collective-permute-start | bytes 1081352 | tf_op jit(solution)/shard_map/ppermute | solution.py:730
  450.2 75.2 %collective-permute-start.25 = (bf16[4,64,2048]{2,1,0:T(8,128)(2,1)}, bf16[4,64,2048]{2,1,0:T(8,128)(2,1)}, u32[]{:S(2)}, u32[]{:S(2)}) collective-permute-start(bf16[4,64,2048]{2,1,0:T(8,128)(2,1)} %fusion.17.refs_19_.refs_23_), channel_id=1, source_target_pairs={{0,2},{1,3},{2,0},{3,1},{4,6},{5,7},{6,4},{7,5},{8,10},{9,11},{10,... | collective-permute-start | bytes 3145736 | tf_op jit(solution)/shard_map/ppermute | solution.py:730
  454.8 72.3 %collective-permute-start.26 = (bf16[2,128,2048]{2,1,0:T(8,128)(2,1)}, bf16[2,128,2048]{2,1,0:T(8,128)(2,1)}, u32[]{:S(2)}, u32[]{:S(2)}) collective-permute-start(bf16[2,128,2048]{2,1,0:T(8,128)(2,1)} %fusion.15.refs_20_.refs_24_), channel_id=1, source_target_pairs={{0,4},{1,5},{2,6},{3,7},{4,0},{5,1},{6,2},{7,3},{8,12},{9,13},{10,... | collective-permute-start | bytes 3145736 | tf_op jit(solution)/shard_map/ppermute | solution.py:730
  487.6 64.9 %collective-permute-start.27 = (bf16[1,176,1024]{2,1,0:T(8,128)(2,1)S(1)}, bf16[1,176,1024]{2,1,0:T(8,128)(2,1)S(1)}, u32[]{:S(2)}, u32[]{:S(2)}) collective-permute-start(bf16[1,176,1024]{2,1,0:T(8,128)(2,1)S(1)} %constant_dynamic-slice_fusion.6.refs_20_), channel_id=1, source_target_pairs={{0,8},{8,0},{16,24},{24,16},{1,9},{9,1},{17,25},{25,17},{2,10},{10... | collective-permute-start | bytes 1081352 | tf_op jit(solution)/shard_map/ppermute | solution.py:730
  489.8 64.6 %collective-permute-start.28 = (bf16[1,64,1408]{2,1,0:T(8,128)(2,1)}, bf16[1,64,1408]{2,1,0:T(8,128)(2,1)}, u32[]{:S(2)}, u32[]{:S(2)}) collective-permute-start(bf16[1,64,1408]{2,1,0:T(8,128)(2,1)} %constant_dynamic-slice_fusion.5.refs_21_), channel_id=1, source_target_pairs={{0,8},{8,0},{16,24},{24,16},{1,9},{9,1},{17,25},{25,17},{2,10},{10... | collective-permute-start | bytes 540680 | tf_op jit(solution)/shard_map/ppermute | solution.py:730
  500.5 75.3 %collective-permute-start.29 = (bf16[1,64,4224]{2,1,0:T(8,128)(2,1)S(1)}, bf16[1,64,4224]{2,1,0:T(8,128)(2,1)S(1)}, u32[]{:S(2)}, u32[]{:S(2)}) collective-permute-start(bf16[1,64,4224]{2,1,0:T(8,128)(2,1)S(1)} %constant_dynamic-slice_fusion.4.refs_22_), channel_id=1, source_target_pairs={{0,8},{8,0},{16,24},{24,16},{1,9},{9,1},{17,25},{25,17},{2,10},{10... | collective-permute-start | bytes 1622024 | tf_op jit(solution)/shard_map/ppermute | solution.py:730
  529.3 43.6 %collective-permute-start.30 = (bf16[2,64,2048]{2,1,0:T(8,128)(2,1)S(1)}, bf16[2,64,2048]{2,1,0:T(8,128)(2,1)S(1)}, u32[]{:S(2)}, u32[]{:S(2)}) collective-permute-start(bf16[2,64,2048]{2,1,0:T(8,128)(2,1)S(1)} %dynamic-slice_bitcast_fusion.8.refs_23_), channel_id=1, source_target_pairs={{0,4},{1,5},{2,6},{3,7},{4,0},{5,1},{6,2},{7,3},{8,12},{9,13},{10,... | collective-permute-start | bytes 1572872 | tf_op jit(solution)/shard_map/ppermute | solution.py:730
  530.9 41.1 %collective-permute-start.31 = (bf16[2,64,2048]{2,1,0:T(8,128)(2,1)S(1)}, bf16[2,64,2048]{2,1,0:T(8,128)(2,1)S(1)}, u32[]{:S(2)}, u32[]{:S(2)}) collective-permute-start(bf16[2,64,2048]{2,1,0:T(8,128)(2,1)S(1)} %dynamic-slice_bitcast_fusion.7.refs_24_), channel_id=1, source_target_pairs={{0,2},{1,3},{2,0},{3,1},{4,6},{5,7},{6,4},{7,5},{8,10},{9,11},{10,... | collective-permute-start | bytes 1572872 | tf_op jit(solution)/shard_map/ppermute | solution.py:730
  572.9 78.1 %collective-permute-start.46 = (bf16[1,64,2048]{2,1,0:T(8,128)(2,1)}, bf16[1,64,2048]{2,1,0:T(8,128)(2,1)}, u32[]{:S(2)}, u32[]{:S(2)}) collective-permute-start(bf16[1,64,2048]{2,1,0:T(8,128)(2,1)} %constant_dynamic-slice_fusion.2.refs_24_.refs_10_), channel_id=1, source_target_pairs={{0,8},{8,0},{16,24},{24,16},{1,9},{9,1},{17,25},{25,17},{2,10},{10... | collective-permute-start | bytes 786440 | tf_op jit(solution)/shard_map/ppermute | solution.py:730
  573.8 87.8 %collective-permute-start.49 = (bf16[1,64,2048]{2,1,0:T(8,128)(2,1)}, bf16[1,64,2048]{2,1,0:T(8,128)(2,1)}, u32[]{:S(2)}, u32[]{:S(2)}) collective-permute-start(bf16[1,64,2048]{2,1,0:T(8,128)(2,1)} %constant_dynamic-slice_fusion.3.refs_23_.refs_9_), channel_id=1, source_target_pairs={{0,8},{8,0},{16,24},{24,16},{1,9},{9,1},{17,25},{25,17},{2,10},{10... | collective-permute-start | bytes 786440 | tf_op jit(solution)/shard_map/ppermute | solution.py:730
  644.4 75.5 %collective-permute-start.33 = (bf16[512,1024]{1,0:T(8,128)(2,1)}, bf16[512,1024]{1,0:T(8,128)(2,1)S(1)}, u32[]{:S(2)}, u32[]{:S(2)}) collective-permute-start(bf16[512,1024]{1,0:T(8,128)(2,1)} %get-tuple-element.234), channel_id=1, source_target_pairs={{0,0},{16,1},{2,2},{18,3},{4,4},{20,5},{6,6},{22,7},{1,8},{17,9},{... | collective-permute-start | bytes 3145736 | tf_op jit(solution)/shard_map/ppermute | solution.py:679
  646.3 73.6 %collective-permute-start.34 = (bf16[512,1024]{1,0:T(8,128)(2,1)}, bf16[512,1024]{1,0:T(8,128)(2,1)}, u32[]{:S(2)}, u32[]{:S(2)}) collective-permute-start(bf16[512,1024]{1,0:T(8,128)(2,1)} %get-tuple-element.235), channel_id=1, source_target_pairs={{8,0},{24,1},{10,2},{26,3},{12,4},{28,5},{14,6},{30,7},{9,8},{25,9... | collective-permute-start | bytes 3145736 | tf_op jit(solution)/shard_map/ppermute | solution.py:679
  650.3 62.3 %collective-permute-start.35 = (bf16[512,2048]{1,0:T(8,128)(2,1)}, bf16[512,2048]{1,0:T(8,128)(2,1)}, u32[]{:S(2)}, u32[]{:S(2)}) collective-permute-start(bf16[512,2048]{1,0:T(8,128)(2,1)} %convolution_convert_fusion.2), channel_id=1, source_target_pairs={{0,1},{1,0},{2,3},{3,2},{4,5},{5,4},{6,7},{7,6},{8,9},{9,8},{10,11... | collective-permute-start | bytes 6291464 | tf_op jit(solution)/shard_map/ppermute | solution.py:656
  (120 other events, 1029.2 us)

commit v2 on v1

--- a/solution.py
+++ b/solution.py
@@ -17,6 +17,14 @@
 MASK = -float(2.0**100)
 NEAR = 128
 VMEM = 56 * 1024 * 1024
+CHUNK = 512
+PAD = 16
+FEED = 512
+COST = {
+    "entry": 6, "query": 6, "gather": 5, "self_forward": 23, "middle": 9, "cross_forward": 20, "feed_forward": 70,
+    "weight_grads": 9, "stage": 4, "cross_backward": 31, "back_middle": 12, "self_backward": 18, "exit": 11,
+}
+COST_SCALE = 0.001e9
 GELU_A = math.sqrt(2.0 / math.pi)
 GELU_B = GELU_A * 0.044715
 
@@ -55,7 +63,7 @@
         out_shape=list(out_shape) + [jax.ShapeDtypeStruct(x.shape, x.dtype) for x in hold],
         input_output_aliases=aliases,
         compiler_params=pltpu.CompilerParams(vmem_limit_bytes=VMEM),
-        cost_estimate=pl.CostEstimate(flops=int(flops), bytes_accessed=10**7, transcendentals=0),
+        cost_estimate=pl.CostEstimate(flops=int(COST.get(name, 5) * COST_SCALE), bytes_accessed=10**4, transcendentals=0),
         name=name,
     )(*inputs, *hold, *after)
     return list(outs[:count_out]), list(outs[count_out:])
@@ -88,13 +96,14 @@
 
 
 def chunk_of(member, part, chunks):
-    return jnp.where(part == 0, member, chunks - 1 - member)
+    high = jnp.bitwise_xor(part, member % 2)
+    return jnp.where(high == 0, member // 2, chunks - 1 - member // 2)
 
 
 def slot_of(member, chunk, chunks):
     high = (chunk >= chunks // 2).astype(jnp.int32)
     other = jnp.where(chunk >= chunks // 2, chunks - 1 - chunk, chunk)
-    return 2 * jnp.bitwise_xor(other, member) + high
+    return 2 * jnp.bitwise_xor(other, member // 2) + jnp.bitwise_xor(high, member % 2)
 
 
 def first_block(meta, member, chunk, chunks):
@@ -202,7 +211,7 @@
 
 
 def self_backward_kernel(chunks, sub, meta, q_ref, do_ref, o_ref, lse_ref, k_ref, v_ref, qf_ref, kf_ref,
-                         near_ref, corner_ref, dq_ref, dkv_ref, near_out, corner_out,
+                         near_ref, corner_ref, dq_ref, own_ref, peer_ref, near_out, corner_out,
                          dq_acc, dk_acc, dv_acc, near_acc, corner_acc):
     size = q_ref.shape[0]
     member = meta[0]
@@ -280,8 +289,11 @@
 
     @pl.when(last)
     def _():
-        dkv_ref[0] = dk_acc[...].astype(BF16)
-        dkv_ref[1] = dv_acc[...].astype(BF16)
+        for side, acc in enumerate((dk_acc, dv_acc)):
+            own_ref[side] = acc[: 2 * size, :].astype(BF16)
+            for other in range(peer_ref.shape[0]):
+                at = 2 * size * (other + 1)
+                peer_ref[other, side] = acc[at:at + 2 * size, :].astype(BF16)
 
     @pl.when(pl.program_id(2) == 1)
     def _():
@@ -290,26 +302,42 @@
             corner_out[head] = diagonal_sums(corner_acc[head])
 
 
-def self_forward(meta, q, kv, qf, kf, near, corner, chunks, hold=(), after=()):
+def with_before(kernel, inputs, in_specs, before):
+    if before is None:
+        return kernel, tuple(inputs), list(in_specs), None
+    count = len(inputs)
+
+    def body(*refs):
+        kernel(*refs[:count], *refs[count + len(before):])
+
+    specs = list(in_specs) + [pl.BlockSpec(memory_space=pl.ANY)] * len(before)
+    return body, tuple(inputs) + tuple(before), specs, {count + i: i for i in range(len(before))}
+
+
+def self_forward(meta, q, kv, qf, kf, near, corner, chunks, part, parts, before, hold=(), after=()):
     size = q.shape[0] // 2
     sub = min(256, size)
     length = kv.shape[0]
-    own = pl.BlockSpec((size, 128), lambda b, c, m: (c, b))
-    return call(
+    blocks = 8 // parts
+    shift = blocks * part
+    own = pl.BlockSpec((size, 128), lambda b, c, m: (c, b + shift))
+    kernel, inputs, in_specs, alias = with_before(
         functools.partial(self_forward_kernel, chunks, sub),
         (meta, q, kv, kv, qf, kf, near, corner),
         [
             own,
-            pl.BlockSpec((length, 128), lambda b, c, m: (0, b // 2)),
-            pl.BlockSpec((length, 128), lambda b, c, m: (0, 4 + b // 2)),
+            pl.BlockSpec((length, 128), lambda b, c, m: (0, (b + shift) // 2)),
+            pl.BlockSpec((length, 128), lambda b, c, m: (0, 4 + (b + shift) // 2)),
             pl.BlockSpec((size, 128), lambda b, c, m: (c, 0)),
             pl.BlockSpec((length, 128), lambda b, c, m: (0, 0)),
-            pl.BlockSpec((2, sub, sub), lambda b, c, m: (b, 0, 0)),
-            pl.BlockSpec((2, NEAR, NEAR), lambda b, c, m: (b, 0, 0)),
-        ],
+            pl.BlockSpec((2, sub, sub), lambda b, c, m: (b + shift, 0, 0)),
+            pl.BlockSpec((2, NEAR, NEAR), lambda b, c, m: (b + shift, 0, 0)),
+        ], before)
+    return call(
+        kernel, inputs, in_specs,
         [jax.ShapeDtypeStruct(q.shape, BF16), jax.ShapeDtypeStruct(q.shape, F32)],
         [own, own],
-        "self_forward", 4e10, grid=(8, 2), prefetch=1, hold=hold, after=after,
+        "self_forward", 4e10 / parts, grid=(blocks, 2), prefetch=1, hold=hold, after=after, alias=alias,
         scratch=[pltpu.VMEM((size, 256), F32), pltpu.VMEM((2, size, 128), F32)],
     )
 
@@ -331,29 +359,22 @@
         pl.BlockSpec((2, sub, sub), lambda g, b, c, m: (2 * (g + shift) + b, 0, 0)),
         pl.BlockSpec((2, NEAR, NEAR), lambda g, b, c, m: (2 * (g + shift) + b, 0, 0)),
     ]
-    kernel = functools.partial(self_backward_kernel, chunks, sub)
-    alias = None
-    if before is not None:
-        count = len(inputs)
-        alias = {count + i: i for i in range(len(before))}
-        inputs += before
-        in_specs += [pl.BlockSpec(memory_space=pl.ANY)] * len(before)
-        inner = kernel
-
-        def kernel(*refs):
-            inner(*refs[:count], *refs[count + len(before):])
-
+    kernel, inputs, in_specs, alias = with_before(
+        functools.partial(self_backward_kernel, chunks, sub), inputs, in_specs, before)
+    others = length // (2 * size) - 1
     return call(
-        kernel, tuple(inputs), in_specs,
+        kernel, inputs, in_specs,
         [
             jax.ShapeDtypeStruct(q.shape, BF16),
-            jax.ShapeDtypeStruct((2, length, 512), BF16),
+            jax.ShapeDtypeStruct((2, 2 * size, 512), BF16),
+            jax.ShapeDtypeStruct((others, 2, 2 * size, 512), BF16),
             jax.ShapeDtypeStruct((16, 8, 2 * sub), F32),
             jax.ShapeDtypeStruct((16, 8, 2 * NEAR), F32),
         ],
         [
             own,
-            pl.BlockSpec((2, length, 128), lambda g, b, c, m: (0, 0, g + shift)),
+            pl.BlockSpec((2, 2 * size, 128), lambda g, b, c, m: (0, 0, g + shift)),
+            pl.BlockSpec((others, 2, 2 * size, 128), lambda g, b, c, m: (0, 0, 0, g + shift)),
             pl.BlockSpec((2, 8, 2 * sub), lambda g, b, c, m: (2 * (g + shift) + b, 0, 0)),
             pl.BlockSpec((2, 8, 2 * NEAR), lambda g, b, c, m: (2 * (g + shift) + b, 0, 0)),
         ],
@@ -368,10 +389,15 @@
     )
 
 
-def cross_forward_kernel(q_ref, k_ref, v_ref, o_ref, lse_ref):
-    length = k_ref.shape[0]
-    keys = k_ref[...]
-    low, high = halves(v_ref[...])
+def stacked(refs):
+    return refs[0][...] if len(refs) == 1 else jnp.concatenate([ref[...] for ref in refs], axis=0)
+
+
+def cross_forward_kernel(count, q_ref, *refs):
+    keys, v = stacked(refs[:count]), stacked(refs[count:2 * count])
+    o_ref, lse_ref = refs[2 * count:]
+    length = keys.shape[0]
+    low, high = halves(v)
     one_low, one_high = halves(jnp.ones((length, 128), BF16))
     values = rows(lanes(low, one_low), lanes(high, one_high))
     weights, tops = [], []
@@ -387,7 +413,9 @@
     lse_ref[...] = jnp.where(is_low, tops[0], tops[1]) + jnp.log(total)
 
 
-def cross_backward_kernel(q_ref, do_ref, o_ref, lse_ref, k_ref, v_ref, dq_ref, dkv_ref, dk_acc, dv_acc):
+def cross_backward_kernel(count, q_ref, do_ref, o_ref, lse_ref, *refs):
+    k, v = stacked(refs[:count]), stacked(refs[count:2 * count])
+    dq_ref, dkv_refs, (dk_acc, dv_acc) = refs[2 * count], refs[2 * count + 1:3 * count + 1], refs[3 * count + 1:]
     first = (pl.program_id(1) == 0) & (pl.program_id(2) == 0)
     last = (pl.program_id(1) == 1) & (pl.program_id(2) == 1)
 
@@ -397,10 +425,9 @@
         dv_acc[...] = jnp.zeros_like(dv_acc)
 
     q_both, do_both, q_wide, do_wide = back_operands(q_ref, do_ref, o_ref, lse_ref, None)
-    k = k_ref[...]
     lane = lax.broadcasted_iota(jnp.int32, k.shape, 1)
     minus = jnp.where((lane >= 4) & (lane < 7), -1.0, 0.0).astype(BF16)
-    keys, vals = lanes(k, minus), lanes(v_ref[...], minus)
+    keys, vals = lanes(k, minus), lanes(v, minus)
     weights, grads = [], []
     for head in range(2):
         p = jnp.exp(nt(keys, q_wide[head]))
@@ -413,41 +440,54 @@
 
     @pl.when(last)
     def _():
-        dkv_ref[0] = dk_acc[...].astype(BF16)
-        dkv_ref[1] = dv_acc[...].astype(BF16)
-
-
-def cross_forward(q, kv, hold=(), after=()):
-    size, length = q.shape[0] // 2, kv.shape[0]
+        part = dk_acc.shape[0] // count
+        for number, ref in enumerate(dkv_refs):
+            at = slice(number * part, (number + 1) * part)
+            ref[0] = dk_acc[at, :].astype(BF16)
+            ref[1] = dv_acc[at, :].astype(BF16)
+
+
+def cross_forward(q, memories, hold=(), after=()):
+    size, part, count = q.shape[0] // 2, memories[0].shape[0], len(memories)
     own = pl.BlockSpec((size, 128), lambda b, c: (c, b))
     return call(
-        cross_forward_kernel, (q, kv, kv),
-        [
-            own,
-            pl.BlockSpec((length, 128), lambda b, c: (0, b // 2)),
-            pl.BlockSpec((length, 128), lambda b, c: (0, 4 + b // 2)),
-        ],
+        functools.partial(cross_forward_kernel, count), (q, *memories, *memories),
+        [own] + [pl.BlockSpec((part, 128), lambda b, c: (0, b // 2))] * count
+        + [pl.BlockSpec((part, 128), lambda b, c: (0, 4 + b // 2))] * count,
         [jax.ShapeDtypeStruct(q.shape, BF16), jax.ShapeDtypeStruct(q.shape, F32)],
         [own, own],
         "cross_forward", 15e9, grid=(8, 2), hold=hold, after=after,
     )
 
 
-def cross_backward(q, do, o, lse, kv, hold=(), after=()):
-    size, length = q.shape[0] // 2, kv.shape[0]
+def cross_backward(q, do, o, lse, memories, hold=(), after=()):
+    size, part, count = q.shape[0] // 2, memories[0].shape[0], len(memories)
     own = pl.BlockSpec((size, 128), lambda g, b, c: (c, 2 * g + b))
     return call(
-        cross_backward_kernel, (q, do, o, lse, kv, kv),
-        [
-            own, own, own, own,
-            pl.BlockSpec((length, 128), lambda g, b, c: (0, g)),
-            pl.BlockSpec((length, 128), lambda g, b, c: (0, 4 + g)),
-        ],
-        [jax.ShapeDtypeStruct(q.shape, BF16), jax.ShapeDtypeStruct((2, length, 512), BF16)],
-        [own, pl.BlockSpec((2, length, 128), lambda g, b, c: (0, 0, g))],
+        functools.partial(cross_backward_kernel, count), (q, do, o, lse, *memories, *memories),
+        [own, own, own, own] + [pl.BlockSpec((part, 128), lambda g, b, c: (0, g))] * count
+        + [pl.BlockSpec((part, 128), lambda g, b, c: (0, 4 + g))] * count,
+        [jax.ShapeDtypeStruct(q.shape, BF16)] + [jax.ShapeDtypeStruct((2, part, 512), BF16)] * count,
+        [own] + [pl.BlockSpec((2, part, 128), lambda g, b, c: (0, 0, g))] * count,
         "cross_backward", 30e9, grid=(4, 2, 2), hold=hold, after=after,
-        scratch=[pltpu.VMEM((length, 128), F32), pltpu.VMEM((length, 128), F32)],
+        scratch=[pltpu.VMEM((part * count, 128), F32), pltpu.VMEM((part * count, 128), F32)],
     )
+
+
+def add_kernel(*refs):
+    terms, outs = refs[:-2], refs[-2:]
+    for number, out in enumerate(outs):
+        at = slice(number * out.shape[0], (number + 1) * out.shape[0])
+        sides = [sum((ref[side, at, :].astype(F32) for ref in terms[1:]), terms[0][side, at, :].astype(F32)) for side in range(2)]
+        out[...] = lanes(*sides).astype(BF16)
+
+
+def add_memory(terms, hold=(), after=()):
+    shape = jax.ShapeDtypeStruct((terms[0].shape[1] // 2, 2 * terms[0].shape[2]), BF16)
+    (low, high), kept = call(
+        add_kernel, tuple(terms), [pl.BlockSpec(x.shape, lambda: (0, 0, 0)) for x in terms],
+        [shape] * 2, [pl.BlockSpec(shape.shape, lambda: (0, 0))] * 2, "add_memory", 1e9, hold=hold, after=after)
+    return low, high, kept
 
 
 def bias_kernel(sub, near_ref, corner_ref, near_out, back_out, corner_out, corner_back):
@@ -497,9 +537,100 @@
     return scale * (dn * gain - unit * share), gain_part
 
 
-def entry_kernel(x_ref, gain_ref, weight_ref, n_ref, kv_ref):
-    n_ref[...] = norm(x_ref[...].astype(F32), gain_ref[...])
-    kv_ref[...] = nn(n_ref[...], weight_ref[...]).astype(BF16)
+def entry_kernel(a_ref, b_ref, gain_ref, weight_ref, x_ref, n_ref, message_ref):
+    tokens = x_ref.shape[0]
+    size = tokens // 2
+    tile = min(256, size)
+    for side, ref in enumerate((a_ref, b_ref)):
+        for i in range(size // tile):
+            at = slice(side * size + i * tile, side * size + (i + 1) * tile)
+            x = ref[i * tile:(i + 1) * tile, :]
+            x_ref[at, :] = x
+            n_ref[at, :] = norm(x.astype(F32), gain_ref[...])
+            message_ref[at, :] = nn(n_ref[at, :], weight_ref[...]).astype(BF16)
+        message_ref[tokens + side * PAD:tokens + (side + 1) * PAD, :] = ref[size:, :]
+
+
+def entry(way_a, way_b, gain, weight, hold=(), after=()):
+    tokens, width = 2 * (way_a.shape[0] - PAD), way_a.shape[1]
+    inputs = (way_a, way_b, gain, weight)
+    shapes = [jax.ShapeDtypeStruct((count, width), BF16) for count in (tokens, tokens, tokens + 2 * PAD)]
+    return call(entry_kernel, inputs, [pl.BlockSpec(y.shape, lambda: (0, 0)) for y in inputs], shapes,
+                [pl.BlockSpec(s.shape, lambda: (0, 0)) for s in shapes], "entry", 2e9, hold=hold, after=after)
+
+
+def unpack_kernel(a_ref, b_ref, memory_ref, g_ref):
+    span, size = memory_ref.shape[0] // 2, g_ref.shape[0] // 2
+    for side, ref in enumerate((a_ref, b_ref)):
+        g_ref[side * size:(side + 1) * size, :] = ref[:size, :]
+        memory_ref[side * span:(side + 1) * span, :] = ref[size:, :]
+
+
+def unpack(second_a, second_b, size, after):
+    count, width = second_a.shape
+    whole = pl.BlockSpec((count, width), lambda: (0, 0))
+    shapes = [jax.ShapeDtypeStruct((2 * (count - size), width), BF16), jax.ShapeDtypeStruct((2 * size, width), BF16)]
+    outs, _ = call(unpack_kernel, (second_a, second_b), [whole, whole], shapes,
+                   [pl.BlockSpec(s.shape, lambda: (0, 0)) for s in shapes], "unpack", 1e9, after=after)
+    return outs
+
+
+def query_kernel(n_ref, weight_ref, q_ref):
+    q_ref[...] = nn(n_ref[...], weight_ref[...]).astype(BF16) * BF16(0.125)
+
+
+def gather_kernel(member_ref, *refs):
+    messages = refs[:len(refs) - 4]
+    kv_ref, key_ref, query_ref, meta_ref = refs[len(refs) - 4:]
+    step = pl.program_id(0)
+    tokens = messages[0].shape[0] - 2 * PAD
+    size = tokens // 2
+    for p, message in enumerate(messages):
+        @pl.when(step == p)
+        def _(p=p, message=message):
+            kv_ref[...] = message[:tokens, :]
+            shape = (size, 128)
+            lane = lax.broadcasted_iota(jnp.int32, shape, 1)
+            place = lax.broadcasted_iota(jnp.int32, (8, 128), 1)
+            chunks = 2 * len(messages)
+            meta = meta_ref[...]
+            if p == 0:
+                meta = jnp.where(place == 0, member_ref[0], 0)
+            for side in range(2):
+                at = tokens + side * PAD
+                numbers = message[at:at + PAD, :size].astype(F32)[:1]
+                column = jnp.broadcast_to(numbers, (128, size)).T.astype(jnp.int32)
+                same = (column == lane) & (lane < 4)
+                marks = jnp.where(lane < 4, jnp.where(same, 0.0, MASK), jnp.where(lane < 7, -1.0, 0.0))
+                key_ref[side * size:(side + 1) * size, :] = marks.astype(BF16)
+                if p == 0:
+                    query_ref[side * size:(side + 1) * size, :] = jnp.where(same, 1.0, 0.0).astype(BF16)
+                slot = 2 * p + side
+                meta = jnp.where(place == 1 + slot, column[:1, :], meta)
+                meta = jnp.where(place == 1 + chunks + slot, column[size - 1:, :], meta)
+            meta_ref[...] = meta
+
+
+def gather(member, messages, hold=(), after=()):
+    tokens, width = messages[0].shape[0] - 2 * PAD, messages[0].shape[1]
+    count = len(messages)
+    shapes = [
+        jax.ShapeDtypeStruct((count * tokens, width), BF16),
+        jax.ShapeDtypeStruct((count * tokens, 128), BF16),
+        jax.ShapeDtypeStruct((tokens, 128), BF16),
+        jax.ShapeDtypeStruct((8, 128), jnp.int32),
+    ]
+    outs, kept = call(
+        gather_kernel, (member,) + tuple(messages),
+        [pl.BlockSpec(m.shape, lambda i, s: (0, 0)) for m in messages], shapes,
+        [
+            pl.BlockSpec((tokens, width), lambda i, s: (i, 0)),
+            pl.BlockSpec((tokens, 128), lambda i, s: (i, 0)),
+            pl.BlockSpec((tokens, 128), lambda i, s: (0, 0)),
+            pl.BlockSpec((8, 128), lambda i, s: (0, 0)),
+        ],
+        "gather", 1e9, grid=(count,), prefetch=1, hold=hold, after=after)
+    return (outs[0], outs[1], outs[2], outs[3][0]), kept
 
 
 def middle_kernel(x_ref, o_ref, out_ref, gain_ref, query_ref, h_ref, n_ref, c_ref):
@@ -522,11 +653,16 @@
     do_ref[...] = nt(r_ref[...], out_ref[...]).astype(BF16)
 
 
-def exit_kernel(dq_ref, query_ref, dkv_ref, keyvalue_ref, x_ref, gain_ref, dh_ref, dx_ref, dgain_ref):
+def exit_kernel(dq_ref, query_ref, own_ref, *refs):
+    peers = refs[:len(refs) - 7]
+    keyvalue_ref, x_ref, gain_ref, dh_ref, dx_ref, dkv_ref, dgain_ref = refs[len(refs) - 7:]
+
     @pl.when(pl.program_id(0) == 0)
     def _():
         dgain_ref[...] = jnp.zeros_like(dgain_ref)
 
+    sides = [sum((ref[side].astype(F32) for ref in peers), own_ref[side].astype(F32)) for side in range(2)]
+    dkv_ref[...] = lanes(sides[0], sides[1]).astype(BF16)
     dn = nt(dq_ref[...], query_ref[...]) + nt(dkv_ref[...], keyvalue_ref[...])
     back, part = norm_back(x_ref[...].astype(F32), dn, gain_ref[...])
     dgain_ref[...] += part
@@ -537,7 +673,13 @@
     tokens = next(x.shape[0] for x, cut in arrays if cut)
     tile = min(256, tokens)
     blocks = pl.BlockSpec((tile, width), lambda i: (i, 0))
-    in_specs = [blocks if cut else pl.BlockSpec(x.shape, lambda i: (0, 0)) for x, cut in arrays]
+
+    def spec(x, cut):
+        if x.ndim == 3:
+            return pl.BlockSpec((x.shape[0], tile, x.shape[2]), lambda i: (0, i, 0))
+        return blocks if cut else pl.BlockSpec(x.shape, lambda i: (0, 0))
+
+    in_specs = [spec(x, cut) for x, cut in arrays]
     shapes = [jax.ShapeDtypeStruct((tokens, width), kind) for kind in outs]
     specs = [blocks] * len(outs)
     if dgain:
@@ -547,7 +689,7 @@
                 grid=(tokens // tile,), hold=hold, after=after)
 
 
-def feed_kernel(tile_rows, h1_ref, co_ref, cross_ref, g_ref, gain_ref, gate_ref, up_ref, down_ref,
+def feed_kernel(tile_rows, rest, h1_ref, co_ref, cross_ref, g_ref, gain_ref, gate_ref, up_ref, down_ref,
                 out_ref, n_ref, hidden_ref, dgu_ref, dh_ref, low_ref, dco_ref, dgain_ref,
                 out_acc, dn_acc, h_acc):
     tokens, width = h1_ref.shape
@@ -574,11 +716,11 @@
         each(start)
         dgain_ref[...] = jnp.zeros_like(dgain_ref)
 
-    def main(at):
+    def main(at, tile):
         n = n_ref[at, :]
-        gate = nn(n, gate_ref[...])
-        up = nn(n, up_ref[...])
-        dhidden = nt(g_ref[at, :], down_ref[...])
+        gate = nn(n, gate_ref[:, :tile])
+        up = nn(n, up_ref[:, :tile])
+        dhidden = nt(g_ref[at, :], down_ref[:tile, :])
         square = gate * gate
         bend = jnp.tanh(gate * (GELU_A + GELU_B * square))
         half = 0.5 + 0.5 * bend
@@ -587,13 +729,18 @@
         hidden = (gelu * up).astype(BF16)
         dgate = (dhidden * up * slope).astype(BF16)
         dup = (dhidden * gelu).astype(BF16)
-        hidden_ref[at, :] = hidden
+        hidden_ref[at, :tile] = hidden
         dgu_ref[at, :tile] = dgate
-        dgu_ref[at, tile:] = dup
-        out_acc[at, :] += nn(hidden, down_ref[...])
-        dn_acc[at, :] += nt(dgate, gate_ref[...]) + nt(dup, up_ref[...])
-
-    each(main)
+        dgu_ref[at, tile:2 * tile] = dup
+        out_acc[at, :] += nn(hidden, down_ref[:tile, :])
+        dn_acc[at, :] += nt(dgate, gate_ref[:, :tile]) + nt(dup, up_ref[:, :tile])
+
+    steps = pl.num_programs(0)
+    if rest == tile:
+        each(functools.partial(main, tile=tile))
+    else:
+        pl.when(step < steps - 1)(lambda: each(functools.partial(main, tile=tile)))
+        pl.when(step == steps - 1)(lambda: each(functools.partial(main, tile=rest)))
 
     @pl.when(step == pl.num_programs(0) - 1)
     def _():
@@ -613,13 +760,14 @@
 def feed_forward(h, co, cross_output, g, gain, feed_gate, feed_up, feed_down, hold=(), after=()):
     tokens, width = h.shape
     hidden = feed_gate.shape[1]
-    tile = 256
+    tile = FEED
+    rest = hidden - (hidden - 1) // tile * tile
     whole = pl.BlockSpec((tokens, width), lambda i: (0, 0), pipeline_mode=pl.Buffered(1))
     square = pl.BlockSpec((width, width), lambda i: (0, 0), pipeline_mode=pl.Buffered(1))
     row = pl.BlockSpec((1, width), lambda i: (0, 0))
     low, wide = jax.ShapeDtypeStruct(h.shape, BF16), jax.ShapeDtypeStruct(h.shape, F32)
     return call(
-        functools.partial(feed_kernel, 256),
+        functools.partial(feed_kernel, min(1024, tokens), rest),
         (h, co, cross_output, g, gain, feed_gate, feed_up, feed_down),
         [
             whole, whole, square, whole, row,
@@ -631,7 +779,7 @@
          wide, low, low, jax.ShapeDtypeStruct((8, width), F32)],
         [whole, whole, pl.BlockSpec((tokens, tile), lambda i: (0, i)), pl.BlockSpec((tokens, 2 * tile), lambda i: (0, i)),
          whole, whole, whole, pl.BlockSpec((8, width), lambda i: (0, 0))],
-        "feed_forward", 45e9, grid=(hidden // tile,), hold=hold, after=after,
+        "feed_forward", 45e9, grid=(pl.cdiv(hidden, tile),), hold=hold, after=after,
         scratch=[pltpu.VMEM((tokens, width), F32) for _ in range(3)],
     )
 
@@ -645,7 +793,6 @@
         self.members = self.S // 2
         self.member = (self.s // 4) * 2 + self.core
         self.first_half = self.s < self.S // 2
-        self.even_row = self.s % 2 == 0
         self.places = [(s, r) for s in range(self.S) for r in range(self.R)]
 
     def index(self, s, r):
@@ -672,15 +819,9 @@
     def go(self, x, way):
         return lax.ppermute(x, ("seq", "row"), self.route(way))
 
-    def back_part(self, low, high, way):
-        return jnp.where(self.even_row == (way == 0), low, high)
-
     def back(self, x, way):
         return lax.ppermute(x, ("seq", "row"), [(t, f) for f, t in self.route(way)])
 
-    def low_high(self, a, b):
-        return jnp.where(self.even_row, a, b), jnp.where(self.even_row, b, a)
-
     def two_rows(self, a, b):
         return jnp.where(self.first_half, a, b), jnp.where(self.first_half, b, a)
 
@@ -693,95 +834,197 @@
     def core_swap(self, x):
         return self.send(x, lambda s, r: (s, r ^ 1))
 
-    def all_sum(self, x):
-        for axis, size in (("row", self.R), ("seq", self.S)):
-            step = 1
-            while step < size:
-                x = x + lax.ppermute(x, axis, [(i, i ^ step) for i in range(size)])
-                step *= 2
-        return x
-
-    def halves_of(self, left):
-        half = left.shape[1] // 2
-        theirs = lax.dynamic_slice_in_dim(left, (1 - self.core) * half, half, 1)
-        return theirs, lax.dynamic_slice_in_dim(left, self.core * half, half, 1)
-
-    def bit(self, name):
-        return ((self.s if name[0] == "seq" else self.r) >> name[1]) & 1
+    def sum_axes(self):
+        sizes = [("row", self.R), ("seq", self.S)]
+        return [(axis, bit) for axis, size in sizes for bit in range(size.bit_length() - 1)]
 
     def names(self):
         top = self.S.bit_length() - 2
         row_bits = list(range(1, self.R.bit_length() - 1))
         return [("seq", k) for k in reversed(range(top))] + [("row", k) for k in reversed(row_bits)] + [("row", 0)]
 
-    def begin(self, x):
-        names = self.names()
-        return x.reshape((2,) * len(names) + (x.shape[0] // 2 ** len(names), x.shape[1])), names
-
-    def split(self, x, names, name):
-        at = names.index(name)
-        flat = x.reshape(math.prod(x.shape[:at]), 2, math.prod(x.shape[at + 1:-1]), x.shape[-1])
-        give = lax.dynamic_index_in_dim(flat, 1 - self.bit(name), 1, keepdims=False)
-        keep = lax.dynamic_index_in_dim(flat, self.bit(name), 1, keepdims=False)
-        return give, keep
+    def bits(self):
+        values = [((self.s if kind == "seq" else self.r) >> bit) & 1 for kind, bit in self.names()[:-1]]
+        return jnp.stack(values + [self.s >> (self.S.bit_length() - 2)]).astype(jnp.int32)
 
     def swap(self, give, name):
         size = self.S if name[0] == "seq" else self.R
         return lax.ppermute(give, name[0], [(i, i ^ (1 << name[1])) for i in range(size)])
 
-    def merge(self, keep, got, x, names, name):
-        at = names.index(name)
-        total = (keep.astype(F32) + got.astype(F32)).astype(BF16)
-        return total.reshape(x.shape[:at] + x.shape[at + 1:]), names[:at] + names[at + 1:]
-
-    def last_sends(self, x):
-        top = self.S.bit_length() - 2
-        upper, half = self.s >> top, self.S // 2
-        straight = lax.dynamic_index_in_dim(x, upper, 0, keepdims=False)
-        crossed = lax.dynamic_index_in_dim(x, 1 - upper, 0, keepdims=False)
+    def last_sends(self, straight, crossed):
+        half = self.S // 2
         one = self.send(straight, lambda s, r: ((r % 2) * half + s % half, (r - r % 2) + s // half))
         two = self.send(crossed, lambda s, r: ((r % 2) * half + s % half, (r - r % 2) + 1 - s // half))
         return one, two
 
 
-class Scatter:
-    def __init__(self, group, x, flip=False):
-        self.group = group
-        self.x, self.names = group.begin(x)
-        row_names = [name for name in self.names if name[0] == "row" and name[1]]
-        seq_names = [name for name in self.names if name[0] == "seq"]
-        self.stages = (row_names if flip else row_names[::-1]) + seq_names[::-1]
-
-    def start(self):
-        if self.stages:
-            self.give = self.group.split(self.x, self.names, self.stages[0])[0]
-            self.got = self.group.swap(self.give, self.stages[0])
-        else:
-            self.got = self.group.last_sends(self.x)
-            self.give = self.x
-
-    def end(self):
-        name = self.stages.pop(0)
-        keep = self.group.split(self.x, self.names, name)[1]
-        self.x, self.names = self.group.merge(keep, self.got, self.x, self.names, name)
-
-    def step(self):
-        if self.stages:
-            self.end()
-            self.start()
+def grad_kernel(jobs, blocks, rows_in, half_ref, *refs):
+    out_ref = refs[2 * len(jobs)]
+    step = pl.program_id(0)
+    rows_out = -(-rows_in // 16) * 16
+
+    def one(left_ref, right_ref, count, paired):
+        total = tn(left_ref[...], right_ref[:, :count * CHUNK])
+        for chunk in range(count):
+            block = total[:, chunk * CHUNK:(chunk + 1) * CHUNK].reshape(blocks, rows_in, CHUNK)
+            if paired:
+                block = block.reshape(-1, 2, 2, 64 // rows_in, rows_in, CHUNK)
+                block = jnp.swapaxes(block, 1, 2).reshape(blocks, rows_in, CHUNK)
+            if rows_out > rows_in:
+                block = jnp.concatenate([block, jnp.zeros((blocks, rows_out - rows_in, CHUNK), F32)], axis=1)
+            out_ref[:, chunk * rows_out:(chunk + 1) * rows_out, :] = block.astype(BF16)
+
+    for k, (start, full, rest, paired) in enumerate(jobs):
+        if full:
+            run = functools.partial(one, refs[2 * k], refs[2 * k + 1], 2, paired)
+            pl.when((step >= start) & (step < start + full))(run)
+        if rest:
+            run = functools.partial(one, refs[2 * k], refs[2 * k + 1], 1, paired)
+            pl.when(step == start + full)(run)
+
+
+def grad_part(half, pairs, blocks, rows_in, total, offset=0, before=None, hold=(), after=(), holds=False):
+    rows_out = -(-rows_in // 16) * 16
+    jobs, inputs, in_specs = [], [half], []
+    start = 0
+    for left, right, *paired in pairs:
+        full, rest = divmod(right.shape[1] // CHUNK, 2)
+        steps = full + rest
+        tokens, side = left.shape[0], left.shape[1] // 2
+        jobs.append((start, full, rest, bool(paired)))
+        inputs += [left, right]
+        in_specs += [
+            pl.BlockSpec((tokens, side), lambda i, h: (0, h[0])),
+            pl.BlockSpec((tokens, 2 * CHUNK), lambda i, h, start=start, steps=steps: (0, jnp.clip(i - start, 0, steps - 1))),
+        ]
+        start += steps
+    first = offset // (2 * rows_out)
+    kernel, inputs, in_specs, alias = with_before(
+        functools.partial(grad_kernel, tuple(jobs), blocks, rows_in), inputs, in_specs, before)
+    (out,), kept = call(
+        kernel, inputs, in_specs,
+        [jax.ShapeDtypeStruct((blocks, total, CHUNK), BF16)],
+        [pl.BlockSpec((blocks, 2 * rows_out, CHUNK), lambda i, h: (0, first + i, 0))],
+        "weight_grads", 1e9, grid=(start,), prefetch=1, hold=hold, after=after, alias=alias,
+    )
+    return (out, kept) if holds else out
+
+
+def stage_kernel(plan, bits_ref, *refs):
+    count = max(max(terms) for _, terms, _ in plan) + 1
+    for out, terms, at in plan:
+        total = sum((refs[t][...].astype(F32) for t in terms[1:]), refs[terms[0]][...].astype(F32))
+        refs[count + out][:, at, :] = total.astype(BF16)
+
+
+class Stream:
+    def __init__(self, terms, names, order, rows_in):
+        self.terms, self.names, self.order, self.rows_in = terms, names, list(order), rows_in
+
+    def got(self, array, names):
+        self.terms.append((array, names, 0))
+
+
+def stage(group, bits, streams, keep=True, join=False, after=(), hold=()):
+    all_names = group.names()
+    inputs, in_specs, shapes, out_specs, plan = [bits], [], [], [], []
+    grid = 2 ** (len(streams[0].names) - 1)
+    lead = 2 if streams[0].order[0] != all_names[-1] and grid > 1 else 1
+    for number, stream in enumerate(streams):
+        axis = stream.order[0]
+        rest = [name for name in stream.names if name != axis]
+
+        def spec(names, part, give, rest=rest, axis=axis, rows_in=stream.rows_in):
+            def place(i, b):
+                index = 0
+                for name in names if lead == 1 else names[:-1]:
+                    own = b[all_names.index(name)]
+                    if name == axis:
+                        value = 1 - own if give else own
+                    elif name in rest:
+                        value = (i * lead >> (len(rest) - 1 - rest.index(name))) & 1
+                    else:
+                        value = own
+                    index = index * 2 + value
+                return (index, part, 0)
+
+            return pl.BlockSpec((lead, rows_in, CHUNK), place)
+
+        sides = (True, False) if keep else (True,)
+        for give in sides:
+            terms = []
+            for array, names, part in stream.terms:
+                terms.append(len(inputs) - 1)
+                inputs.append(array)
+                in_specs.append(spec(names, part, give))
+            count = stream.rows_in
+            if join:
+                plan.append((0 if give else 1, tuple(terms), slice(number * count, (number + 1) * count)))
+            else:
+                plan.append((len(shapes), tuple(terms), slice(0, count)))
+            if not join or number == 0:
+                full = count * (len(streams) if join else 1)
+                shapes.append(jax.ShapeDtypeStruct((grid, full, CHUNK), BF16))
+                out_specs.append(pl.BlockSpec((lead, full, CHUNK), lambda i, b: (i, 0, 0)))
+    return call(functools.partial(stage_kernel, tuple(plan)), tuple(inputs), in_specs, shapes, out_specs, "stage", 1e9,
+                grid=(grid // lead,), prefetch=1, after=after, hold=hold)
+
+
+class Bundle:
+    def __init__(self, group, bits):
+        self.group, self.bits = group, bits
+
+    def swap(self, theirs):
+        self.other = self.group.core_swap(theirs)
+
+    def begin(self, mine, after=(), hold=()):
+        names = self.group.names()
+        rows_axes = [name for name in names if name[0] == "row" and name[1]]
+        seq_axes = [name for name in names if name[0] == "seq"][::-1]
+        half = mine.shape[1] // 2
+        self.streams = [
+            Stream([(mine, names, n), (self.other, names, n)], names, (rows_axes[::-1], rows_axes)[n] + seq_axes + [("row", 0)], half)
+            for n in range(2)
+        ]
+        self.gives, kept = stage(self.group, self.bits, self.streams, keep=False, after=after, hold=hold)
+        self.send()
+        return kept
+
+    def send(self):
+        self.fly = [self.group.swap(give, s.order[0]) for give, s in zip(self.gives, self.streams)]
+
+    def step(self, after=(), hold=()):
+        if not self.streams[0].order[1:]:
+            return list(hold)
+        for stream, got in zip(self.streams, self.fly):
+            axis = stream.order.pop(0)
+            stream.names = [name for name in stream.names if name != axis]
+            stream.got(got, list(stream.names))
+        one = self.streams[0]
+        join = len(self.streams) == 2 and one.names == self.streams[1].names and one.order == self.streams[1].order
+        outs, kept = stage(self.group, self.bits, self.streams, join=join, after=after, hold=hold)
+        axis = one.order[0]
+        if join:
+            self.streams = [Stream([], list(one.names), one.order, 2 * one.rows_in)]
+        if axis == ("row", 0):
+            crossed, straight = outs
+            self.gives = [crossed]
+            self.ends = self.group.last_sends(straight, crossed)
+            return kept
+        self.gives = []
+        for n, stream in enumerate(self.streams):
+            self.gives.append(outs[2 * n])
+            rest = [name for name in stream.names if name != stream.order[0]]
+            stream.terms = [(outs[2 * n + 1], rest, 0)]
+        self.send()
+        return kept
+
+    def finish(self):
+        while self.streams[0].order[1:]:
+            self.step()
 
     def result(self):
-        while self.stages:
-            self.step()
-        return self.got[0].astype(F32) + self.got[1].astype(F32)
-
-
-def through(function, *args, run=(), hold=(), **more):
-    hold = list(hold)
-    outs, kept = function(*args, hold=hold + [one.x for one in run], after=[one.give for one in run], **more)
-    for one, x in zip(run, kept[len(hold):]):
-        one.x = x
-    return outs, kept[:len(hold)]
+        return self.ends[0][0].astype(F32) + self.ends[1][0].astype(F32)
 
 
 def by_pairs(weight, axis):
@@ -829,160 +1072,189 @@
     group = Group()
     size, width = tokens.shape[1:]
     span = memory.shape[1]
+    hidden_width = feed_gate.shape[1]
     chunks = group.chunks
     sub = min(256, size)
-    pad = 16
-
-    numbers = jnp.pad(segment_ids.astype(BF16)[:, None, :], ((0, 0), (0, pad - 1), (0, width - size)))
-    token_message = jnp.concatenate([tokens, numbers], axis=1)
-    way_a = group.go(group.part(token_message, 0), 0)
-    way_b = group.go(group.part(token_message, 1), 1)
+    bits = group.bits()
+    core = group.core.astype(jnp.int32)[None]
+    devices = group.S * group.R
+    blocks = devices // 2
+
+    def token_part(way):
+        numbers = group.part(segment_ids, way).astype(BF16)
+        numbers = jnp.pad(numbers[None], ((0, PAD - 1), (0, width - size)))
+        return jnp.concatenate([group.part(tokens, way), numbers], axis=0)
+
+    way_a = group.go(token_part(0), 0)
+    way_b = group.go(token_part(1), 1)
 
     memory_rows = memory.reshape(-1, width)
     pairs = nn(memory_rows, cross_keyvalue).astype(BF16).reshape(2, span, width)
     own_query, own_output = by_pairs(self_query, 1), by_pairs(self_output, 0)
     other_query, other_output = by_pairs(cross_query, 1), by_pairs(cross_output, 0)
     near, near_back, corner, corner_back = bias_tiles(*bias_rows(bias_table, sub), sub)
-    pairs_a, pairs_b = group.part(pairs, 0), group.part(pairs, 1)
-
-    low, high = group.low_high(way_a, way_b)
-    x = rows(low[:size], high[:size])
-    memory_a = group.go(pairs_a, 0)
-
-    (n1, kv), (pairs_b,) = by_rows(
-        entry_kernel, "entry", 2e9, [(x, True), (gain_attend[None], False), (self_keyvalue, False)], [BF16, BF16], width,
-        hold=[pairs_b], after=[pairs_a, own_query, own_output, other_query, other_output, near])
-    memory_b = group.go(pairs_b, 1)
-    kv_messages = group.peers(jnp.concatenate([kv, low[size:], high[size:]], axis=0))
-    q = nn(n1, own_query).astype(BF16) * BF16(0.125)
-    kv = jnp.concatenate([part[:2 * size] for part in kv_messages], axis=0)
-    segments = jnp.concatenate([part[2 * size::pad, :size] for part in kv_messages], axis=0).astype(jnp.int32)
-    meta = jnp.concatenate([group.member[None].astype(jnp.int32), segments[:, 0], segments[:, -1]])
-    lane = jnp.arange(128)[None]
-    same = (segments.reshape(-1, 1) == lane) & (lane < 4)
-    key_marks = jnp.where(lane < 4, jnp.where(same, 0.0, MASK), jnp.where(lane < 7, -1.0, 0.0)).astype(BF16)
-    query_marks = same[: 2 * size].astype(BF16)
-    grad_a, grad_b = group.part(cotangent, 0), group.part(cotangent, 1)
-    g_a = group.go(grad_a, 0)
-    (o, lse), (grad_b, memory_a) = self_forward(
-        meta, q, kv, query_marks, key_marks, near, corner, chunks, hold=[grad_b, memory_a], after=[grad_a, memory_b])
-    g_b = group.go(grad_b, 1)
-    memory_kv = rows(*group.low_high(memory_a, memory_b))
-    (h1, n2, c), (memory_kv,) = by_rows(
+    second = [jnp.concatenate([group.part(cotangent, way), group.part(pairs, way)], axis=0) for way in range(2)]
+
+    (x, n1, message), (second_a,) = entry(
+        way_a, way_b, gain_attend[None], self_keyvalue, hold=[second[0]],
+        after=[own_query, own_output, other_query, other_output, near, second[1]])
+    messages = group.peers(message)
+    second_a = group.go(second_a, 0)
+    second_b = group.go(second[1], 1)
+    (q,), _ = by_rows(query_kernel, "query", 2e9, [(n1, True), (own_query, False)], [BF16], width)
+    (kv, key_marks, query_marks, meta), _ = gather(
+        (2 * group.member + group.s % 2).astype(jnp.int32)[None], messages, after=[q])
+    (o, lse), _ = self_forward(meta, q, kv, query_marks, key_marks, near, corner, chunks, 0, 1, None)
+    memory_own, g = unpack(second_a, second_b, size, [o])
+    memories = group.peers(memory_own)
+    (h1, n2, c), _ = by_rows(
         middle_kernel, "middle", 5e9,
         [(x, True), (o, True), (own_output, False), (gain_cross[None], False), (other_query, False)],
-        [F32, BF16, BF16], width, hold=[memory_kv], after=[grad_b, g_a])
-    memory_kv = jnp.concatenate(group.peers(memory_kv), axis=0)
-    (co, cross_lse), _ = cross_forward(c, memory_kv, after=[grad_b])
-    g = rows(*group.low_high(g_a, g_b))
+        [F32, BF16, BF16], width, after=[memory_own])
+    (co, cross_lse), _ = cross_forward(c, memories)
     (out, n3, hidden, dgu, dh2, r2, dco, dgain_feed), _ = feed_forward(
         h1, co, other_output, g, gain_feed[None], feed_gate, feed_up, feed_down)
-    out_parts = [group.back_part(out[:size], out[size:], way) for way in range(2)]
-    out_a = group.back(out_parts[0], 0)
-
-    hidden_theirs, hidden_mine = group.halves_of(hidden)
-    n3_theirs, n3_mine = group.halves_of(n3)
-    down_other = group.core_swap(tn(hidden_theirs, g).astype(BF16))
-    dgu_other = group.core_swap(tn(n3_theirs, dgu).astype(BF16))
-    down_part = (tn(hidden_mine, g) + down_other.astype(F32)).astype(BF16)
-    dgu_part = (tn(n3_mine, dgu) + dgu_other.astype(F32)).astype(BF16)
-    quarter = dgu_part.shape[1] // 4
-    feed = [
-        Scatter(group, down_part),
-        Scatter(group, dgu_part[:, :quarter]),
-        Scatter(group, dgu_part[:, quarter:], True),
-    ]
-    for one in feed:
-        one.start()
-
-    out_b = group.back(out_parts[1], 1)
-    (dc, dm), (out_a,) = through(
-        cross_backward, c, dco, co, cross_lse, memory_kv, run=feed, hold=[out_a])
-    dm = lanes(dm[0], dm[1]).reshape(group.members, 2 * span, width)
-    dm_parts = [dm[0]] + [group.peer(dm[p], p) for p in range(1, group.members)]
-    (dh1, r1, do, dgain_cross), (out_a, dm_own) = through(
-        by_rows, back_middle_kernel, "back_middle", 5e9,
+
+    feed_rows = hidden.shape[1] // devices
+    if feed_rows % 8:
+        padded = -(-feed_rows // 16) * 16
+        hidden = jnp.pad(hidden.reshape(-1, devices, feed_rows), ((0, 0), (0, 0), (0, padded - feed_rows)))
+        hidden = hidden.reshape(-1, devices * padded)
+    down_rows = hidden.shape[1] // devices
+    down_out = -(-down_rows // 16) * 16
+    square_rows = width // devices
+    square_out = -(-square_rows // 16) * 16
+    down_total = down_out * (width // CHUNK)
+    feed_total = -(-(down_total + square_out * (dgu.shape[1] // CHUNK)) // 32) * 32
+
+    def feed_half(which, after=(), hold=()):
+        base = grad_part(which, [(hidden, g)], blocks, down_rows, feed_total, after=after)
+        return grad_part(which, [(n3, dgu)], blocks, square_rows, feed_total, down_total, [base], hold=hold, holds=True)
+
+    out_a, out_b = out[:size], out[size:]
+    theirs, (out_b,) = feed_half(1 - core, after=[out_a], hold=[out_b])
+    out_a = group.back(out_a, 0)
+    feed = Bundle(group, bits)
+    feed.swap(theirs)
+    mine, (out_b,) = feed_half(core, after=[theirs], hold=[out_b])
+    out_a, = feed.begin(mine, hold=[out_a])
+    out_b = group.back(out_b, 1)
+
+    (dc, dm, *dm_peers), _ = cross_backward(c, dco, co, cross_lse, memories, after=feed.gives)
+    (dh1, r1, do, dgain_cross), _ = by_rows(
+        back_middle_kernel, "back_middle", 5e9,
         [(dc, True), (other_query, False), (h1, True), (gain_cross[None], False), (dh2, True), (own_output, False)],
-        [F32, BF16, BF16], width, dgain=True, run=feed, hold=[out_a, dm_parts[0]])
-    layer_output = jnp.stack(group.two_rows(out_a, out_b))
-    dm = sum((part.astype(F32) for part in dm_parts[1:]), dm_own.astype(F32)).astype(BF16)
-    dm_a = group.back(group.back_part(dm[:span], dm[span:], 0), 0)
-    dm_b = group.back(group.back_part(dm[:span], dm[span:], 1), 1)
-    for one in feed:
-        one.step()
-    cross_lefts = [group.halves_of(left) for left in (co, n2, o)]
-    cross_others = [group.core_swap(tn(left[0], right).astype(BF16)) for left, right in zip(cross_lefts, (r2, dc, r1))]
-    cross_parts = [
-        (tn(left[1], right) + other.astype(F32)).astype(BF16)
-        for left, right, other in zip(cross_lefts, (r2, dc, r1), cross_others)
-    ]
+        [F32, BF16, BF16], width, dgain=True)
+    cross_pairs = [(co, r2, True), (n2, dc), (o, r1, True)]
+    cross_total = 3 * square_out * (width // CHUNK)
+    theirs, (out_b, *dm_peers) = grad_part(
+        1 - core, cross_pairs, blocks, square_rows, cross_total, hold=[out_b] + dm_peers, holds=True)
+    theirs, = feed.step(hold=[theirs], after=[out_b])
+    cross = Bundle(group, bits)
+    cross.swap(theirs)
+    dm_peers = [group.peer(term, p + 1) for p, term in enumerate(dm_peers)]
+    mine, (dm,) = grad_part(
+        core, cross_pairs, blocks, square_rows, cross_total, after=[theirs] + feed.gives, hold=[dm], holds=True)
+    dm_a, dm_b, _ = add_memory([dm] + dm_peers)
+
+    def backward(part, before, after, hold=()):
+        return self_backward(meta, q, do, o, lse, kv, query_marks, key_marks, near_back, corner_back, chunks,
+                             part, 4, before, after=after, hold=hold)
+
+    back, (dm_b, mine) = backward(0, None, [dm_a, cross.other], [dm_b, mine])
+    dm_a = group.back(dm_a, 0)
+    dm_a, = feed.step(after=[back[0], mine], hold=[dm_a])
+    cross.begin(mine, after=feed.gives)
+    back, (dm_b,) = backward(1, back, feed.gives + cross.gives, [dm_b])
+    feed.step(after=[back[0]])
+    cross.step(after=[back[0]] + feed.gives)
+    back, (dm_b,) = backward(2, back, feed.gives + cross.gives, [dm_b])
+    feed.finish()
+    cross.step(after=[back[0]] + list(feed.ends))
+    dm_b = group.back(dm_b, 1)
+    back, _ = backward(3, back, cross.gives)
+    dq, dkv_own, dkv_peers, near_sum, corner_sum = back
+    dm_b, dkv_peers = cross.step(after=[dq], hold=[dm_b, dkv_peers])
+    cross.finish()
+    dkv_peers = [group.peer(dkv_peers[p - 1], p) for p in range(1, group.members)]
     dm = rows(*group.two_rows(dm_a, dm_b))
-    memory_lefts = group.halves_of(memory_rows)
-    memory_other = group.core_swap(tn(memory_lefts[0], dm).astype(BF16))
-    memory_grad = nt(dm, cross_keyvalue).astype(BF16).reshape(memory.shape)
-    memory_part = (tn(memory_lefts[1], dm) + memory_other.astype(F32)).astype(BF16)
-    cross = [
-        Scatter(group, jnp.concatenate([by_pairs(cross_parts[0], 0), cross_parts[1]], axis=1)),
-        Scatter(group, jnp.concatenate([by_pairs(cross_parts[2], 0), memory_part], axis=1), True),
-    ]
-    for one in cross:
-        one.start()
-
-    back = None
-    parts = 4
-    for part in range(parts):
-        back, _ = through(
-            self_backward, meta, q, do, o, lse, kv, query_marks, key_marks, near_back, corner_back, chunks,
-            part, parts, back, run=feed + cross)
-        if part == 0:
-            for one in feed:
-                one.step()
-        if part == 1:
-            for one in cross:
-                one.step()
-        if part == 2:
-            for one in feed + cross:
-                one.step()
-    dq, dkv, near_sum, corner_sum = back
-    dkv = lanes(dkv[0], dkv[1]).reshape(group.members, 2 * size, width)
-    dkv = sum((group.peer(dkv[p], p).astype(F32) for p in range(1, group.members)), dkv[0].astype(F32)).astype(BF16)
-    (tokens_grad, dgain_attend), _ = through(
-        by_rows, exit_kernel, "exit", 5e9,
-        [(dq, True), (own_query, False), (dkv, True), (self_keyvalue, False), (x, True), (gain_attend[None], False), (dh1, True)],
-        [BF16], width, dgain=True, run=cross)
-    token_a = group.back(group.back_part(tokens_grad[:size], tokens_grad[size:], 0), 0)
-    left = group.halves_of(n1)
-    right = lanes(dq, dkv)
-    other = group.core_swap(tn(left[0], right).astype(BF16))
-    own_part = (tn(left[1], right) + other.astype(F32)).astype(BF16)
-    own = [Scatter(group, own_part[:, :width]), Scatter(group, own_part[:, width:], True)]
-    for one in own:
-        one.start()
-    token_b = group.back(group.back_part(tokens_grad[:size], tokens_grad[size:], 1), 1)
-    tokens_grad = jnp.stack(group.two_rows(token_a, token_b))
-    grad_own = [one.result() for one in own]
-    grad_cross = [one.result() for one in cross]
-    grad_feed = [one.result() for one in feed]
-
+    own_total = 3 * square_out * (width // CHUNK)
+    step = square_out * (width // CHUNK)
+    theirs = grad_part(1 - core, [(n1, dq), (memory_rows, dm)], blocks, square_rows, own_total, after=cross.gives)
+    (tokens_grad, dkv, dgain_attend), (theirs,) = by_rows(
+        exit_kernel, "exit", 5e9,
+        [(dq, True), (own_query, False), (dkv_own, True)] + [(y, True) for y in dkv_peers]
+        + [(self_keyvalue, False), (x, True), (gain_attend[None], False), (dh1, True)],
+        [BF16, BF16], width, dgain=True, hold=[theirs])
+    token_a, token_b = tokens_grad[:size], tokens_grad[size:]
+    theirs, (token_b,) = grad_part(1 - core, [(n1, dkv)], blocks, square_rows, own_total, 2 * step, [theirs],
+                                   after=[token_a], hold=[token_b], holds=True)
+    token_a = group.back(token_a, 0)
+    own = Bundle(group, bits)
+    own.swap(theirs)
+    mine, (out_a, out_b, *ends) = grad_part(
+        core, [(n1, dq), (memory_rows, dm), (n1, dkv)], blocks, square_rows, own_total, after=[theirs],
+        hold=[out_a, out_b, near_sum, dgain_attend, dm] + list(feed.ends) + list(cross.ends), holds=True)
+    near_sum, dgain_attend, dm_late, *ends = ends
+    feed.ends, cross.ends = ends[:2], ends[2:]
     dbias = bias_table_sums(near_sum, corner_sum)
     small = jnp.stack([jnp.sum(dgain_attend, axis=0), jnp.sum(dgain_cross, axis=0), jnp.sum(dgain_feed, axis=0),
                        jnp.pad(dbias.reshape(-1), (0, width - dbias.size))])
-    small = group.all_sum(small)
-
-    dgu = jnp.concatenate(grad_feed[1:], axis=1).reshape(-1, feed_gate.shape[1] // 256, 2, 256)
+    sum_axes = group.sum_axes()
+
+    def small_step(x):
+        return x + group.swap(x, sum_axes.pop(0))
+
+    small = small_step(small)
+    layer_output = jnp.stack(group.two_rows(out_a, out_b))
+    memory_grad = nt(dm_late, cross_keyvalue).astype(BF16).reshape(memory.shape)
+    token_b, token_a, small, *ends = own.begin(
+        mine, after=[layer_output, memory_grad], hold=[token_b, token_a, small] + list(feed.ends) + list(cross.ends))
+    feed.ends, cross.ends = ends[:2], ends[2:]
+    token_b = group.back(token_b, 1)
+    small = small_step(small)
+
+    def squares(bundle, start, columns):
+        rest = bundle[start:start + square_out * (columns // CHUNK)].reshape(columns // CHUNK, square_out, CHUNK)
+        return jnp.swapaxes(rest[:, :square_rows], 0, 1).reshape(square_rows, columns)
+
+    feed_sum, cross_sum = feed.result(), cross.result()
+    grad_cross = [squares(cross_sum, n * step, width) for n in range(3)]
+    grad_cross[1] = by_pairs(grad_cross[1], 1)
+    grad_dgu = squares(feed_sum, down_total, dgu.shape[1])
+    whole = hidden_width // FEED * FEED
+    grad_dgu, grad_rest = grad_dgu[:, :2 * whole].reshape(square_rows, -1, 2, FEED), grad_dgu[:, 2 * whole:]
+    grad_rest = grad_rest.reshape(square_rows, 2, hidden_width - whole)
+    grad_gate, grad_up = [
+        jnp.concatenate([grad_dgu[:, :, n].reshape(square_rows, -1), grad_rest[:, n]], axis=1) for n in range(2)]
+    grad_down = feed_sum[:down_total].reshape(width // CHUNK, down_out, CHUNK)[:, :feed_rows]
+    grad_down = jnp.swapaxes(grad_down, 0, 1).reshape(feed_rows, width)
+
+    token_a, token_b, small = own.step(hold=[token_a, token_b, small], after=grad_cross + [grad_gate, grad_up, grad_down])
+    small = small_step(small)
+    tokens_grad = jnp.stack(group.two_rows(token_a, token_b))
+    small, = own.step(hold=[small], after=[tokens_grad])
+    small = small_step(small)
+    small, = own.step(hold=[small])
+    own.finish()
+    while sum_axes:
+        small = small_step(small)
+    own_sum = own.result()
+    grad_own = [squares(own_sum, n * step, width) for n in (0, 2, 1)]
+
     return (
         layer_output,
         tokens_grad,
         memory_grad,
         by_pairs(grad_own[0], 1),
         grad_own[1],
-        grad_cross[1][:, :width],
-        by_pairs(grad_cross[0][:, width:], 1),
-        grad_cross[1][:, width:],
-        grad_cross[0][:, :width],
-        dgu[:, :, 0].reshape(-1, feed_gate.shape[1]),
-        dgu[:, :, 1].reshape(-1, feed_gate.shape[1]),
-        grad_feed[0],
+        grad_cross[2],
+        grad_cross[1],
+        grad_own[2],
+        grad_cross[0],
+        grad_gate,
+        grad_up,
+        grad_down,
         small[0],
         small[1],
         small[2],

time: 773 us -> 666 us (0.86)
  Pallas kernels: 307 us -> 437 us
  waiting for transfers between devices: 91.1 us -> 25.2 us
  matrix products: 68 us -> 6.98 us
  other arithmetic: 76.8 us -> 22.2 us
  starting transfers between devices: 126 us -> 85 us
  local copies, waits for them, and re-layouts: 89.3 us -> 78.2 us
    pallas_call x12 -> x37, Pallas kernels: 300 us -> 430 us  [call(): pl.pallas_call(body, grid_spec=pltpu.PrefetchScalarGridSpec(num_scalar_pr...]
    dot_general x14 -> x0, matrix products: 58.4 us -> none  [tn(): lax.dot_general(a, b, (((0,), (0,)), ((), ())), preferred_element_type=F32)]
    ppermute x5 -> x0, waiting for transfers between devices: 35.2 us -> none  [all_sum(): x = x + lax.ppermute(x, axis, [(i, i ^ step) for i in range(size)])]
    ppermute x25 -> x13, starting transfers between devices: 42.7 us -> 15.1 us  [send(): return lax.ppermute(x, ('seq', 'row'), pairs)]
    convert_element_type x25 -> x1, other arithmetic: 24.7 us -> 0.86 us  [token_part(): numbers = group.part(segment_ids, way).astype(BF16)]
    ppermute x25 -> x13, waiting for transfers between devices: 25.4 us -> 7.59 us  [send(): return lax.ppermute(x, ('seq', 'row'), pairs)]
    squeeze x28 -> x2, local copies, waits for them, and re-layouts: 12.4 us -> 1.21 us  [the longest x1 1.2 us: gather(): return ((outs[0], outs[1], outs[2], outs[3][0]), kept)]
    concatenate x9 -> x6, other arithmetic: 15.3 us -> 4.99 us  [the longest x2 2.34 us: on_device(): jnp.concatenate([group.part(cotangent, way), group.part(pairs, way)], axi...]
  transfers between devices with their start and end apart: 63 -> 43, of which waited for: 17 -> 5; matrix products, arithmetic and copies ran while one was open for 26% -> 12% of each run, Pallas kernels for 29% -> 42%
where the time goes in v2:
time: 666 us; the launch traced here: 656 us
  Pallas kernels  437 us (66%)
  starting transfers between devices  85 us (13%)
  local copies, waits for them, and re-layouts  78.2 us (12%)
  waiting for transfers between devices  25.2 us (4%)
  other arithmetic  22.2 us (3%)
  matrix products  6.98 us (1%)
    pallas_call x37, Pallas kernels, call(): pl.pallas_call(body, grid_spec=pltpu.PrefetchScalarGridSpec(num_scalar_pr...  430 us
    unnamed x107, local copies, waits for them, and re-layouts  30 us
    ppermute x6, starting transfers between devices, back(): return lax.ppermute(x, ('seq', 'row'), [(t, f) for f, t in self.route(way)])  29.3 us
    ppermute x20, starting transfers between devices, swap(): lax.ppermute(give, name[0], [(i, i ^ 1 << name[1]) for i in range(size)])  20.5 us
    ppermute x4, starting transfers between devices, go(): return lax.ppermute(x, ('seq', 'row'), self.route(way))  20.2 us
    ppermute x20, waiting for transfers between devices, swap(): lax.ppermute(give, name[0], [(i, i ^ 1 << name[1]) for i in range(size)])  15.9 us
    ppermute x13, starting transfers between devices, send(): return lax.ppermute(x, ('seq', 'row'), pairs)  15.1 us
  transfers between devices with their start and end apart: 43, of which 5 were waited for; matrix products, arithmetic and copies ran while one was open for 12% of the time, Pallas kernels for 42%

profile of v2, /device:TPU:0, one launch (start us, length us, event | category | flops | bytes accessed | tf_op | source)
XLA Modules:
  0.0 656.2 jit_solution(6935546872375447934)
XLA Ops:
  65.9 11.5 %collective-permute-start.3 = (bf16[640,1024]{1,0:T(8,128)(2,1)}, bf16[640,1024]{1,0:T(8,128)(2,1)}, u32[]{:S(2)}, u32[]{:S(2)}) collective-permute-start(bf16[640,1024]{1,0:T(8,128)(2,1)} %get-tuple-element.160), channel_id=1, source_target_pairs={{0,0},{1,16},{2,2},{3,18},{4,4},{5,20},{6,6},{7,22},{8,1},{9,17},{... | collective-permute-start | bytes 3932168 | tf_op jit(solution)/shard_map/ppermute | solution.py:820
  89.5 55.1 %self_forward.1 = (bf16[1024,1024]{1,0:T(8,128)(2,1)}, f32[1024,1024]{1,0:T(8,128)}) custom-call(s32[128]{0:T(128)} %slice_bitcast_fusion.refs_0_, bf16[1024,1024]{1,0:T(8,128)(2,1)} %query.1.refs_3_.refs_1_, bf16[2048,1024]{1,0:T(8,128)(2,1)} %get-tuple-element.155.refs_2_.refs_3_.refs_5_.refs_6_, ...), custom_call_target="tpu_custom_call" | custom-call | flops 23000000 | bytes 10000 | tf_op jit(solution)/shard_map/self_forward/pallas_call | solution.py:54
  148.0 9.2 %middle.1 = (f32[1024,1024]{1,0:T(8,128)}, bf16[1024,1024]{1,0:T(8,128)(2,1)}, bf16[1024,1024]{1,0:T(8,128)(2,1)}) custom-call(bf16[1024,1024]{1,0:T(8,128)(2,1)} %get-tuple-element.154.refs_0_.refs_5_, bf16[1024,1024]{1,0:T(8,128)(2,1)} %get-tuple-element.159.refs_2_.refs_1_.refs_5_.refs_3_, bf16[1024,1024]{1,0:T(8,128)(2,1)} %bitcast.128, ...), custom_call_target="tpu_custom_call" | custom-call | flops 9000000 | bytes 10000 | tf_op jit(solution)/shard_map/middle/pallas_call | solution.py:54
  158.0 19.7 %cross_forward.1 = (bf16[1024,1024]{1,0:T(8,128)(2,1)}, f32[1024,1024]{1,0:T(8,128)}) custom-call(bf16[1024,1024]{1,0:T(8,128)(2,1)} %get-tuple-element.162.refs_0_, bf16[256,1024]{1,0:T(8,128)(2,1)} %get-tuple-element.161.refs_5_.refs_1_.refs_3_.refs_4_.refs_6_, bf16[256,1024]{1,0:T(8,128)(2,1)} %copy-done.12, ...), custom_call_target="tpu_custom_call" | custom-call | flops 20000000 | bytes 10000 | tf_op jit(solution)/shard_map/cross_forward/pallas_call | solution.py:54
  177.8 56.9 %feed_forward.1 = (bf16[1024,1024]{1,0:T(8,128)(2,1)}, bf16[1024,1024]{1,0:T(8,128)(2,1)}, bf16[1024,2816]{1,0:T(8,128)(2,1)}, bf16[1024,5632]{1,0:T(8,128)(2,1)...) custom-call(f32[1024,1024]{1,0:T(8,128)} %get-tuple-element.163.refs_0_.re, ...), custom_call_target="tpu_custom_call" | custom-call | flops 70000000 | bytes 10000 | tf_op jit(solution)/shard_map/feed_forward/pallas_call | solution.py:54
  237.7 7.4 %weight_grads.9.refs_3_ = bf16[16,544,512]{2,1,0:T(8,128)(2,1)} custom-call(s32[1]{0:T(128)S(6)} %sub.24.refs_0_, bf16[1024,2816]{1,0:T(8,128)(2,1)} %get-tuple-element.170.refs_1_, bf16[1024,1024]{1,0:T(8,128)(2,1)} %get-tuple-element.165.refs_3_.refs_2_, bf16[512,1024]{1,0:T(8,128)(2,1)} %get-tuple-element.359.refs_3_), custom_call_target="tpu_custom_call" | custom-call | flops 9000000 | bytes 10000 | tf_op jit(solution)/shard_map/weight_grads/pallas_call | solution.py:54
  245.1 11.4 %weight_grads.10 = (bf16[16,544,512]{2,1,0:T(8,128)(2,1)}, bf16[512,1024]{1,0:T(8,128)(2,1)}) custom-call(s32[1]{0:T(128)S(6)} %sub.24.refs_0_, bf16[1024,1024]{1,0:T(8,128)(2,1)} %get-tuple-element.168.refs_1_, bf16[1024,5632]{1,0:T(8,128)(2,1)} %get-tuple-element.169.refs_2_, ...), custom_call_target="tpu_custom_call", output_to_operand_aliasing={{1}: (4, {}), {0}: (3, {})} | custom-call | flops 9000000 | bytes 10000 | tf_op jit(solution)/shard_map/weight_grads/pallas_call | solution.py:54
  259.4 7.3 %weight_grads.11.refs_3_ = bf16[16,544,512]{2,1,0:T(8,128)(2,1)} custom-call(s32[1]{0:T(128)} %bitcast.refs_0_, bf16[1024,2816]{1,0:T(8,128)(2,1)} %get-tuple-element.170.refs_1_, bf16[1024,1024]{1,0:T(8,128)(2,1)} %get-tuple-element.165.refs_3_.refs_2_, bf16[16,544,512]{2,1,0:T(8,128)(2,1)} %get-tuple-element.172.refs_3_), custom_call_target="tpu_custom_call" | custom-call | flops 9000000 | bytes 10000 | tf_op jit(solution)/shard_map/weight_grads/pallas_call | solution.py:54
  266.8 11.3 %weight_grads.12 = (bf16[16,544,512]{2,1,0:T(8,128)(2,1)}, bf16[512,1024]{1,0:T(8,128)(2,1)}) custom-call(s32[1]{0:T(128)} %bitcast.refs_0_, bf16[1024,1024]{1,0:T(8,128)(2,1)} %get-tuple-element.168.refs_1_, bf16[1024,5632]{1,0:T(8,128)(2,1)} %get-tuple-element.169.refs_2_, ...), custom_call_target="tpu_custom_call", output_to_operand_aliasing={{1}: (4, {}), {0}: (3, {})} | custom-call | flops 9000000 | bytes 10000 | tf_op jit(solution)/shard_map/weight_grads/pallas_call | solution.py:54
  294.4 31.7 %cross_backward.1 = (bf16[1024,1024]{1,0:T(8,128)(2,1)}, bf16[2,256,512]{2,1,0:T(8,128)(2,1)}, bf16[2,256,512]{2,1,0:T(8,128)(2,1)}) custom-call(bf16[1024,1024]{1,0:T(8,128)(2,1)} %get-tuple-element.162.refs_0_, bf16[1024,1024]{1,0:T(8,128)(2,1)} %get-tuple-element.166.refs_1_, bf16[1024,1024]{1,0:T(8,128)(2,1)} %get-tuple-element.164.refs_1_.refs_2_, ...), custom_call_target="tpu_custom_call" | custom-call | flops 31000000 | bytes 10000 | tf_op jit(solution)/shard_map/cross_backward/pallas_call | solution.py:54
  326.1 11.4 %back_middle.1 = (f32[1024,1024]{1,0:T(8,128)}, bf16[1024,1024]{1,0:T(8,128)(2,1)}, bf16[1024,1024]{1,0:T(8,128)(2,1)}, f32[8,1024]{1,0:T(8,128)}) custom-call(bf16[1024,1024]{1,0:T(8,128)(2,1)} %get-tuple-element.177.refs_0_.refs_4_, bf16[1024,1024]{1,0:T(8,128)(2,1)} %copy.168.refs_7_.refs_4_.refs_1_, f32[1024,1024]{1,0:T(8,128)} %get-tuple-element.163.refs_0_.refs_2_, ...), custom_call_target="tpu_custom_call" | custom-call | flops 12000000 | bytes 10000 | tf_op jit(solution)/shard_map/back_middle/pallas_call | solution.py:54
  338.5 8.7 %weight_grads.13 = (bf16[16,192,512]{2,1,0:T(8,128)(2,1)}, bf16[512,1024]{1,0:T(8,128)(2,1)}, bf16[2,256,512]{2,1,0:T(8,128)(2,1)}) custom-call(s32[1]{0:T(128)S(6)} %sub.24.refs_0_, bf16[1024,1024]{1,0:T(8,128)(2,1)} %get-tuple-element.164.refs_1_.refs_2_, ...), custom_call_target="tpu_custom_call", output_to_operand_aliasing={{1}: (7, {}), {2}: (8, {})} | custom-call | flops 9000000 | bytes 10000 | tf_op jit(solution)/shard_map/weight_grads/pallas_call | solution.py:54
  348.5 8.6 %stage.13 = (bf16[4,272,512]{2,1,0:T(8,128)(2,1)}, bf16[4,272,512]{2,1,0:T(8,128)(2,1)}, bf16[4,272,512]{2,1,0:T(8,128)(2,1)}, bf16[4,272,512]{2,1,0:T(8,128)(2,1)}, bf16[16,192,512]{2,1,0:T(8,128)(2,1)}) custom-call(s32[4]{0:T(128)} %pad_add_fusion.refs_0_, ...), custom_call_target="tpu_custom_call", output_to_operand_aliasing={{4}: (13, {})} | custom-call | flops 4000000 | bytes 10000 | tf_op jit(solution)/shard_map/stage/pallas_call | solution.py:54
  359.4 8.6 %weight_grads.14 = (bf16[16,192,512]{2,1,0:T(8,128)(2,1)}, bf16[2,256,512]{2,1,0:T(8,128)(2,1)}) custom-call(s32[1]{0:T(128)} %bitcast.refs_0_, bf16[1024,1024]{1,0:T(8,128)(2,1)} %get-tuple-element.164.refs_1_.refs_2_, bf16[1024,1024]{1,0:T(8,128)(2,1)} %get-tuple-element.183.refs_2_, ...), custom_call_target="tpu_custom_call", output_to_operand_aliasing={{1}: (7, {})} | custom-call | flops 9000000 | bytes 10000 | tf_op jit(solution)/shard_map/weight_grads/pallas_call | solution.py:54
  373.4 21.5 %self_backward.4 = (bf16[1024,1024]{1,0:T(8,128)(2,1)}, bf16[2,1024,512]{2,1,0:T(8,128)(2,1)}, bf16[1,2,1024,512]{3,2,1,0:T(8,128)(2,1)}, f32[16,8,512]{2,1,0:T(...) custom-call(s32[128]{0:T(128)} %slice_bitcast_fusion.refs_0_, ...), custom_call_target="tpu_custom_call", output_to_operand_aliasing={{5}: (11, {}), {6}: (12, {})} | custom-call | flops 18000000 | bytes 10000 | tf_op jit(solution)/shard_map/self_backward/pallas_call | solution.py:54
  410.1 21.3 %self_backward.5 = (bf16[1024,1024]{1,0:T(8,128)(2,1)}, bf16[2,1024,512]{2,1,0:T(8,128)(2,1)}, bf16[1,2,1024,512]{3,2,1,0:T(8,128)(2,1)}, f32[16,8,512]{2,1,0:T(...) custom-call(s32[128]{0:T(128)} %slice_bitcast_fusion.refs_0_, ...), custom_call_target="tpu_custom_call", output_to_operand_aliasing={{5}: (16, {}), {0}: (11, {}), {1}: (12, {}), {2}: (13, {}),... | custom-call | flops 18000000 | bytes 10000 | tf_op jit(solution)/shard_map/self_backward/pallas_call | solution.py:54
  447.5 21.3 %self_backward.6 = (bf16[1024,1024]{1,0:T(8,128)(2,1)}, bf16[2,1024,512]{2,1,0:T(8,128)(2,1)}, bf16[1,2,1024,512]{3,2,1,0:T(8,128)(2,1)}, f32[16,8,512]{2,1,0:T(...) custom-call(s32[128]{0:T(128)} %slice_bitcast_fusion.refs_0_, ...), custom_call_target="tpu_custom_call", output_to_operand_aliasing={{5}: (16, {}), {0}: (11, {}), {1}: (12, {}), {2}: (13, {}),... | custom-call | flops 18000000 | bytes 10000 | tf_op jit(solution)/shard_map/self_backward/pallas_call | solution.py:54
  477.2 21.3 %self_backward.7 = (bf16[1024,1024]{1,0:T(8,128)(2,1)}, bf16[2,1024,512]{2,1,0:T(8,128)(2,1)}, bf16[1,2,1024,512]{3,2,1,0:T(8,128)(2,1)}, f32[16,8,512]{2,1,0:T(8,128)}, f32[16,8,256]{2,1,0:T(8,128)}) custom-call(s32[128]{0:T(128)} %slice_bitcast_fusion.refs_0_, ...), custom_call_target="tpu_custom_call", output_to_operand_aliasing={{0}: (11, {}), {1}: (12, {}), {2}: (13, {}), {3}: (14, {}),... | custom-call | flops 18000000 | bytes 10000 | tf_op jit(solution)/shard_map/self_backward/pallas_call | solution.py:54
  510.1 11.0 %exit.1 = (bf16[1024,1024]{1,0:T(8,128)(2,1)}, bf16[1024,1024]{1,0:T(8,128)(2,1)}, f32[8,1024]{1,0:T(8,128)}, bf16[16,192,512]{2,1,0:T(8,128)(2,1)}) custom-call(bf16[1024,1024]{1,0:T(8,128)(2,1)} %get-tuple-element.230.refs_7_.refs_2_.refs_0_, bf16[1024,1024]{1,0:T(8,128)(2,1)} %copy.167.refs_5_.refs_1_, ...), custom_call_target="tpu_custom_call", output_to_operand_aliasing={{3}: (8, {})} | custom-call | flops 11000000 | bytes 10000 | tf_op jit(solution)/shard_map/exit/pallas_call | solution.py:54
  533.4 9.5 %collective-permute-start.29 = (bf16[512,1024]{1,0:T(8,128)(2,1)}, bf16[512,1024]{1,0:T(8,128)(2,1)}, u32[]{:S(2)}, u32[]{:S(2)}) collective-permute-start(bf16[512,1024]{1,0:T(8,128)(2,1)} %get-tuple-element.356.refs_5_), channel_id=1, source_target_pairs={{0,0},{16,1},{2,2},{18,3},{4,4},{20,5},{6,6},{22,7},{1,8},{17,9},{... | collective-permute-start | bytes 3145736 | tf_op jit(solution)/shard_map/ppermute | solution.py:823
  543.6 8.1 %weight_grads.17 = (bf16[16,192,512]{2,1,0:T(8,128)(2,1)}, bf16[512,1024]{1,0:T(8,128)(2,1)}, bf16[512,1024]{1,0:T(8,128)(2,1)}, f32[16,8,512]{2,1,0:T(8,128)}, ...) custom-call(s32[1]{0:T(128)} %bitcast.refs_0_, ...), custom_call_target="tpu_custom_call", output_to_operand_aliasing={{1}: (7, {}), {2}: (8, {}), {3}: (9, {}), {4}: (10, {}), {5... | custom-call | flops 9000000 | bytes 10000 | tf_op jit(solution)/shard_map/weight_grads/pallas_call | solution.py:54
  570.4 7.6 %collective-permute-start.33 = (bf16[512,1024]{1,0:T(8,128)(2,1)S(1)}, bf16[512,1024]{1,0:T(8,128)(2,1)}, u32[]{:S(2)}, u32[]{:S(2)}) collective-permute-start(bf16[512,1024]{1,0:T(8,128)(2,1)S(1)} %copy-done.6), channel_id=1, source_target_pairs={{8,0},{24,1},{10,2},{26,3},{12,4},{28,5},{14,6},{30,7},{9,8},{25,9... | collective-permute-start | bytes 3145736 | tf_op jit(solution)/shard_map/ppermute | solution.py:823
  623.7 10.0 %collective-permute-done.39 = f32[4,1024]{1,0:T(4,128)S(1)} collective-permute-done((f32[4,1024]{1,0:T(4,128)}, f32[4,1024]{1,0:T(4,128)S(1)}, u32[]{:S(2)}, u32[]{:S(2)}) %collective-permute-start.39) | collective-permute-done | bytes 16416 | tf_op jit(solution)/shard_map/ppermute | solution.py:852
  645.6 7.6 %collective-permute-done.41 = bf16[1,192,512]{2,1,0:T(8,128)(2,1)S(1)} collective-permute-done((bf16[1,192,512]{2,1,0:T(8,128)(2,1)}, bf16[1,192,512]{2,1,0:T(8,128)(2,1)S(1)}, u32[]{:S(2)}, u32[]{:S(2)}) %collective-permute-start.41) | collective-permute-done | bytes 196640 | tf_op jit(solution)/shard_map/ppermute | solution.py:803
  (298 shorter events, 256.6 us)
Async XLA Ops:
  3.3 49.5 %collective-permute-start = (bf16[528,1024]{1,0:T(8,128)(2,1)S(1)}, bf16[528,1024]{1,0:T(8,128)(2,1)}, u32[]{:S(2)}, u32[]{:S(2)}) collective-permute-start(bf16[528,1024]{1,0:T(8,128)(2,1)S(1)} %fusion.2), channel_id=1, source_target_pairs={{0,0},{1,16},{2,2},{3,18},{4,4},{5,20},{6,6},{7,22},{8,1},{9,17},{... | collective-permute-start | bytes 3244040 | tf_op jit(solution)/shard_map/ppermute | solution.py:820
  6.0 46.7 %collective-permute-start.1 = (bf16[528,1024]{1,0:T(8,128)(2,1)}, bf16[528,1024]{1,0:T(8,128)(2,1)}, u32[]{:S(2)}, u32[]{:S(2)}) collective-permute-start(bf16[528,1024]{1,0:T(8,128)(2,1)} %fusion.3), channel_id=1, source_target_pairs={{0,8},{1,24},{2,10},{3,26},{4,12},{5,28},{6,14},{7,30},{8,9},{9,25... | collective-permute-start | bytes 3244040 | tf_op jit(solution)/shard_map/ppermute | solution.py:820
  59.7 23.8 %collective-permute-start.2 = (bf16[1056,1024]{1,0:T(8,128)(2,1)}, bf16[1056,1024]{1,0:T(8,128)(2,1)}, u32[]{:S(2)}, u32[]{:S(2)}) collective-permute-start(bf16[1056,1024]{1,0:T(8,128)(2,1)} %get-tuple-element.152.refs_1_), channel_id=1, source_target_pairs={{0,1},{1,0},{2,3},{3,2},{4,5},{5,4},{6,7},{7,6},{8,9},{9,8},{10,11... | collective-permute-start | bytes 6488072 | tf_op jit(solution)/shard_map/ppermute | solution.py:803
  64.0 80.7 %collective-permute-start.4 = (bf16[640,1024]{1,0:T(8,128)(2,1)S(1)}, bf16[640,1024]{1,0:T(8,128)(2,1)}, u32[]{:S(2)}, u32[]{:S(2)}) collective-permute-start(bf16[640,1024]{1,0:T(8,128)(2,1)S(1)} %copy-done.13), channel_id=1, source_target_pairs={{0,8},{1,24},{2,10},{3,26},{4,12},{5,28},{6,14},{7,30},{8,9},{9,25... | collective-permute-start | bytes 3932168 | tf_op jit(solution)/shard_map/ppermute | solution.py:820
  65.9 78.8 %collective-permute-start.3 = (bf16[640,1024]{1,0:T(8,128)(2,1)}, bf16[640,1024]{1,0:T(8,128)(2,1)}, u32[]{:S(2)}, u32[]{:S(2)}) collective-permute-start(bf16[640,1024]{1,0:T(8,128)(2,1)} %get-tuple-element.160), channel_id=1, source_target_pairs={{0,0},{1,16},{2,2},{3,18},{4,4},{5,20},{6,6},{7,22},{8,1},{9,17},{... | collective-permute-start | bytes 3932168 | tf_op jit(solution)/shard_map/ppermute | solution.py:820
  286.0 61.2 %collective-permute-start.8 = (bf16[8,272,512]{2,1,0:T(8,128)(2,1)}, bf16[8,272,512]{2,1,0:T(8,128)(2,1)S(1)}, u32[]{:S(2)}, u32[]{:S(2)}) collective-permute-start(bf16[8,272,512]{2,1,0:T(8,128)(2,1)} %get-tuple-element.175.refs_8_), channel_id=1, source_target_pairs={{0,2},{1,3},{2,0},{3,1},{4,6},{5,7},{6,4},{7,5},{8,10},{9,11},{10,... | collective-permute-start | bytes 6684680 | tf_op jit(solution)/shard_map/ppermute | solution.py:852
  287.5 59.7 %collective-permute-start.9 = (bf16[8,272,512]{2,1,0:T(8,128)(2,1)}, bf16[8,272,512]{2,1,0:T(8,128)(2,1)}, u32[]{:S(2)}, u32[]{:S(2)}) collective-permute-start(bf16[8,272,512]{2,1,0:T(8,128)(2,1)} %get-tuple-element.176.refs_9_), channel_id=1, source_target_pairs={{0,4},{1,5},{2,6},{3,7},{4,0},{5,1},{6,2},{7,3},{8,12},{9,13},{10,... | collective-permute-start | bytes 6684680 | tf_op jit(solution)/shard_map/ppermute | solution.py:852
  287.6 49.9 %collective-permute-start.10 = (bf16[512,1024]{1,0:T(8,128)(2,1)S(1)}, bf16[512,1024]{1,0:T(8,128)(2,1)S(1)}, u32[]{:S(2)}, u32[]{:S(2)}) collective-permute-start(bf16[512,1024]{1,0:T(8,128)(2,1)S(1)} %copy-done.7), channel_id=1, source_target_pairs={{8,0},{24,1},{10,2},{26,3},{12,4},{28,5},{14,6},{30,7},{9,8},{25,9... | collective-permute-start | bytes 3145736 | tf_op jit(solution)/shard_map/ppermute | solution.py:823
  357.2 37.7 %collective-permute-start.13 = (bf16[4,272,512]{2,1,0:T(8,128)(2,1)}, bf16[4,272,512]{2,1,0:T(8,128)(2,1)S(1)}, u32[]{:S(2)}, u32[]{:S(2)}) collective-permute-start(bf16[4,272,512]{2,1,0:T(8,128)(2,1)} %get-tuple-element.192.refs_9_), channel_id=1, source_target_pairs={{0,4},{1,5},{2,6},{3,7},{4,0},{5,1},{6,2},{7,3},{8,12},{9,13},{10,... | collective-permute-start | bytes 3342344 | tf_op jit(solution)/shard_map/ppermute | solution.py:852
  359.2 35.7 %collective-permute-start.14 = (bf16[4,272,512]{2,1,0:T(8,128)(2,1)}, bf16[4,272,512]{2,1,0:T(8,128)(2,1)S(1)}, u32[]{:S(2)}, u32[]{:S(2)}) collective-permute-start(bf16[4,272,512]{2,1,0:T(8,128)(2,1)} %get-tuple-element.193.refs_10_), channel_id=1, source_target_pairs={{0,2},{1,3},{2,0},{3,1},{4,6},{5,7},{6,4},{7,5},{8,10},{9,11},{10,... | collective-permute-start | bytes 3342344 | tf_op jit(solution)/shard_map/ppermute | solution.py:852
  370.1 24.8 %collective-permute-start.15 = (bf16[128,1024]{1,0:T(8,128)(2,1)}, bf16[128,1024]{1,0:T(8,128)(2,1)S(1)}, u32[]{:S(2)}, u32[]{:S(2)}) collective-permute-start(bf16[128,1024]{1,0:T(8,128)(2,1)} %get-tuple-element.198.refs_13_), channel_id=1, source_target_pairs={{0,0},{16,1},{2,2},{18,3},{4,4},{20,5},{6,6},{22,7},{1,8},{17,9},{... | collective-permute-start | bytes 786440 | tf_op jit(solution)/shard_map/ppermute | solution.py:823
  401.0 30.4 %collective-permute-start.16 = (bf16[2,544,512]{2,1,0:T(8,128)(2,1)}, bf16[2,544,512]{2,1,0:T(8,128)(2,1)S(1)}, u32[]{:S(2)}, u32[]{:S(2)}) collective-permute-start(bf16[2,544,512]{2,1,0:T(8,128)(2,1)} %get-tuple-element.208.refs_5_.refs_17_), channel_id=1, source_target_pairs={{0,8},{8,0},{16,24},{24,16},{1,9},{9,1},{17,25},{25,17},{2,10},{10... | collective-permute-start | bytes 3342344 | tf_op jit(solution)/shard_map/ppermute | solution.py:852
  407.1 31.7 %collective-permute-start.17 = (bf16[8,96,512]{2,1,0:T(8,128)(2,1)}, bf16[8,96,512]{2,1,0:T(8,128)(2,1)S(1)}, u32[]{:S(2)}, u32[]{:S(2)}) collective-permute-start(bf16[8,96,512]{2,1,0:T(8,128)(2,1)} %get-tuple-element.209.refs_18_), channel_id=1, source_target_pairs={{0,2},{1,3},{2,0},{3,1},{4,6},{5,7},{6,4},{7,5},{8,10},{9,11},{10,... | collective-permute-start | bytes 2359304 | tf_op jit(solution)/shard_map/ppermute | solution.py:852
  407.6 31.2 %collective-permute-start.18 = (bf16[8,96,512]{2,1,0:T(8,128)(2,1)}, bf16[8,96,512]{2,1,0:T(8,128)(2,1)S(1)}, u32[]{:S(2)}, u32[]{:S(2)}) collective-permute-start(bf16[8,96,512]{2,1,0:T(8,128)(2,1)} %get-tuple-element.210.refs_19_), channel_id=1, source_target_pairs={{0,4},{1,5},{2,6},{3,7},{4,0},{5,1},{6,2},{7,3},{8,12},{9,13},{10,... | collective-permute-start | bytes 2359304 | tf_op jit(solution)/shard_map/ppermute | solution.py:852
  435.8 33.0 %collective-permute-start.21 = (bf16[1,544,512]{2,1,0:T(8,128)(2,1)}, bf16[1,544,512]{2,1,0:T(8,128)(2,1)S(1)}, u32[]{:S(2)}, u32[]{:S(2)}) collective-permute-start(bf16[1,544,512]{2,1,0:T(8,128)(2,1)} %get-tuple-element.228), channel_id=1, source_target_pairs={{0,0},{1,16},{2,2},{3,18},{4,4},{5,20},{6,6},{7,22},{8,8},{9,24},{... | collective-permute-start | bytes 1671176 | tf_op jit(solution)/shard_map/ppermute | solution.py:803
  437.5 31.3 %collective-permute-start.22 = (bf16[1,544,512]{2,1,0:T(8,128)(2,1)}, bf16[1,544,512]{2,1,0:T(8,128)(2,1)S(1)}, u32[]{:S(2)}, u32[]{:S(2)}) collective-permute-start(bf16[1,544,512]{2,1,0:T(8,128)(2,1)} %get-tuple-element.218.refs_14_.refs_17_), channel_id=1, source_target_pairs={{0,1},{1,17},{2,3},{3,19},{4,5},{5,21},{6,7},{7,23},{8,9},{9,25},{... | collective-permute-start | bytes 1671176 | tf_op jit(solution)/shard_map/ppermute | solution.py:803
  445.3 23.4 %collective-permute-start.19 = (bf16[4,96,512]{2,1,0:T(8,128)(2,1)}, bf16[4,96,512]{2,1,0:T(8,128)(2,1)S(1)}, u32[]{:S(2)}, u32[]{:S(2)}) collective-permute-start(bf16[4,96,512]{2,1,0:T(8,128)(2,1)} %get-tuple-element.219.refs_18_), channel_id=1, source_target_pairs={{0,4},{1,5},{2,6},{3,7},{4,0},{5,1},{6,2},{7,3},{8,12},{9,13},{10,... | collective-permute-start | bytes 1179656 | tf_op jit(solution)/shard_map/ppermute | solution.py:852
  473.3 25.1 %collective-permute-start.23 = (bf16[2,192,512]{2,1,0:T(8,128)(2,1)}, bf16[2,192,512]{2,1,0:T(8,128)(2,1)S(1)}, u32[]{:S(2)}, u32[]{:S(2)}) collective-permute-start(bf16[2,192,512]{2,1,0:T(8,128)(2,1)} %get-tuple-element.229.refs_16_), channel_id=1, source_target_pairs={{0,8},{8,0},{16,24},{24,16},{1,9},{9,1},{17,25},{25,17},{2,10},{10... | collective-permute-start | bytes 1179656 | tf_op jit(solution)/shard_map/ppermute | solution.py:852
  528.5 32.5 %collective-permute-start.28 = (bf16[16,192,512]{2,1,0:T(8,128)(2,1)}, bf16[16,192,512]{2,1,0:T(8,128)(2,1)}, u32[]{:S(2)}, u32[]{:S(2)}) collective-permute-start(bf16[16,192,512]{2,1,0:T(8,128)(2,1)} %get-tuple-element.247.refs_16_), channel_id=1, source_target_pairs={{0,1},{1,0},{2,3},{3,2},{4,5},{5,4},{6,7},{7,6},{8,9},{9,8},{10,11... | collective-permute-start | bytes 9437192 | tf_op jit(solution)/shard_map/ppermute | solution.py:803
  533.4 27.5 %collective-permute-start.29 = (bf16[512,1024]{1,0:T(8,128)(2,1)}, bf16[512,1024]{1,0:T(8,128)(2,1)}, u32[]{:S(2)}, u32[]{:S(2)}) collective-permute-start(bf16[512,1024]{1,0:T(8,128)(2,1)} %get-tuple-element.356.refs_5_), channel_id=1, source_target_pairs={{0,0},{16,1},{2,2},{18,3},{4,4},{20,5},{6,6},{22,7},{1,8},{17,9},{... | collective-permute-start | bytes 3145736 | tf_op jit(solution)/shard_map/ppermute | solution.py:823
  568.3 28.2 %collective-permute-start.34 = (f32[4,1024]{1,0:T(4,128)S(1)}, f32[4,1024]{1,0:T(4,128)}, u32[]{:S(2)}, u32[]{:S(2)}) collective-permute-start(f32[4,1024]{1,0:T(4,128)S(1)} %copy-done.40), channel_id=1, source_target_pairs={{0,2},{1,3},{2,0},{3,1},{4,6},{5,7},{6,4},{7,5},{8,10},{9,11},{10,... | collective-permute-start | bytes 49160 | tf_op jit(solution)/shard_map/ppermute | solution.py:852
  570.3 27.5 %collective-permute-start.31 = (bf16[8,96,512]{2,1,0:T(8,128)(2,1)}, bf16[8,96,512]{2,1,0:T(8,128)(2,1)}, u32[]{:S(2)}, u32[]{:S(2)}) collective-permute-start(bf16[8,96,512]{2,1,0:T(8,128)(2,1)} %get-tuple-element.262), channel_id=1, source_target_pairs={{0,2},{1,3},{2,0},{3,1},{4,6},{5,7},{6,4},{7,5},{8,10},{9,11},{10,... | collective-permute-start | bytes 2359304 | tf_op jit(solution)/shard_map/ppermute | solution.py:852
  570.3 27.5 %collective-permute-start.32 = (bf16[8,96,512]{2,1,0:T(8,128)(2,1)}, bf16[8,96,512]{2,1,0:T(8,128)(2,1)}, u32[]{:S(2)}, u32[]{:S(2)}) collective-permute-start(bf16[8,96,512]{2,1,0:T(8,128)(2,1)} %get-tuple-element.263), channel_id=1, source_target_pairs={{0,4},{1,5},{2,6},{3,7},{4,0},{5,1},{6,2},{7,3},{8,12},{9,13},{10,... | collective-permute-start | bytes 2359304 | tf_op jit(solution)/shard_map/ppermute | solution.py:852
  570.4 29.1 %collective-permute-start.33 = (bf16[512,1024]{1,0:T(8,128)(2,1)S(1)}, bf16[512,1024]{1,0:T(8,128)(2,1)}, u32[]{:S(2)}, u32[]{:S(2)}) collective-permute-start(bf16[512,1024]{1,0:T(8,128)(2,1)S(1)} %copy-done.6), channel_id=1, source_target_pairs={{8,0},{24,1},{10,2},{26,3},{12,4},{28,5},{14,6},{30,7},{9,8},{25,9... | collective-permute-start | bytes 3145736 | tf_op jit(solution)/shard_map/ppermute | solution.py:823
  (68 other events, 448.4 us)
